TPU v7x, 256 devices: a whole 4x4x8 slice. The times are simulated.
256 devices in a mesh: seq: 16 (over z_hi, x, core), chan: 16 (over y, z_lo).
Axes of the slice: x: 4, y: 4, z: 8 (z_hi: 2, z_lo: 4; z = z_hi * 4 + z_lo), core: 2. Of those that a mesh axis runs over, the one named last changes fastest.
Arguments:
- layer_input: bfloat16 [65536, 2560], P('seq', 'chan'), may hold values from -6 to 6
- query_scale: float32 [2560], P('chan'), may hold values from 0.5 to 2
- key_scale: float32 [2560], P('chan'), may hold values from 0.5 to 2
- twiddle: float32 [128, 512], P('seq'), may hold values from 0.5 to 2
- seq_inner: bfloat16 [512, 512], replicated, may hold values from -0.25 to 0.25
- seq_outer: bfloat16 [128, 128], replicated, may hold values from -0.5 to 0.5
- grad_output: bfloat16 [65536, 2560], P('seq', 'chan'), may hold values from -6 to 6
- hidden_pre: bfloat16 [65536, 6144], P('seq', 'chan'), may hold values from -8 to 8
- up_right: bfloat16 [16, 384, 640], P('chan'), may hold values from -0.25 to 0.25
- up_left: bfloat16 [4, 4, 1536], replicated, may hold values from -3 to 3
- down_right: bfloat16 [16, 640, 384], P('chan'), may hold values from -0.15625 to 0.15625
- down_left: bfloat16 [4, 4, 640], replicated, may hold values from -3 to 3
Outputs:
- grad_input: bfloat16 [65536, 2560], P('seq', 'chan')
- grad_up_right: float32 [16, 384, 640], P('chan', None, 'seq')
- grad_down_right: float32 [16, 640, 384], P('chan', 'seq')
- grad_query_scale: float32 [2560], P('chan')
- grad_key_scale: float32 [2560], P('chan')
- grad_seq_inner: float32 [512, 512], replicated
- grad_seq_outer: float32 [128, 128], replicated
All inputs are finite; a program needn't handle non-finite values.
Results may differ from a plain program's by a relative error of at most 0.0077.
Values may be sent and summed in bfloat16 or wider, within the bound.
No kernel may reach another device: no remote copies, remote signals or barrier semaphores. Data moves between devices by JAX's collectives and lax.ppermute only.
A program may use at most 128 MiB of HBM per device.

v0:
```python
import jax
import jax.numpy as jnp
from jax import lax
from jax.sharding import PartitionSpec as P

NB = 4


def from_partner(block, axis, stride):
    count = lax.axis_size(axis)
    route = []
    for low in range(count):
        high = low | 1 << stride
        if high != low and high < count:
            route += [(low, high), (high, low)]
    return lax.ppermute(block, axis, route)


def lower_mask(size):
    return jnp.arange(size)[:, None] >= jnp.arange(size)[None, :]


def group_gather(values, member, group_bits):
    gathered = values
    for bit_section in range(group_bits):
        partner = from_partner(gathered, "chan", bit_section)
        high_half = jnp.bitwise_and(jnp.right_shift(member, bit_section), 1) == 1
        gathered = jnp.where(
            high_half,
            jnp.concatenate([partner, gathered], axis=1),
            jnp.concatenate([gathered, partner], axis=1),
        )
    return gathered


def group_slots(buffer):
    slot_count = buffer.shape[0]
    for bit_section in range(slot_count.bit_length() - 1):
        slot_span = 1 << bit_section
        shaped = buffer.reshape((slot_count // (2 * slot_span), 2, slot_span) + buffer.shape[1:])
        received = from_partner(shaped[:, 1], "chan", bit_section)
        buffer = jnp.stack([shaped[:, 0], received], axis=1).reshape(buffer.shape)
    return buffer


def by_tokens(values, weight):
    full_width = weight.shape[2]
    spread = lax.all_to_all(values, "chan", split_axis=0, concat_axis=1, tiled=True)
    row_count = spread.shape[0]
    blocks = spread.reshape(row_count, NB, full_width)
    result = jnp.einsum("jkw,tjw->tkw", weight, blocks, preferred_element_type=jnp.float32).astype(
        jnp.bfloat16
    )
    return lax.all_to_all(
        result.reshape(row_count, NB * full_width), "chan", split_axis=1, concat_axis=0, tiled=True
    )


def group_sum(partial_value, member, group_size):
    tokens_here = partial_value.shape[0]
    pieces = (
        partial_value.reshape(tokens_here, group_size, -1).transpose(1, 0, 2).astype(jnp.bfloat16)
    )
    slot_order = jnp.bitwise_xor(member, jnp.arange(group_size, dtype=jnp.int32))
    arrived = group_slots(jnp.take(pieces, slot_order, axis=0))
    return jnp.sum(arrived.astype(jnp.float32), axis=0)


def body(
    layer_input,
    query_scale,
    key_scale,
    twiddle,
    seq_inner,
    seq_outer,
    grad_output,
    hidden_pre,
    up_right,
    up_left,
    down_right,
    down_left,
):
    seq_count = lax.axis_size("seq")
    chan_count = lax.axis_size("chan")
    outer_here, inner_len = twiddle.shape
    tokens_here, chan_here = layer_input.shape
    outer_len = seq_outer.shape[0]
    group_size = chan_count // NB
    group_bits = group_size.bit_length() - 1
    chan_index = lax.axis_index("chan")
    member = chan_index % group_size
    inner_mask = lower_mask(inner_len)
    outer_mask = lower_mask(outer_len)
    inner_tri = jnp.where(inner_mask, seq_inner, jnp.zeros_like(seq_inner))
    outer_tri = jnp.where(outer_mask, seq_outer, jnp.zeros_like(seq_outer))
    inputs = layer_input.astype(jnp.float32).reshape(outer_here, inner_len, chan_here)
    key_input = (inputs * key_scale).astype(jnp.bfloat16)
    first_pass = (
        jnp.einsum("bk,akc->abc", inner_tri, key_input, preferred_element_type=jnp.float32)
        * twiddle[:, :, None]
    ).astype(jnp.bfloat16)
    first_cols = lax.all_to_all(first_pass, "seq", split_axis=1, concat_axis=0, tiled=True)
    conv_cols = jnp.einsum(
        "ij,jbc->ibc", outer_tri, first_cols, preferred_element_type=jnp.float32
    ).astype(jnp.bfloat16)
    convolved = lax.all_to_all(conv_cols, "seq", split_axis=0, concat_axis=1, tiled=True)
    conv_f = convolved.astype(jnp.float32)
    mixed = (
        (inputs + inputs * query_scale * conv_f)
        .astype(jnp.bfloat16)
        .reshape(tokens_here, chan_here)
    )
    down_grad = by_tokens(grad_output, down_left)
    down_rows = group_gather(down_grad, member, group_bits)
    hidden_grad = jnp.dot(down_rows, down_right[0], preferred_element_type=jnp.float32)
    pre_values = hidden_pre.astype(jnp.float32)
    activated = jax.nn.gelu(pre_values).astype(jnp.bfloat16)
    down_terms = jnp.einsum("tp,tq->pq", down_rows, activated, preferred_element_type=jnp.float32)
    token_scale = (seq_count * tokens_here) ** (-0.5)
    grad_down = lax.psum_scatter(down_terms, "seq", scatter_dimension=0, tiled=True) * token_scale
    pre_grad = jax.vjp(jax.nn.gelu, pre_values)[1](hidden_grad)[0].astype(jnp.bfloat16)
    right_grad = by_tokens(pre_grad, up_left)
    up_rows = group_gather(mixed, member, group_bits)
    up_terms = jnp.einsum("tq,tp->qp", right_grad, up_rows, preferred_element_type=jnp.float32)
    grad_up = lax.psum_scatter(up_terms, "seq", scatter_dimension=1, tiled=True) * token_scale
    partial_value = jnp.dot(right_grad, up_right[0], preferred_element_type=jnp.float32)
    mix_grad = grad_output.astype(jnp.float32) + group_sum(partial_value, member, group_size)
    mix_grad = mix_grad.reshape(outer_here, inner_len, chan_here)
    conv_grad = (mix_grad * inputs * query_scale).astype(jnp.bfloat16)
    query_terms = jnp.sum(mix_grad * inputs * conv_f, axis=(0, 1))
    grad_cols = lax.all_to_all(conv_grad, "seq", split_axis=1, concat_axis=0, tiled=True)
    first_grad_cols = jnp.einsum(
        "ij,ibc->jbc", outer_tri, grad_cols, preferred_element_type=jnp.float32
    ).astype(jnp.bfloat16)
    outer_terms = jnp.einsum(
        "ibc,jbc->ij", grad_cols, first_cols, preferred_element_type=jnp.float32
    )
    outer_terms = jnp.where(outer_mask, outer_terms, jnp.zeros_like(outer_terms))
    first_grad = lax.all_to_all(first_grad_cols, "seq", split_axis=0, concat_axis=1, tiled=True)
    back_pass = (first_grad.astype(jnp.float32) * twiddle[:, :, None]).astype(jnp.bfloat16)
    key_grad = jnp.einsum("bk,abc->akc", inner_tri, back_pass, preferred_element_type=jnp.float32)
    inner_terms = jnp.einsum(
        "abc,akc->bk", back_pass, key_input, preferred_element_type=jnp.float32
    )
    inner_terms = jnp.where(inner_mask, inner_terms, jnp.zeros_like(inner_terms))
    grad_input = (
        (mix_grad * (1.0 + query_scale * conv_f) + key_scale * key_grad)
        .astype(jnp.bfloat16)
        .reshape(tokens_here, chan_here)
    )
    key_terms = jnp.sum(key_grad * inputs, axis=(0, 1))
    query_total, key_total = lax.psum((query_terms, key_terms), "seq")
    inner_total, outer_total = lax.psum((inner_terms, outer_terms), ("seq", "chan"))
    model_width = chan_count * chan_here
    grad_seq_inner = inner_total * (outer_len * model_width) ** (-0.5)
    grad_seq_outer = outer_total * (inner_len * model_width) ** (-0.5)
    return (
        grad_input,
        grad_up[None],
        grad_down[None],
        query_total * token_scale,
        key_total * token_scale,
        grad_seq_inner,
        grad_seq_outer,
    )


def solution(mesh):
    return jax.shard_map(
        body,
        mesh=mesh,
        in_specs=(
            P("seq", "chan"),
            P("chan"),
            P("chan"),
            P("seq", None),
            P(),
            P(),
            P("seq", "chan"),
            P("seq", "chan"),
            P("chan", None, None),
            P(),
            P("chan", None, None),
            P(),
        ),
        out_specs=(
            P("seq", "chan"),
            P("chan", None, "seq"),
            P("chan", "seq", None),
            P("chan"),
            P("chan"),
            P(),
            P(),
        ),
        check_vma=False,
    )
```

profile of v0, /device:TPU:32, one launch (start us, length us, event | category | flops | bytes accessed | tf_op | source)
XLA Modules:
  0.0 1219.8 jit_solution(2949782027503512952)
XLA Ops:
  8.0 2.6 copy.187
  10.6 8.7 all-to-all-start
  19.7 28.6 %all-to-all-done = bf16[16,256,160]{1,2,0:T(8,128)(2,1)S(1)} async-done(((bf16[16,256,160]{1,2,0:T(8,128)(2,1)}), bf16[16,256,160]{1,2,0:T(8,128)(2,1)S(1)}, u32[]{:S(2)}, u32[]{:S(2)}) %all-to-all-start) | async-done | bytes 1310752 | tf_op jit(solution)/shard_map/all_to_all | solution.py:48
  49.7 39.8 %all_to_all.124 = bf16[256,16,160]{0,2,1:T(8,128)(2,1)S(1)} all-to-all(bf16[256,16,160]{0,2,1:T(8,128)(2,1)S(1)} %bitcast.165), channel_id=1, replica_groups=mesh['seq'=16,'chan'=16] {'chan'}, dimensions={1} | all-to-all | bytes 2621440 | tf_op jit(solution)/shard_map/all_to_all | solution.py:54
  91.4 27.9 %collective-permute-done = bf16[4096,160]{0,1:T(8,128)(2,1)S(1)} collective-permute-done((bf16[4096,160]{0,1:T(8,128)(2,1)S(1)}, bf16[4096,160]{0,1:T(8,128)(2,1)S(1)}, u32[]{:S(2)}, u32[]{:S(2)}) %collective-permute-start) | collective-permute-done | bytes 1310752 | tf_op jit(solution)/shard_map/ppermute | solution.py:16
  119.3 2.1 maximum_select_fusion.3
  122.2 111.6 %collective-permute-done.1 = bf16[4096,320]{0,1:T(8,128)(2,1)S(1)} collective-permute-done((bf16[4096,320]{0,1:T(8,128)(2,1)}, bf16[4096,320]{0,1:T(8,128)(2,1)S(1)}, u32[]{:S(2)}, u32[]{:S(2)}) %collective-permute-start.1) | collective-permute-done | bytes 2621472 | tf_op jit(solution)/shard_map/ppermute | solution.py:16
  233.8 11.4 fusion.3
  245.2 4.7 copy.117
  249.9 8.3 all-to-all-start.2
  259.3 67.3 %all-to-all-done.2 = bf16[16,256,384]{1,2,0:T(8,128)(2,1)} async-done(((bf16[16,256,384]{1,2,0:T(8,128)(2,1)}), bf16[16,256,384]{1,2,0:T(8,128)(2,1)}, u32[]{:S(2)}, u32[]{:S(2)}) %all-to-all-start.2) | async-done | bytes 3145760 | tf_op jit(solution)/shard_map/all_to_all | solution.py:48
  326.6 4.7 convert_bitcast_fusion.2
  331.3 2.0 copy.120
  333.4 11.4 all-to-all-start.3
  347.5 1.9 fusion.32
  349.5 4.4 copy.126
  353.9 58.8 %all-to-all-done.3 = bf16[256,16,384]{0,2,1:T(8,128)(2,1)} async-done(((bf16[256,16,384]{0,2,1:T(8,128)(2,1)}), bf16[256,16,384]{0,2,1:T(8,128)(2,1)}, u32[]{:S(2)}, u32[]{:S(2)}) %all-to-all-start.3) | async-done | bytes 3145760 | tf_op jit(solution)/shard_map/all_to_all | solution.py:54
  412.6 8.4 all-to-all-start.4
  421.0 4.7 copy.121
  425.7 6.5 fusion.10
  432.3 5.7 gather_fusion
  437.9 3.1 broadcast_select_fusion
  441.0 2.6 slice_bitcast_fusion.3
  443.6 4.7 collective-permute-start.2
  448.4 27.5 %all-to-all-done.4 = bf16[8,512,160]{2,0,1:T(8,128)(2,1)} async-done(((bf16[8,512,160]{2,0,1:T(8,128)(2,1)}), bf16[8,512,160]{2,0,1:T(8,128)(2,1)}, u32[]{:S(2)}, u32[]{:S(2)}) %all-to-all-start.4) | async-done | bytes 1310752 | tf_op jit(solution)/shard_map/all_to_all | solution.py:102
  475.8 3.5 copy.128
  479.4 4.3 copy.129
  486.8 4.4 copy.130
  491.2 4.7 all-to-all-start.5
  495.8 32.9 %collective-permute-done.2 = bf16[2,1,4096,160]{2,3,0,1:T(8,128)(2,1)} collective-permute-done((bf16[2,1,4096,160]{2,3,0,1:T(8,128)(2,1)}, bf16[2,1,4096,160]{2,3,0,1:T(8,128)(2,1)}, u32[]{:S(2)}, u32[]{:S(2)}) %collective-permute-start.2) | collective-permute-done | bytes 2621472 | tf_op jit(solution)/shard_map/ppermute | solution.py:16
  528.7 3.0 maximum_bitcast_fusion
  531.7 2.7 slice_bitcast_fusion.1
  534.4 31.8 %all-to-all-done.5 = bf16[128,32,160]{2,1,0:T(8,128)(2,1)} async-done(((bf16[128,32,160]{2,1,0:T(8,128)(2,1)}), bf16[128,32,160]{2,1,0:T(8,128)(2,1)}, u32[]{:S(2)}, u32[]{:S(2)}) %all-to-all-start.5) | async-done | bytes 1310752 | tf_op jit(solution)/shard_map/all_to_all | solution.py:106
  566.2 2.1 convert_bitcast_fusion.1
  568.3 2.3 copy.131
  570.5 5.1 copy.145
  575.6 109.2 %collective-permute-done.3 = bf16[1,2,4096,160]{2,3,1,0:T(8,128)(2,1)} collective-permute-done((bf16[1,2,4096,160]{2,3,1,0:T(8,128)(2,1)}, bf16[1,2,4096,160]{2,3,1,0:T(8,128)(2,1)}, u32[]{:S(2)}, u32[]{:S(2)}) %collective-permute-start.3) | collective-permute-done | bytes 2621472 | tf_op jit(solution)/shard_map/ppermute | solution.py:16
  684.8 4.0 convert_reduce_fusion
  688.9 2.7 multiply_reduce_fusion
  693.4 1.9 fusion.25
  695.3 4.4 copy.136
  699.6 7.0 all-to-all-start.6
  706.7 16.9 %collective-permute-done.4 = bf16[4096,160]{0,1:T(8,128)(2,1)} collective-permute-done((bf16[4096,160]{0,1:T(8,128)(2,1)}, bf16[4096,160]{0,1:T(8,128)(2,1)}, u32[]{:S(2)}, u32[]{:S(2)}) %collective-permute-start.4) | collective-permute-done | bytes 1310752 | tf_op jit(solution)/shard_map/ppermute | solution.py:16
  723.6 4.3 maximum_select_fusion.4
  727.9 25.9 %collective-permute-start.5 = (bf16[4096,320]{0,1:T(8,128)(2,1)}, bf16[4096,320]{0,1:T(8,128)(2,1)}, u32[]{:S(2)}, u32[]{:S(2)}) collective-permute-start(bf16[4096,320]{0,1:T(8,128)(2,1)} %maximum_select_fusion.4), channel_id=1, source_target_pairs={{0,2},{2,0},{1,3},{3,1},{4,6},{6,4},{5,7},{7,5},{8,10},{10,8},{9,1... | collective-permute-start | bytes 7864328 | tf_op jit(solution)/shard_map/ppermute | solution.py:16
  753.8 7.8 fusion.21
  761.6 10.0 all-to-all-done.6
  771.7 3.6 copy.138
  775.2 4.4 copy.139
  782.7 4.5 copy.140
  787.1 5.0 all-to-all-start.7
  792.5 5.1 copy.132
  797.6 68.5 %reduce-scatter.9.cloned.1.call-done = f32[40,384]{1,0:T(8,128)} async-done(((f32[640,384]{1,0:T(8,128)}), f32[40,384]{1,0:T(8,128)}) %reduce-scatter.9.cloned.1.call-update) | async-done | bytes 61456
  867.6 2.9 fusion.42
  870.5 59.9 %collective-permute-done.5 = bf16[4096,320]{0,1:T(8,128)(2,1)} collective-permute-done((bf16[4096,320]{0,1:T(8,128)(2,1)}, bf16[4096,320]{0,1:T(8,128)(2,1)}, u32[]{:S(2)}, u32[]{:S(2)}) %collective-permute-start.5) | collective-permute-done | bytes 2621472 | tf_op jit(solution)/shard_map/ppermute | solution.py:16
  930.4 8.8 fusion.11
  939.3 1.9 multiply_convert_fusion
  941.4 2.1 convert_bitcast_fusion
  944.1 2.0 fusion.18
  948.0 4.8 fusion.26
  954.0 47.3 %all-reduce.3 = (f32[160]{0:T(256)S(1)}, f32[160]{0:T(256)S(1)}) all-reduce(f32[160]{0:T(256)S(1)} %get-tuple-element.11, f32[160]{0:T(256)S(1)} %get-tuple-element.18), channel_id=1, replica_groups=mesh['seq'=16,'chan'=16] {'seq'}, use_global_device_ids=true, to_apply=%region_4.5 | all-reduce | flops 320 | bytes 2560 | tf_op jit(solution)/shard_map/psum | solution.py:152
  1001.9 16.3 %reduce-scatter.7.cloned.1.call-done = f32[384,40]{0,1:T(8,128)} async-done(((f32[384,640]{0,1:T(8,128)}), f32[384,40]{0,1:T(8,128)}) %reduce-scatter.7.cloned.1.call-update) | async-done | bytes 61456
  1019.7 188.5 %all-reduce.6.cloned.1.call-done = (f32[512,512]{1,0:T(8,128)}, f32[128,128]{1,0:T(8,128)}) async-done(((f32[512,512]{1,0:T(8,128)}, f32[128,128]{1,0:T(8,128)}), (f32[512,512]{1,0:T(8,128)}, f32[128,128]{1,0:T(8,128)})) %all-reduce.6.cloned.1.call-update) | async-done | bytes 1114128 | tf_op jit(solution)/shard_map/psum | solution.py:153
  1208.2 2.3 broadcast_multiply_fusion
  (71 shorter events, 25.6 us)
Async XLA Ops:
  8.0 225.8 %copy-start = (bf16[1,640,384]{2,1,0:T(8,128)(2,1)S(1)}, bf16[1,640,384]{2,1,0:T(8,128)(2,1)}, u32[]{:S(2)}) copy-start(bf16[1,640,384]{2,1,0:T(8,128)(2,1)} %param.22) | copy-start | bytes 1474564
  8.0 11.2 copy-start.13
  10.6 37.7 %all-to-all-start = ((bf16[16,256,160]{1,2,0:T(8,128)(2,1)}), bf16[16,256,160]{1,2,0:T(8,128)(2,1)S(1)}, u32[]{:S(2)}, u32[]{:S(2)}) async-start(bf16[16,256,160]{1,2,0:T(8,128)(2,1)} %bitcast.149), calls=%async_computation | async-start | bytes 2621440 | tf_op jit(solution)/shard_map/all_to_all | solution.py:48
  89.6 29.7 %collective-permute-start = (bf16[4096,160]{0,1:T(8,128)(2,1)S(1)}, bf16[4096,160]{0,1:T(8,128)(2,1)S(1)}, u32[]{:S(2)}, u32[]{:S(2)}) collective-permute-start(bf16[4096,160]{0,1:T(8,128)(2,1)S(1)} %bitcast.167), channel_id=1, source_target_pairs={{0,1},{1,0},{2,3},{3,2},{4,5},{5,4},{6,7},{7,6},{8,9},{9,8},{10,11... | collective-permute-start | bytes 3932168 | tf_op jit(solution)/shard_map/ppermute | solution.py:16
  121.4 112.4 %collective-permute-start.1 = (bf16[4096,320]{0,1:T(8,128)(2,1)}, bf16[4096,320]{0,1:T(8,128)(2,1)S(1)}, u32[]{:S(2)}, u32[]{:S(2)}) collective-permute-start(bf16[4096,320]{0,1:T(8,128)(2,1)} %maximum_select_fusion.3), channel_id=1, source_target_pairs={{0,2},{2,0},{1,3},{3,1},{4,6},{6,4},{5,7},{7,5},{8,10},{10,8},{9,1... | collective-permute-start | bytes 7864328 | tf_op jit(solution)/shard_map/ppermute | solution.py:16
  233.8 11.4 copy-start.17
  249.9 8.3 copy-start.12
  249.9 76.7 %all-to-all-start.2 = ((bf16[16,256,384]{1,2,0:T(8,128)(2,1)}), bf16[16,256,384]{1,2,0:T(8,128)(2,1)}, u32[]{:S(2)}, u32[]{:S(2)}) async-start(bf16[16,256,384]{1,2,0:T(8,128)(2,1)} %copy.117), calls=%async_computation.2 | async-start | bytes 6291456 | tf_op jit(solution)/shard_map/all_to_all | solution.py:48
  333.4 11.4 copy-start.8
  333.4 79.2 %all-to-all-start.3 = ((bf16[256,16,384]{0,2,1:T(8,128)(2,1)}), bf16[256,16,384]{0,2,1:T(8,128)(2,1)}, u32[]{:S(2)}, u32[]{:S(2)}) async-start(bf16[256,16,384]{0,2,1:T(8,128)(2,1)} %bitcast.158), calls=%async_computation.3 | async-start | bytes 6291456 | tf_op jit(solution)/shard_map/all_to_all | solution.py:54
  344.8 2.7 copy-start.11
  344.8 2.7 copy-start.15
  345.8 1.7 copy-start.7
  412.6 63.2 %all-to-all-start.4 = ((bf16[8,512,160]{2,0,1:T(8,128)(2,1)}), bf16[8,512,160]{2,0,1:T(8,128)(2,1)}, u32[]{:S(2)}, u32[]{:S(2)}) async-start(bf16[8,512,160]{2,0,1:T(8,128)(2,1)} %copy.126), calls=%async_computation.4 | async-start | bytes 4194304 | tf_op jit(solution)/shard_map/all_to_all | solution.py:102
  421.0 4.7 copy-start.9
  443.6 85.1 %collective-permute-start.2 = (bf16[2,1,4096,160]{2,3,0,1:T(8,128)(2,1)}, bf16[2,1,4096,160]{2,3,0,1:T(8,128)(2,1)}, u32[]{:S(2)}, u32[]{:S(2)}) collective-permute-start(bf16[2,1,4096,160]{2,3,0,1:T(8,128)(2,1)} %get-tuple-element.16), channel_id=1, source_target_pairs={{0,1},{1,0},{2,3},{3,2},{4,5},{5,4},{6,7},{7,6},{8,9},{9,8},{10,11... | collective-permute-start | bytes 7864328 | tf_op jit(solution)/shard_map/ppermute | solution.py:16
  479.4 4.3 copy-start.10
  491.2 75.0 %all-to-all-start.5 = ((bf16[128,32,160]{2,1,0:T(8,128)(2,1)}), bf16[128,32,160]{2,1,0:T(8,128)(2,1)}, u32[]{:S(2)}, u32[]{:S(2)}) async-start(bf16[128,32,160]{2,1,0:T(8,128)(2,1)} %copy.130), calls=%async_computation.5 | async-start | bytes 4194304 | tf_op jit(solution)/shard_map/all_to_all | solution.py:106
  534.4 150.4 %collective-permute-start.3 = (bf16[1,2,4096,160]{2,3,1,0:T(8,128)(2,1)}, bf16[1,2,4096,160]{2,3,1,0:T(8,128)(2,1)}, u32[]{:S(2)}, u32[]{:S(2)}) collective-permute-start(bf16[1,2,4096,160]{2,3,1,0:T(8,128)(2,1)} %get-tuple-element.14), channel_id=1, source_target_pairs={{0,2},{2,0},{1,3},{3,1},{4,6},{6,4},{5,7},{7,5},{8,10},{10,8},{9,1... | collective-permute-start | bytes 7864328 | tf_op jit(solution)/shard_map/ppermute | solution.py:16
  684.8 4.0 copy-start.3
  684.8 4.0 copy-start.4
  684.8 4.1 copy-start.5
  684.8 4.1 copy-start.14
  691.6 1.8 copy-start.2
  691.6 32.0 %collective-permute-start.4 = (bf16[4096,160]{0,1:T(8,128)(2,1)}, bf16[4096,160]{0,1:T(8,128)(2,1)}, u32[]{:S(2)}, u32[]{:S(2)}) collective-permute-start(bf16[4096,160]{0,1:T(8,128)(2,1)} %get-tuple-element.17), channel_id=1, source_target_pairs={{0,1},{1,0},{2,3},{3,2},{4,5},{5,4},{6,7},{7,6},{8,9},{9,8},{10,11... | collective-permute-start | bytes 3932168 | tf_op jit(solution)/shard_map/ppermute | solution.py:16
  699.6 72.0 %all-to-all-start.6 = ((bf16[8,512,160]{2,0,1:T(8,128)(2,1)}), bf16[8,512,160]{2,0,1:T(8,128)(2,1)}, u32[]{:S(2)}, u32[]{:S(2)}) async-start(bf16[8,512,160]{2,0,1:T(8,128)(2,1)} %copy.136), calls=%async_computation.6 | async-start | bytes 4194304 | tf_op jit(solution)/shard_map/all_to_all | solution.py:131
  706.6 159.5 %reduce-scatter.9.cloned.1.call-start = ((), (), s32[]{:S(2)}) async-start(), calls=%async_computation.11 | async-start | bytes 1044480
  706.7 47.1 %copy-start.16 = (bf16[4096,384]{1,0:T(8,128)(2,1)S(1)}, bf16[4096,384]{1,0:T(8,128)(2,1)}, u32[]{:S(2)}) copy-start(bf16[4096,384]{1,0:T(8,128)(2,1)} %param.19) | copy-start | bytes 9437188
  727.9 202.5 %collective-permute-start.5 = (bf16[4096,320]{0,1:T(8,128)(2,1)}, bf16[4096,320]{0,1:T(8,128)(2,1)}, u32[]{:S(2)}, u32[]{:S(2)}) collective-permute-start(bf16[4096,320]{0,1:T(8,128)(2,1)} %maximum_select_fusion.4), channel_id=1, source_target_pairs={{0,2},{2,0},{1,3},{3,1},{4,6},{6,4},{5,7},{7,5},{8,10},{10,8},{9,1... | collective-permute-start | bytes 7864328 | tf_op jit(solution)/shard_map/ppermute | solution.py:16
  787.1 152.1 %all-to-all-start.7 = ((bf16[128,32,160]{2,1,0:T(8,128)(2,1)}), bf16[128,32,160]{2,1,0:T(8,128)(2,1)}, u32[]{:S(2)}, u32[]{:S(2)}) async-start(bf16[128,32,160]{2,1,0:T(8,128)(2,1)} %copy.140), calls=%async_computation.7 | async-start | bytes 4194304 | tf_op jit(solution)/shard_map/all_to_all | solution.py:139
  792.1 226.1 %reduce-scatter.7.cloned.1.call-start = ((), (), s32[]{:S(2)}) async-start(), calls=%async_computation.10 | async-start | bytes 1044480
  939.2 268.9 %all-reduce.6.cloned.1.call-start = ((), (), s32[]{:S(2)}) async-start(), calls=%async_computation.12 | async-start | bytes 2228224 | tf_op jit(solution)/shard_map/psum | solution.py:153
  944.1 2.0 copy-start.6
  948.0 263.9 %copy-start.1 = (bf16[1,640,384]{2,1,0:T(8,128)(2,1)S(1)}, bf16[1,640,384]{2,1,0:T(8,128)(2,1)}, u32[]{:S(2)}) copy-start(bf16[1,640,384]{2,1,0:T(8,128)(2,1)} %param.22) | copy-start | bytes 1474564
Sparse Core Ops, SparseCore 0:
  761.8 104.3 reduce-scatter.8
  939.4 78.8 reduce-scatter.6
Sparse Core Ops, SparseCore 1:
  948.1 260.0 all-reduce.5
where the time goes:
time: 1230 us; the launch traced here: 1220 us
  waiting for transfers between devices  856 us (70%)
  starting transfers between devices  88.7 us (7%)
  blocking collectives  87.1 us (7%)
  local copies, waits for them, and re-layouts  75.8 us (6%)
  matrix products  55.6 us (5%)
  other arithmetic  40.6 us (3%)
  between operations  16.3 us (1%)
    ppermute x6, waiting for transfers between devices, from_partner(): return lax.ppermute(block, axis, route)  358 us
    psum x1, waiting for transfers between devices, body(): lax.psum((inner_terms, outer_terms), ('seq', 'chan'))  188 us
    all_to_all x2, waiting for transfers between devices, by_tokens(): lax.all_to_all(values, 'chan', split_axis=0, concat_axis=1, tiled=True)  95.9 us
    unnamed x5, waiting for transfers between devices  84.8 us
    all_to_all x1, waiting for transfers between devices, by_tokens(): lax.all_to_all(result.reshape(row_count, NB * full_width), 'chan', split_...  58.8 us
    psum x1, blocking collectives, body(): query_total, key_total = lax.psum((query_terms, key_terms), 'seq')  47.3 us
    all_to_all x1, blocking collectives, by_tokens(): lax.all_to_all(result.reshape(row_count, NB * full_width), 'chan', split_...  39.8 us
    ppermute x6, starting transfers between devices, from_partner(): return lax.ppermute(block, axis, route)  35 us
  transfers between devices with their start and end apart: 16, of which 15 were waited for; matrix products, arithmetic and copies ran while one was open for 11% of the time, Pallas kernels for 0%

commit v1 on v0

v1 whole, which is shorter than its diff:
```python
import jax
import jax.numpy as jnp
from jax import lax
from jax.sharding import PartitionSpec as P

BF = jnp.bfloat16
F32 = jnp.float32
BLOCKS = 4
GROUP = 4
SEQ = 16
CHAN = 16
Z_LO = [0, 1, 2, 3]
Y = [0, 4, 8, 12]
CORE = [0, 16]
X = [0, 32, 64, 96]
Z_HI = [0, 128]


def join(high, low):
    return [h ^ l for h in high for l in low]


def swap(value, mask):
    if mask == 0:
        return value
    route = [(i, i ^ mask) for i in range(SEQ * CHAN)]
    return lax.ppermute(value, ("seq", "chan"), route)


def spread(take, me, masks, out_shape, dtype, axis):
    size = out_shape[axis] // len(masks)
    out = jnp.zeros(out_shape, dtype)
    for step, mask in enumerate(masks):
        other = jnp.bitwise_xor(me, step)
        arrived = swap(take(other), mask)
        out = lax.dynamic_update_slice_in_dim(out, arrived, other * size, axis)
    return out


def part_of(value, index, count, axis):
    size = value.shape[axis] // count
    return lax.dynamic_slice_in_dim(value, index * size, size, axis)


def sum_spread(take, me, masks):
    total = None
    for step, mask in enumerate(masks):
        piece = take(jnp.bitwise_xor(me, step))
        arrived = swap(piece.astype(BF), mask).astype(F32) if mask else piece.astype(F32)
        total = arrived if total is None else total + arrived
    return total


def sum_spread_f32(take, me, masks):
    total = None
    for step, mask in enumerate(masks):
        arrived = swap(take(jnp.bitwise_xor(me, step)), mask)
        total = arrived if total is None else total + arrived
    return total


def gather(value, me, masks, axis):
    shape = list(value.shape)
    shape[axis] *= len(masks)
    return spread(lambda other: value, me, masks, tuple(shape), value.dtype, axis)


def seq_exchange(value, core, zx):
    rows, width = value.shape[1:]
    by_core = value.reshape(8, 2, rows, width)
    near = spread(
        lambda other: lax.dynamic_index_in_dim(by_core, other, 1, keepdims=True).transpose(1, 0, 2, 3),
        core, CORE, (2, 8, rows, width), value.dtype, 0,
    )
    near = near.transpose(1, 0, 2, 3)
    far = spread(
        lambda other: lax.dynamic_index_in_dim(near, other, 0, keepdims=True),
        zx, join(Z_HI, X), (8, 2, rows, width), value.dtype, 0,
    )
    return far.reshape(16, rows, width)


def lower_mask(size):
    return jnp.arange(size)[:, None] >= jnp.arange(size)[None, :]


def weight_total(terms, core, x, z_hi, z_lo):
    split = terms.reshape(8, 2, terms.shape[0] // 16, terms.shape[1])
    pair = sum_spread(lambda other: lax.dynamic_index_in_dim(split, other, 1, keepdims=False), core, CORE)
    pair = pair.reshape((2, 4) + pair.shape[1:])
    line = sum_spread(lambda other: lax.dynamic_index_in_dim(pair, other, 1, keepdims=False), x, X)

    def take(other):
        rows = lax.dynamic_index_in_dim(line, other // 4, 0, keepdims=False)
        return part_of(rows, other % 4, 4, 1)

    return sum_spread(take, z_hi * 4 + z_lo, join(Z_HI, Z_LO))


def body(
    layer_input,
    query_scale,
    key_scale,
    twiddle,
    seq_inner,
    seq_outer,
    grad_output,
    hidden_pre,
    up_right,
    up_left,
    down_right,
    down_left,
):
    outer_here, inner_len = twiddle.shape
    tokens, width = layer_input.shape
    outer_len = seq_outer.shape[0]
    hidden = hidden_pre.shape[1]
    quarter = tokens // GROUP
    seq = lax.axis_index("seq")
    chan = lax.axis_index("chan")
    z_lo, y = chan % 4, chan // 4
    core, x, z_hi = seq % 2, (seq // 2) % 4, seq // 8
    zx = seq // 2
    mine = width // SEQ
    inner_mask = lower_mask(inner_len)
    outer_mask = lower_mask(outer_len)
    inner_tri = jnp.where(inner_mask, seq_inner, jnp.zeros_like(seq_inner))
    outer_tri = jnp.where(outer_mask, seq_outer, jnp.zeros_like(seq_outer))
    layer_t = layer_input.T
    grad_t = grad_output.T

    pre_values = spread(
        lambda other: part_of(hidden_pre, other, 4, 0), z_lo, Z_LO, (quarter, 4 * hidden), BF, 1
    )

    grad_split = grad_t.reshape(width, GROUP, BLOCKS, quarter // BLOCKS)
    grad_blocks = spread(
        lambda other: lax.dynamic_index_in_dim(grad_split, other, 2, keepdims=False)[None],
        y, Y, (BLOCKS, width, GROUP, quarter // BLOCKS), BF, 0,
    )
    left_here = part_of(down_left, z_lo, 4, 2).astype(F32)
    grad_blocks = grad_blocks.astype(F32)
    down_mix = jnp.stack(
        [
            sum(left_here[j, k][:, None, None] * grad_blocks[j] for j in range(BLOCKS)).astype(BF)
            for k in range(BLOCKS)
        ]
    )
    down_here = spread(
        lambda other: lax.dynamic_index_in_dim(down_mix, other, 0, keepdims=False)[:, :, None],
        y, Y, (width, GROUP, BLOCKS, quarter // BLOCKS), BF, 2,
    ).reshape(width, tokens)
    down_grad = spread(
        lambda other: part_of(down_here, other, 4, 1), z_lo, Z_LO, (4 * width, quarter), BF, 0
    )

    right = jnp.stack([down_right[0], up_right[0].T])
    right = part_of(right, seq % 8, 8, 1)
    right = gather(right, z_lo, Z_LO, 2)
    right = gather(right, core, CORE, 1)
    right = gather(right, x, X, 1)

    layer_rows = layer_t.reshape(SEQ, mine * outer_here, inner_len)
    layer_cols = seq_exchange(layer_rows, core, zx)

    def to_cols(value):
        return (
            value.reshape(SEQ, mine, outer_here, inner_len)
            .transpose(1, 0, 2, 3)
            .reshape(mine, outer_len, inner_len)
        )

    def to_rows(value):
        return (
            value.reshape(mine, SEQ, outer_here, inner_len)
            .transpose(1, 0, 2, 3)
            .reshape(SEQ, mine * outer_here, inner_len)
        )

    twiddle_all = gather(gather(twiddle, core, CORE, 0), zx, join(Z_HI, X), 0)
    layer_cols = to_cols(layer_cols).astype(F32)
    key_mine = part_of(key_scale, seq, SEQ, 0)[:, None, None]
    query_mine = part_of(query_scale, seq, SEQ, 0)
    key_input = (layer_cols * key_mine).astype(BF)
    first_pass = (
        jnp.einsum("bk,cak->cab", inner_tri, key_input, preferred_element_type=F32) * twiddle_all
    ).astype(BF)
    conv_cols = jnp.einsum("ij,cjb->cib", outer_tri, first_pass, preferred_element_type=F32).astype(BF)
    convolved = seq_exchange(to_rows(conv_cols), core, zx).reshape(width, tokens).astype(F32)
    inputs = layer_t.astype(F32)
    query_col = query_scale[:, None]
    mixed = (inputs + inputs * query_col * convolved).astype(BF)
    mixed_rows = spread(
        lambda other: part_of(mixed, other, 4, 1), z_lo, Z_LO, (4 * width, quarter), BF, 0
    )

    hidden_grad = jnp.einsum("pt,pq->tq", down_grad, right[0], preferred_element_type=F32)
    pre_f = pre_values.astype(F32)
    activated = jax.nn.gelu(pre_f).astype(BF)
    pre_grad = jax.vjp(jax.nn.gelu, pre_f)[1](hidden_grad)[0].astype(BF)
    down_terms = jnp.einsum("pt,tq->pq", down_grad, activated, preferred_element_type=F32)
    pre_blocks = spread(
        lambda other: part_of(pre_grad, other, 4, 0)[None],
        y, Y, (BLOCKS, quarter // BLOCKS, 4 * hidden), BF, 0,
    ).astype(F32)
    left_up = up_left.astype(F32)
    right_mix = jnp.stack(
        [
            sum(left_up[j, k][None, :] * pre_blocks[j] for j in range(BLOCKS)).astype(BF)
            for k in range(BLOCKS)
        ]
    )
    right_grad = spread(
        lambda other: lax.dynamic_index_in_dim(right_mix, other, 0, keepdims=False),
        y, Y, (quarter, 4 * hidden), BF, 0,
    )
    partial_value = jnp.einsum("pq,tq->pt", right[1], right_grad, preferred_element_type=F32).astype(BF)
    arrived = spread(
        lambda other: part_of(partial_value, other, 4, 0), z_lo, Z_LO, (width, tokens), BF, 1
    )
    up_terms = jnp.einsum("pt,tq->pq", mixed_rows, right_grad, preferred_element_type=F32)

    mix_grad = grad_t.astype(F32) + arrived.astype(F32)
    conv_grad = (mix_grad * inputs * query_col).astype(BF)
    conv_grad = to_cols(seq_exchange(conv_grad.reshape(SEQ, mine * outer_here, inner_len), core, zx))
    query_terms = jnp.sum(conv_grad.astype(F32) * conv_cols.astype(F32), axis=(1, 2)) / query_mine
    first_grad = jnp.einsum("ij,cib->cjb", outer_tri, conv_grad, preferred_element_type=F32).astype(BF)
    outer_terms = jnp.einsum("cib,cjb->ij", conv_grad, first_pass, preferred_element_type=F32)
    back_pass = (first_grad.astype(F32) * twiddle_all).astype(BF)
    key_grad = jnp.einsum("bk,cab->cak", inner_tri, back_pass, preferred_element_type=F32)
    inner_terms = jnp.einsum("cab,cak->bk", back_pass, key_input, preferred_element_type=F32)
    key_terms = jnp.sum(key_grad * layer_cols, axis=(1, 2))
    key_back = seq_exchange(to_rows((key_grad * key_mine).astype(BF)), core, zx)
    key_back = key_back.reshape(width, tokens).astype(F32)
    grad_input = (mix_grad * (1.0 + query_col * convolved) + key_back).astype(BF).T

    side = 128
    count = inner_len // side
    tiles = [
        inner_terms[i * side : (i + 1) * side, j * side : (j + 1) * side]
        for i in range(count)
        for j in range(i + 1)
    ]
    model = CHAN * width
    at = chan * width + seq * mine
    scales = jnp.zeros((2, model), F32)
    scales = lax.dynamic_update_slice(scales, jnp.stack([query_terms, key_terms]), (0, at))
    scale_rows = 2 * model // side
    sums = jnp.concatenate(tiles + [outer_terms, scales.reshape(scale_rows, side)], axis=0)
    whole_rows = -(-sums.shape[0] // 512) * 512
    sums = jnp.pad(sums, ((0, whole_rows - sums.shape[0]), (0, 0)))
    for me, masks in ((y, Y), (z_lo, Z_LO), (x, X)):
        sums = sum_spread_f32(lambda other, sums=sums: part_of(sums, other, 4, 0), me, masks)
    sums = sum_spread_f32(lambda other: sums, z_hi * 2 + core, join(Z_HI, CORE))
    for me, masks in ((x, X), (z_lo, Z_LO), (y, Y)):
        sums = gather(sums, me, masks, 0)
    blank = jnp.zeros((side, side), F32)
    rows, taken = [], 0
    for i in range(count):
        rows.append(
            jnp.concatenate(
                [sums[(taken + j) * side : (taken + j + 1) * side] for j in range(i + 1)]
                + [blank] * (count - 1 - i),
                axis=1,
            )
        )
        taken += i + 1
    inner_total = jnp.where(inner_mask, jnp.concatenate(rows, axis=0), 0.0)
    outer_total = jnp.where(outer_mask, sums[taken * side : (taken + 1) * side], 0.0)
    scale_total = sums[(taken + 1) * side : (taken + 1) * side + scale_rows].reshape(2, model)
    scale_total = lax.dynamic_slice_in_dim(scale_total, chan * width, width, 1)

    token_scale = (SEQ * tokens) ** (-0.5)
    grad_down = weight_total(down_terms, core, x, z_hi, z_lo) * token_scale
    grad_up = weight_total(up_terms, core, x, z_hi, z_lo).T * token_scale
    return (
        grad_input,
        grad_up[None],
        grad_down[None],
        scale_total[0] * token_scale,
        scale_total[1] * token_scale,
        inner_total * (outer_len * model) ** (-0.5),
        outer_total * (inner_len * model) ** (-0.5),
    )


def solution(mesh):
    return jax.shard_map(
        body,
        mesh=mesh,
        in_specs=(
            P("seq", "chan"),
            P("chan"),
            P("chan"),
            P("seq", None),
            P(),
            P(),
            P("seq", "chan"),
            P("seq", "chan"),
            P("chan", None, None),
            P(),
            P("chan", None, None),
            P(),
        ),
        out_specs=(
            P("seq", "chan"),
            P("chan", None, "seq"),
            P("chan", "seq", None),
            P("chan"),
            P("chan"),
            P(),
            P(),
        ),
        check_vma=False,
    )
```

time: 1230 us -> 718 us (0.58)
  waiting for transfers between devices: 856 us -> 239 us
  starting transfers between devices: 88.7 us -> 241 us
  local copies, waits for them, and re-layouts: 75.8 us -> 169 us
  blocking collectives: 87.1 us -> 0 us
  matrix products: 55.6 us -> 30.5 us
  other arithmetic: 40.6 us -> 21.9 us
  between operations: 16.3 us -> 2.67 us
    all_to_all x7 -> x0, waiting for transfers between devices: 224 us -> none  [the longest x2 95.9 us: by_tokens(): lax.all_to_all(values, 'chan', split_axis=0, concat_axis=1, tiled=True)]
    ppermute x6 -> x114, starting transfers between devices: 35 us -> 241 us  [swap(): return lax.ppermute(value, ('seq', 'chan'), route)]
    psum x1 -> x0, waiting for transfers between devices: 188 us -> none  [body(): lax.psum((inner_terms, outer_terms), ('seq', 'chan'))]
    ppermute x6 -> x114, waiting for transfers between devices: 358 us -> 239 us  [swap(): return lax.ppermute(value, ('seq', 'chan'), route)]
    dynamic_update_slice x0 -> x99, local copies, waits for them, and re-layouts: none -> 98.6 us  [the longest x98 98.4 us: spread(): out = lax.dynamic_update_slice_in_dim(out, arrived, other * size, axis)]
    unnamed x5 -> x0, waiting for transfers between devices: 84.8 us -> none
    all_to_all x7 -> x0, starting transfers between devices: 53.3 us -> none  [the longest x2 16.9 us: by_tokens(): lax.all_to_all(values, 'chan', split_axis=0, concat_axis=1, tiled=True)]
    psum x1 -> x0, blocking collectives: 47.3 us -> none  [body(): query_total, key_total = lax.psum((query_terms, key_terms), 'seq')]
  transfers between devices with their start and end apart: 16 -> 114, of which waited for: 15 -> 57; matrix products, arithmetic and copies ran while one was open for 11% -> 27% of each run, Pallas kernels for 0% -> 0%
where the time goes in v1:
time: 718 us; the launch traced here: 704 us
  starting transfers between devices  241 us (34%)
  waiting for transfers between devices  239 us (33%)
  local copies, waits for them, and re-layouts  169 us (24%)
  matrix products  30.5 us (4%)
  other arithmetic  21.9 us (3%)
    ppermute x114, starting transfers between devices, swap(): return lax.ppermute(value, ('seq', 'chan'), route)  241 us
    ppermute x114, waiting for transfers between devices, swap(): return lax.ppermute(value, ('seq', 'chan'), route)  239 us
    dynamic_update_slice x98, local copies, waits for them, and re-layouts, spread(): out = lax.dynamic_update_slice_in_dim(out, arrived, other * size, axis)  98.4 us
  transfers between devices with their start and end apart: 114, of which 57 were waited for; matrix products, arithmetic and copies ran while one was open for 27% of the time, Pallas kernels for 0%

profile of v1, /device:TPU:32, one launch (start us, length us, event | category | flops | bytes accessed | tf_op | source)
XLA Modules:
  0.0 704.0 jit_solution(13061423586566828618)
XLA Ops:
  7.7 3.8 constant_dynamic-slice_fusion.21
  38.2 3.0 collective-permute-start.38
  49.1 5.9 collective-permute-start.40
  57.2 6.1 collective-permute-start.41
  63.3 3.3 collective-permute-done.41
  66.6 7.2 %collective-permute-start.42 = (f32[16,512]{1,0:T(8,128)}, f32[16,512]{1,0:T(8,128)S(1)}, u32[]{:S(2)}, u32[]{:S(2)}) collective-permute-start(f32[16,512]{1,0:T(8,128)} %constant_dynamic-update-slice_fusion.42), channel_id=1, source_target_pairs={{0,192},{1,193},{2,194},{3,195},{4,196},{5,197},{6,198},{7,199},{8... | collective-permute-start | bytes 98312 | tf_op jit(solution)/shard_map/ppermute | solution.py:27
  73.7 3.3 collective-permute-done.42
  77.0 8.2 %collective-permute-start.43 = (f32[16,512]{1,0:T(8,128)}, f32[16,512]{1,0:T(8,128)S(1)}, u32[]{:S(2)}, u32[]{:S(2)}) collective-permute-start(f32[16,512]{1,0:T(8,128)} %constant_dynamic-update-slice_fusion.42), channel_id=1, source_target_pairs={{0,224},{1,225},{2,226},{3,227},{4,228},{5,229},{6,230},{7,231},{8... | collective-permute-start | bytes 98312 | tf_op jit(solution)/shard_map/ppermute | solution.py:27
  108.2 4.2 collective-permute-start.11
  113.8 13.5 %dynamic_update_slice.345 = bf16[160,4,4,256]{3,2,1,0:T(4,128)(2,1)} dynamic-update-slice(bf16[160,4,4,256]{3,2,1,0:T(4,128)(2,1)} %broadcast_in_dim.107, bf16[160,4,1,256]{3,2,1,0:T(2,128)(2,1)S(1)} %copy.43, s32[]{:T(128)} %constant.688.clone.1, s32[]{:T(128)} %constant.688.clone.1, s32[]{:T(128)S(6)} %select_n.586, s32[]{:T(128)} %constant.688.clone.1) | dynamic-update-slice | bytes 655364 | tf_op jit(solution)/shard_map/dynamic_update_slice | solution.py:36
  137.9 13.5 %dynamic_update_slice.346 = bf16[160,4,4,256]{3,2,1,0:T(4,128)(2,1)} dynamic-update-slice(bf16[160,4,4,256]{3,2,1,0:T(4,128)(2,1)} %dynamic_update_slice.345, bf16[160,4,1,256]{3,2,1,0:T(2,128)(2,1)S(1)} %copy.44, s32[]{:T(128)} %constant.688.clone.1, s32[]{:T(128)} %constant.688.clone.1, s32[]{:T(128)S(6)} %select_n.587, s32[]{:T(128)} %constant.688.clone.1) | dynamic-update-slice | bytes 655364 | tf_op jit(solution)/shard_map/dynamic_update_slice | solution.py:36
  153.1 13.5 %dynamic_update_slice.347 = bf16[160,4,4,256]{3,2,1,0:T(4,128)(2,1)} dynamic-update-slice(bf16[160,4,4,256]{3,2,1,0:T(4,128)(2,1)} %dynamic_update_slice.346, bf16[160,4,1,256]{3,2,1,0:T(2,128)(2,1)S(1)} %copy.45, s32[]{:T(128)} %constant.688.clone.1, s32[]{:T(128)} %constant.688.clone.1, s32[]{:T(128)S(6)} %select_n.588, s32[]{:T(128)} %constant.688.clone.1) | dynamic-update-slice | bytes 655364 | tf_op jit(solution)/shard_map/dynamic_update_slice | solution.py:36
  168.3 13.5 %dynamic_update_slice.348 = bf16[160,4,4,256]{3,2,1,0:T(4,128)(2,1)} dynamic-update-slice(bf16[160,4,4,256]{3,2,1,0:T(4,128)(2,1)} %dynamic_update_slice.347, bf16[160,4,1,256]{3,2,1,0:T(2,128)(2,1)S(1)} %copy.46, s32[]{:T(128)} %constant.688.clone.1, s32[]{:T(128)} %constant.688.clone.1, s32[]{:T(128)S(6)} %select_n.589, s32[]{:T(128)} %constant.688.clone.1) | dynamic-update-slice | bytes 655364 | tf_op jit(solution)/shard_map/dynamic_update_slice | solution.py:36
  181.9 3.7 reshape.309
  193.1 3.9 collective-permute-start.5
  203.5 12.7 %collective-permute-start.6 = (bf16[2,160,1536]{2,1,0:T(8,128)(2,1)}, bf16[2,160,1536]{2,1,0:T(8,128)(2,1)S(1)}, u32[]{:S(2)}, u32[]{:S(2)}) collective-permute-start(bf16[2,160,1536]{2,1,0:T(8,128)(2,1)} %constant_dynamic-update-slice_fusion.78), channel_id=1, source_target_pairs={{0,96},{1,97},{2,98},{3,99},{4,100},{5,101},{6,102},{7,103},{8,104... | collective-permute-start | bytes 2949128 | tf_op jit(solution)/shard_map/ppermute | solution.py:27
  221.5 6.7 collective-permute-done.15
  232.9 5.9 collective-permute-start.32
  242.6 6.2 collective-permute-start.33
  249.8 8.6 %fusion.3 = bf16[1024,1536]{1,0:T(8,128)(2,1)S(1)} fusion(bf16[1024,1536]{1,0:T(8,128)(2,1)} %constant_dynamic-update-slice_fusion.64, bf16[640,1024]{1,0:T(8,128)(2,1)S(1)} %constant_dynamic-update-slice_fusion.67, bf16[2,640,1536]{2,1,0:T(8,128)(2,1)} %constant_dynamic-update-slice_fusion.74), kind=kOutput, calls=%fused_computation.8 | convolution fusion | flops 2046296064 | bytes 9568256 | tf_op jit(solution)/shard_map/pt,pq->tq/dot_general | solution.py:197
  258.8 3.2 collective-permute-start.34
  262.1 4.5 collective-permute-start.20
  266.6 6.0 collective-permute-start.35
  273.3 5.9 collective-permute-done.19
  279.3 17.9 %collective-permute-done.20 = bf16[1,256,1536]{2,1,0:T(8,128)(2,1)S(1)} collective-permute-done((bf16[1,256,1536]{2,1,0:T(8,128)(2,1)S(1)}, bf16[1,256,1536]{2,1,0:T(8,128)(2,1)S(1)}, u32[]{:S(2)}, u32[]{:S(2)}) %collective-permute-start.20) | collective-permute-done | bytes 786464 | tf_op jit(solution)/shard_map/ppermute | solution.py:27
  297.2 11.2 %collective-permute-done.21 = bf16[1,256,1536]{2,1,0:T(8,128)(2,1)S(1)} collective-permute-done((bf16[1,256,1536]{2,1,0:T(8,128)(2,1)S(1)}, bf16[1,256,1536]{2,1,0:T(8,128)(2,1)S(1)}, u32[]{:S(2)}, u32[]{:S(2)}) %collective-permute-start.21) | collective-permute-done | bytes 786464 | tf_op jit(solution)/shard_map/ppermute | solution.py:27
  319.2 13.4 %collective-permute-done.22 = bf16[256,1536]{1,0:T(8,128)(2,1)S(1)} collective-permute-done((bf16[256,1536]{1,0:T(8,128)(2,1)S(1)}, bf16[256,1536]{1,0:T(8,128)(2,1)S(1)}, u32[]{:S(2)}, u32[]{:S(2)}) %collective-permute-start.22) | collective-permute-done | bytes 786464 | tf_op jit(solution)/shard_map/ppermute | solution.py:27
  332.6 12.9 %collective-permute-done.23 = bf16[256,1536]{1,0:T(8,128)(2,1)S(1)} collective-permute-done((bf16[256,1536]{1,0:T(8,128)(2,1)S(1)}, bf16[256,1536]{1,0:T(8,128)(2,1)S(1)}, u32[]{:S(2)}, u32[]{:S(2)}) %collective-permute-start.23) | collective-permute-done | bytes 786464 | tf_op jit(solution)/shard_map/ppermute | solution.py:27
  348.3 4.9 fusion.21
  354.7 4.4 fusion.10
  364.7 13.7 %collective-permute-done.26 = bf16[160,1024]{1,0:T(8,128)(2,1)S(1)} collective-permute-done((bf16[160,1024]{1,0:T(8,128)(2,1)S(1)}, bf16[160,1024]{1,0:T(8,128)(2,1)S(1)}, u32[]{:S(2)}, u32[]{:S(2)}) %collective-permute-start.26) | collective-permute-done | bytes 327712 | tf_op jit(solution)/shard_map/ppermute | solution.py:27
  378.4 5.8 collective-permute-done.27
  387.1 3.3 reshape_reshape.20
  393.9 4.3 collective-permute-start.84
  402.7 7.5 %collective-permute-done.84 = bf16[2,40,1536]{2,1,0:T(8,128)(2,1)S(1)} collective-permute-done((bf16[2,40,1536]{2,1,0:T(8,128)(2,1)S(1)}, bf16[2,40,1536]{2,1,0:T(8,128)(2,1)S(1)}, u32[]{:S(2)}, u32[]{:S(2)}) %collective-permute-start.84) | collective-permute-done | bytes 245792 | tf_op jit(solution)/shard_map/ppermute | solution.py:27
  415.7 6.4 collective-permute-start.57
  422.9 8.0 %collective-permute-start.59 = (bf16[1,2,80,512]{3,2,1,0:T(8,128)(2,1)S(1)}, bf16[1,2,80,512]{3,2,1,0:T(8,128)(2,1)S(1)}, u32[]{:S(2)}, u32[]{:S(2)}) collective-permute-start(bf16[1,2,80,512]{3,2,1,0:T(8,128)(2,1)S(1)} %get-tuple-element.80), channel_id=1, source_target_pairs={{0,224},{1,225},{2,226},{3,227},{4,228},{5,229},{6,230},{7,231},{8... | collective-permute-start | bytes 491528 | tf_op jit(solution)/shard_map/ppermute | solution.py:27
  430.9 8.9 %collective-permute-done.57 = bf16[1,2,80,512]{3,2,1,0:T(8,128)(2,1)S(1)} collective-permute-done((bf16[1,2,80,512]{3,2,1,0:T(8,128)(2,1)S(1)}, bf16[1,2,80,512]{3,2,1,0:T(8,128)(2,1)S(1)}, u32[]{:S(2)}, u32[]{:S(2)}) %collective-permute-start.57) | collective-permute-done | bytes 163872 | tf_op jit(solution)/shard_map/ppermute | solution.py:27
  439.9 5.2 collective-permute-done.58
  465.5 4.4 collective-permute-start.94
  473.4 4.7 collective-permute-done.94
  495.9 4.5 collective-permute-start.104
  517.1 3.5 collective-permute-start.64
  524.5 4.5 collective-permute-done.64
  528.9 7.3 %collective-permute-start.66 = (bf16[1,2,80,512]{3,2,1,0:T(8,128)(2,1)S(1)}, bf16[1,2,80,512]{3,2,1,0:T(8,128)(2,1)S(1)}, u32[]{:S(2)}, u32[]{:S(2)}) collective-permute-start(bf16[1,2,80,512]{3,2,1,0:T(8,128)(2,1)S(1)} %get-tuple-element.74), channel_id=1, source_target_pairs={{0,192},{1,193},{2,194},{3,195},{4,196},{5,197},{6,198},{7,199},{8... | collective-permute-start | bytes 491528 | tf_op jit(solution)/shard_map/ppermute | solution.py:27
  536.9 5.7 collective-permute-start.67
  546.0 5.1 collective-permute-done.67
  554.2 3.9 collective-permute-done.46
  558.0 6.5 collective-permute-start.48
  565.9 7.9 %collective-permute-done.48 = bf16[1,2,80,512]{3,2,1,0:T(8,128)(2,1)S(1)} collective-permute-done((bf16[1,2,80,512]{3,2,1,0:T(8,128)(2,1)S(1)}, bf16[1,2,80,512]{3,2,1,0:T(8,128)(2,1)S(1)}, u32[]{:S(2)}, u32[]{:S(2)}) %collective-permute-start.48) | collective-permute-done | bytes 163872 | tf_op jit(solution)/shard_map/ppermute | solution.py:27
  580.7 3.3 reshape.321
  584.0 5.2 collective-permute-done.50
  592.2 3.5 collective-permute-start.107
  596.4 3.3 reshape.320
  599.7 5.1 fusion.15
  610.1 5.6 collective-permute-done.68
  617.3 12.9 %collective-permute-done.69 = bf16[160,1024]{1,0:T(8,128)(2,1)S(1)} collective-permute-done((bf16[160,1024]{1,0:T(8,128)(2,1)S(1)}, bf16[160,1024]{1,0:T(8,128)(2,1)S(1)}, u32[]{:S(2)}, u32[]{:S(2)}) %collective-permute-start.69) | collective-permute-done | bytes 327712 | tf_op jit(solution)/shard_map/ppermute | solution.py:27
  630.2 4.0 collective-permute-start.108
  639.0 5.1 collective-permute-done.109
  646.5 5.1 collective-permute-start.89
  651.7 3.6 collective-permute-start.91
  658.9 3.3 collective-permute-done.92
  664.2 6.7 collective-permute-done.112
  691.2 3.7 collective-permute-start.79
  (509 shorter events, 279.1 us)
Async XLA Ops:
  2.9 87.4 %collective-permute-start = (bf16[2,80,384]{2,1,0:T(8,128)(2,1)}, bf16[2,80,384]{2,1,0:T(8,128)(2,1)}, u32[]{:S(2)}, u32[]{:S(2)}) collective-permute-start(bf16[2,80,384]{2,1,0:T(8,128)(2,1)} %get-tuple-element.26), channel_id=1, source_target_pairs={{0,1},{1,0},{2,3},{3,2},{4,5},{5,4},{6,7},{7,6},{8,9},{9,8},{10,11... | collective-permute-start | bytes 368648 | tf_op jit(solution)/shard_map/ppermute | solution.py:27
  4.7 87.4 %collective-permute-start.1 = (bf16[2,80,384]{2,1,0:T(8,128)(2,1)}, bf16[2,80,384]{2,1,0:T(8,128)(2,1)}, u32[]{:S(2)}, u32[]{:S(2)}) collective-permute-start(bf16[2,80,384]{2,1,0:T(8,128)(2,1)} %get-tuple-element.26), channel_id=1, source_target_pairs={{0,2},{1,3},{2,0},{3,1},{4,6},{5,7},{6,4},{7,5},{8,10},{9,11},{10,... | collective-permute-start | bytes 368648 | tf_op jit(solution)/shard_map/ppermute | solution.py:27
  6.2 89.8 %collective-permute-start.2 = (bf16[2,80,384]{2,1,0:T(8,128)(2,1)}, bf16[2,80,384]{2,1,0:T(8,128)(2,1)}, u32[]{:S(2)}, u32[]{:S(2)}) collective-permute-start(bf16[2,80,384]{2,1,0:T(8,128)(2,1)} %get-tuple-element.26), channel_id=1, source_target_pairs={{0,3},{1,2},{2,1},{3,0},{4,7},{5,6},{6,5},{7,4},{8,11},{9,10},{10,... | collective-permute-start | bytes 368648 | tf_op jit(solution)/shard_map/ppermute | solution.py:27
  12.4 85.3 %collective-permute-start.7 = (bf16[1,160,4,256]{3,1,2,0:T(8,128)(2,1)}, bf16[1,160,4,256]{3,1,2,0:T(8,128)(2,1)}, u32[]{:S(2)}, u32[]{:S(2)}) collective-permute-start(bf16[1,160,4,256]{3,1,2,0:T(8,128)(2,1)} %bitcast.370), channel_id=1, source_target_pairs={{0,4},{1,5},{2,6},{3,7},{4,0},{5,1},{6,2},{7,3},{8,12},{9,13},{10,... | collective-permute-start | bytes 983048 | tf_op jit(solution)/shard_map/ppermute | solution.py:27
  14.0 19.5 %collective-permute-start.36 = (f32[8,512]{1,0:T(8,128)S(1)}, f32[8,512]{1,0:T(8,128)S(1)}, u32[]{:S(2)}, u32[]{:S(2)}) collective-permute-start(f32[8,512]{1,0:T(8,128)S(1)} %copy-done.39), channel_id=1, source_target_pairs={{0,16},{1,17},{2,18},{3,19},{4,20},{5,21},{6,22},{7,23},{8,24},{9,... | collective-permute-start | bytes 49160 | tf_op jit(solution)/shard_map/ppermute | solution.py:27
  87.3 12.5 %collective-permute-start.8 = (bf16[1,160,4,256]{3,1,2,0:T(8,128)(2,1)}, bf16[1,160,4,256]{3,1,2,0:T(8,128)(2,1)S(1)}, u32[]{:S(2)}, u32[]{:S(2)}) collective-permute-start(bf16[1,160,4,256]{3,1,2,0:T(8,128)(2,1)} %bitcast.394), channel_id=1, source_target_pairs={{0,8},{1,9},{2,10},{3,11},{4,12},{5,13},{6,14},{7,15},{8,0},{9,1},... | collective-permute-start | bytes 983048 | tf_op jit(solution)/shard_map/ppermute | solution.py:27
  92.1 101.0 %collective-permute-start.16 = (bf16[1024,384]{1,0:T(8,128)(2,1)}, bf16[1024,384]{1,0:T(8,128)(2,1)}, u32[]{:S(2)}, u32[]{:S(2)}) collective-permute-start(bf16[1024,384]{1,0:T(8,128)(2,1)} %get-tuple-element.38), channel_id=1, source_target_pairs={{0,1},{1,0},{2,3},{3,2},{4,5},{5,4},{6,7},{7,6},{8,9},{9,8},{10,11... | collective-permute-start | bytes 2359304 | tf_op jit(solution)/shard_map/ppermute | solution.py:27
  96.0 90.9 %collective-permute-start.28 = (bf16[1,8,80,512]{3,2,0,1:T(8,128)(2,1)}, bf16[1,8,80,512]{3,2,0,1:T(8,128)(2,1)}, u32[]{:S(2)}, u32[]{:S(2)}) collective-permute-start(bf16[1,8,80,512]{3,2,0,1:T(8,128)(2,1)} %dynamic-slice_bitcast_fusion.9), channel_id=1, source_target_pairs={{0,16},{1,17},{2,18},{3,19},{4,20},{5,21},{6,22},{7,23},{8,24},{9,... | collective-permute-start | bytes 1966088 | tf_op jit(solution)/shard_map/ppermute | solution.py:27
  97.6 29.7 %collective-permute-start.3 = (bf16[2,80,1536]{2,1,0:T(8,128)(2,1)}, bf16[2,80,1536]{2,1,0:T(8,128)(2,1)}, u32[]{:S(2)}, u32[]{:S(2)}) collective-permute-start(bf16[2,80,1536]{2,1,0:T(8,128)(2,1)} %constant_dynamic-update-slice_fusion.80), channel_id=1, source_target_pairs={{0,16},{1,17},{2,18},{3,19},{4,20},{5,21},{6,22},{7,23},{8,24},{9,... | collective-permute-start | bytes 1474568 | tf_op jit(solution)/shard_map/ppermute | solution.py:27
  105.5 23.9 %collective-permute-start.10 = (bf16[160,4,1,256]{3,0,2,1:T(8,128)(2,1)}, bf16[160,4,1,256]{3,0,2,1:T(8,128)(2,1)}, u32[]{:S(2)}, u32[]{:S(2)}) collective-permute-start(bf16[160,4,1,256]{3,0,2,1:T(8,128)(2,1)} %get-tuple-element.97), channel_id=1, source_target_pairs={{0,4},{1,5},{2,6},{3,7},{4,0},{5,1},{6,2},{7,3},{8,12},{9,13},{10,... | collective-permute-start | bytes 983048 | tf_op jit(solution)/shard_map/ppermute | solution.py:27
  108.2 43.2 %collective-permute-start.11 = (bf16[160,4,1,256]{3,0,2,1:T(8,128)(2,1)}, bf16[160,4,1,256]{3,0,2,1:T(8,128)(2,1)}, u32[]{:S(2)}, u32[]{:S(2)}) collective-permute-start(bf16[160,4,1,256]{3,0,2,1:T(8,128)(2,1)} %get-tuple-element.96), channel_id=1, source_target_pairs={{0,8},{1,9},{2,10},{3,11},{4,12},{5,13},{6,14},{7,15},{8,0},{9,1},... | collective-permute-start | bytes 983048 | tf_op jit(solution)/shard_map/ppermute | solution.py:27
  127.3 39.4 %collective-permute-start.12 = (bf16[160,4,1,256]{3,0,2,1:T(8,128)(2,1)}, bf16[160,4,1,256]{3,0,2,1:T(8,128)(2,1)}, u32[]{:S(2)}, u32[]{:S(2)}) collective-permute-start(bf16[160,4,1,256]{3,0,2,1:T(8,128)(2,1)} %get-tuple-element.95), channel_id=1, source_target_pairs={{0,12},{1,13},{2,14},{3,15},{4,8},{5,9},{6,10},{7,11},{8,4},{9,5},... | collective-permute-start | bytes 983048 | tf_op jit(solution)/shard_map/ppermute | solution.py:27
  129.4 69.9 %collective-permute-start.17 = (bf16[1024,384]{1,0:T(8,128)(2,1)}, bf16[1024,384]{1,0:T(8,128)(2,1)}, u32[]{:S(2)}, u32[]{:S(2)}) collective-permute-start(bf16[1024,384]{1,0:T(8,128)(2,1)} %get-tuple-element.40), channel_id=1, source_target_pairs={{0,2},{1,3},{2,0},{3,1},{4,6},{5,7},{6,4},{7,5},{8,10},{9,11},{10,... | collective-permute-start | bytes 2359304 | tf_op jit(solution)/shard_map/ppermute | solution.py:27
  151.4 52.1 %collective-permute-start.18 = (bf16[1024,384]{1,0:T(8,128)(2,1)}, bf16[1024,384]{1,0:T(8,128)(2,1)}, u32[]{:S(2)}, u32[]{:S(2)}) collective-permute-start(bf16[1024,384]{1,0:T(8,128)(2,1)} %get-tuple-element.37), channel_id=1, source_target_pairs={{0,3},{1,2},{2,1},{3,0},{4,7},{5,6},{6,5},{7,4},{8,11},{9,10},{10,... | collective-permute-start | bytes 2359304 | tf_op jit(solution)/shard_map/ppermute | solution.py:27
  166.7 61.8 %collective-permute-start.4 = (bf16[2,160,1536]{2,1,0:T(8,128)(2,1)}, bf16[2,160,1536]{2,1,0:T(8,128)(2,1)}, u32[]{:S(2)}, u32[]{:S(2)}) collective-permute-start(bf16[2,160,1536]{2,1,0:T(8,128)(2,1)} %constant_dynamic-update-slice_fusion.78), channel_id=1, source_target_pairs={{0,32},{1,33},{2,34},{3,35},{4,36},{5,37},{6,38},{7,39},{8,40},{9,... | collective-permute-start | bytes 2949128 | tf_op jit(solution)/shard_map/ppermute | solution.py:27
  187.0 29.2 %collective-permute-start.13 = (bf16[160,1024]{1,0:T(8,128)(2,1)S(1)}, bf16[160,1024]{1,0:T(8,128)(2,1)S(1)}, u32[]{:S(2)}, u32[]{:S(2)}) collective-permute-start(bf16[160,1024]{1,0:T(8,128)(2,1)S(1)} %get-tuple-element.93), channel_id=1, source_target_pairs={{0,1},{1,0},{2,3},{3,2},{4,5},{5,4},{6,7},{7,6},{8,9},{9,8},{10,11... | collective-permute-start | bytes 983048 | tf_op jit(solution)/shard_map/ppermute | solution.py:27
  193.1 39.8 %collective-permute-start.5 = (bf16[2,160,1536]{2,1,0:T(8,128)(2,1)}, bf16[2,160,1536]{2,1,0:T(8,128)(2,1)S(1)}, u32[]{:S(2)}, u32[]{:S(2)}) collective-permute-start(bf16[2,160,1536]{2,1,0:T(8,128)(2,1)} %constant_dynamic-update-slice_fusion.78), channel_id=1, source_target_pairs={{0,64},{1,65},{2,66},{3,67},{4,68},{5,69},{6,70},{7,71},{8,72},{9,... | collective-permute-start | bytes 2949128 | tf_op jit(solution)/shard_map/ppermute | solution.py:27
  199.3 22.1 %collective-permute-start.14 = (bf16[160,1024]{1,0:T(8,128)(2,1)S(1)}, bf16[160,1024]{1,0:T(8,128)(2,1)S(1)}, u32[]{:S(2)}, u32[]{:S(2)}) collective-permute-start(bf16[160,1024]{1,0:T(8,128)(2,1)S(1)} %get-tuple-element.92), channel_id=1, source_target_pairs={{0,2},{1,3},{2,0},{3,1},{4,6},{5,7},{6,4},{7,5},{8,10},{9,11},{10,... | collective-permute-start | bytes 983048 | tf_op jit(solution)/shard_map/ppermute | solution.py:27
  203.5 39.1 %collective-permute-start.6 = (bf16[2,160,1536]{2,1,0:T(8,128)(2,1)}, bf16[2,160,1536]{2,1,0:T(8,128)(2,1)S(1)}, u32[]{:S(2)}, u32[]{:S(2)}) collective-permute-start(bf16[2,160,1536]{2,1,0:T(8,128)(2,1)} %constant_dynamic-update-slice_fusion.78), channel_id=1, source_target_pairs={{0,96},{1,97},{2,98},{3,99},{4,100},{5,101},{6,102},{7,103},{8,104... | collective-permute-start | bytes 2949128 | tf_op jit(solution)/shard_map/ppermute | solution.py:27
  221.4 37.2 %collective-permute-start.29 = (bf16[1,2,80,512]{3,2,1,0:T(8,128)(2,1)S(1)}, bf16[1,2,80,512]{3,2,1,0:T(8,128)(2,1)S(1)}, u32[]{:S(2)}, u32[]{:S(2)}) collective-permute-start(bf16[1,2,80,512]{3,2,1,0:T(8,128)(2,1)S(1)} %get-tuple-element.72), channel_id=1, source_target_pairs={{0,32},{1,33},{2,34},{3,35},{4,36},{5,37},{6,38},{7,39},{8,40},{9,... | collective-permute-start | bytes 491528 | tf_op jit(solution)/shard_map/ppermute | solution.py:27
  228.1 30.7 %collective-permute-start.30 = (bf16[1,2,80,512]{3,2,1,0:T(8,128)(2,1)S(1)}, bf16[1,2,80,512]{3,2,1,0:T(8,128)(2,1)S(1)}, u32[]{:S(2)}, u32[]{:S(2)}) collective-permute-start(bf16[1,2,80,512]{3,2,1,0:T(8,128)(2,1)S(1)} %get-tuple-element.71), channel_id=1, source_target_pairs={{0,64},{1,65},{2,66},{3,67},{4,68},{5,69},{6,70},{7,71},{8,72},{9,... | collective-permute-start | bytes 491528 | tf_op jit(solution)/shard_map/ppermute | solution.py:27
  228.5 33.6 %collective-permute-start.31 = (bf16[1,2,80,512]{3,2,1,0:T(8,128)(2,1)S(1)}, bf16[1,2,80,512]{3,2,1,0:T(8,128)(2,1)S(1)}, u32[]{:S(2)}, u32[]{:S(2)}) collective-permute-start(bf16[1,2,80,512]{3,2,1,0:T(8,128)(2,1)S(1)} %get-tuple-element.70), channel_id=1, source_target_pairs={{0,96},{1,97},{2,98},{3,99},{4,100},{5,101},{6,102},{7,103},{8,104... | collective-permute-start | bytes 491528 | tf_op jit(solution)/shard_map/ppermute | solution.py:27
  232.9 33.7 %collective-permute-start.32 = (bf16[1,2,80,512]{3,2,1,0:T(8,128)(2,1)S(1)}, bf16[1,2,80,512]{3,2,1,0:T(8,128)(2,1)S(1)}, u32[]{:S(2)}, u32[]{:S(2)}) collective-permute-start(bf16[1,2,80,512]{3,2,1,0:T(8,128)(2,1)S(1)} %get-tuple-element.69), channel_id=1, source_target_pairs={{0,128},{1,129},{2,130},{3,131},{4,132},{5,133},{6,134},{7,135},{8... | collective-permute-start | bytes 491528 | tf_op jit(solution)/shard_map/ppermute | solution.py:27
  242.6 30.0 %collective-permute-start.33 = (bf16[1,2,80,512]{3,2,1,0:T(8,128)(2,1)S(1)}, bf16[1,2,80,512]{3,2,1,0:T(8,128)(2,1)S(1)}, u32[]{:S(2)}, u32[]{:S(2)}) collective-permute-start(bf16[1,2,80,512]{3,2,1,0:T(8,128)(2,1)S(1)} %get-tuple-element.68), channel_id=1, source_target_pairs={{0,160},{1,161},{2,162},{3,163},{4,164},{5,165},{6,166},{7,167},{8... | collective-permute-start | bytes 491528 | tf_op jit(solution)/shard_map/ppermute | solution.py:27
  258.7 20.5 %collective-permute-start.19 = (bf16[1,256,1536]{2,1,0:T(8,128)(2,1)S(1)}, bf16[1,256,1536]{2,1,0:T(8,128)(2,1)S(1)}, u32[]{:S(2)}, u32[]{:S(2)}) collective-permute-start(bf16[1,256,1536]{2,1,0:T(8,128)(2,1)S(1)} %get-tuple-element.36), channel_id=1, source_target_pairs={{0,4},{1,5},{2,6},{3,7},{4,0},{5,1},{6,2},{7,3},{8,12},{9,13},{10,... | collective-permute-start | bytes 2359304 | tf_op jit(solution)/shard_map/ppermute | solution.py:27
  258.8 53.3 %collective-permute-start.34 = (bf16[1,2,80,512]{3,2,1,0:T(8,128)(2,1)S(1)}, bf16[1,2,80,512]{3,2,1,0:T(8,128)(2,1)S(1)}, u32[]{:S(2)}, u32[]{:S(2)}) collective-permute-start(bf16[1,2,80,512]{3,2,1,0:T(8,128)(2,1)S(1)} %get-tuple-element.67), channel_id=1, source_target_pairs={{0,192},{1,193},{2,194},{3,195},{4,196},{5,197},{6,198},{7,199},{8... | collective-permute-start | bytes 491528 | tf_op jit(solution)/shard_map/ppermute | solution.py:27
  262.1 35.1 %collective-permute-start.20 = (bf16[1,256,1536]{2,1,0:T(8,128)(2,1)S(1)}, bf16[1,256,1536]{2,1,0:T(8,128)(2,1)S(1)}, u32[]{:S(2)}, u32[]{:S(2)}) collective-permute-start(bf16[1,256,1536]{2,1,0:T(8,128)(2,1)S(1)} %get-tuple-element.35), channel_id=1, source_target_pairs={{0,8},{1,9},{2,10},{3,11},{4,12},{5,13},{6,14},{7,15},{8,0},{9,1},... | collective-permute-start | bytes 2359304 | tf_op jit(solution)/shard_map/ppermute | solution.py:27
  266.6 45.6 %collective-permute-start.35 = (bf16[1,2,80,512]{3,2,1,0:T(8,128)(2,1)S(1)}, bf16[1,2,80,512]{3,2,1,0:T(8,128)(2,1)S(1)}, u32[]{:S(2)}, u32[]{:S(2)}) collective-permute-start(bf16[1,2,80,512]{3,2,1,0:T(8,128)(2,1)S(1)} %get-tuple-element.66), channel_id=1, source_target_pairs={{0,224},{1,225},{2,226},{3,227},{4,228},{5,229},{6,230},{7,231},{8... | collective-permute-start | bytes 491528 | tf_op jit(solution)/shard_map/ppermute | solution.py:27
  272.6 35.9 %collective-permute-start.21 = (bf16[1,256,1536]{2,1,0:T(8,128)(2,1)S(1)}, bf16[1,256,1536]{2,1,0:T(8,128)(2,1)S(1)}, u32[]{:S(2)}, u32[]{:S(2)}) collective-permute-start(bf16[1,256,1536]{2,1,0:T(8,128)(2,1)S(1)} %get-tuple-element.34), channel_id=1, source_target_pairs={{0,12},{1,13},{2,14},{3,15},{4,8},{5,9},{6,10},{7,11},{8,4},{9,5},... | collective-permute-start | bytes 2359304 | tf_op jit(solution)/shard_map/ppermute | solution.py:27
  312.0 20.6 %collective-permute-start.22 = (bf16[256,1536]{1,0:T(8,128)(2,1)S(1)}, bf16[256,1536]{1,0:T(8,128)(2,1)S(1)}, u32[]{:S(2)}, u32[]{:S(2)}) collective-permute-start(bf16[256,1536]{1,0:T(8,128)(2,1)S(1)} %get-tuple-element.33), channel_id=1, source_target_pairs={{0,4},{1,5},{2,6},{3,7},{4,0},{5,1},{6,2},{7,3},{8,12},{9,13},{10,... | collective-permute-start | bytes 2359304 | tf_op jit(solution)/shard_map/ppermute | solution.py:27
  312.2 33.4 %collective-permute-start.23 = (bf16[256,1536]{1,0:T(8,128)(2,1)S(1)}, bf16[256,1536]{1,0:T(8,128)(2,1)S(1)}, u32[]{:S(2)}, u32[]{:S(2)}) collective-permute-start(bf16[256,1536]{1,0:T(8,128)(2,1)S(1)} %get-tuple-element.32), channel_id=1, source_target_pairs={{0,8},{1,9},{2,10},{3,11},{4,12},{5,13},{6,14},{7,15},{8,0},{9,1},... | collective-permute-start | bytes 2359304 | tf_op jit(solution)/shard_map/ppermute | solution.py:27
  314.0 34.3 %collective-permute-start.24 = (bf16[256,1536]{1,0:T(8,128)(2,1)S(1)}, bf16[256,1536]{1,0:T(8,128)(2,1)S(1)}, u32[]{:S(2)}, u32[]{:S(2)}) collective-permute-start(bf16[256,1536]{1,0:T(8,128)(2,1)S(1)} %get-tuple-element.31), channel_id=1, source_target_pairs={{0,12},{1,13},{2,14},{3,15},{4,8},{5,9},{6,10},{7,11},{8,4},{9,5},... | collective-permute-start | bytes 2359304 | tf_op jit(solution)/shard_map/ppermute | solution.py:27
  359.2 19.2 %collective-permute-start.26 = (bf16[160,1024]{1,0:T(8,128)(2,1)S(1)}, bf16[160,1024]{1,0:T(8,128)(2,1)S(1)}, u32[]{:S(2)}, u32[]{:S(2)}) collective-permute-start(bf16[160,1024]{1,0:T(8,128)(2,1)S(1)} %get-tuple-element.88), channel_id=1, source_target_pairs={{0,2},{1,3},{2,0},{3,1},{4,6},{5,7},{6,4},{7,5},{8,10},{9,11},{10,... | collective-permute-start | bytes 983048 | tf_op jit(solution)/shard_map/ppermute | solution.py:27
  360.3 23.8 %collective-permute-start.27 = (bf16[160,1024]{1,0:T(8,128)(2,1)S(1)}, bf16[160,1024]{1,0:T(8,128)(2,1)S(1)}, u32[]{:S(2)}, u32[]{:S(2)}) collective-permute-start(bf16[160,1024]{1,0:T(8,128)(2,1)S(1)} %get-tuple-element.87), channel_id=1, source_target_pairs={{0,3},{1,2},{2,1},{3,0},{4,7},{5,6},{6,5},{7,4},{8,11},{9,10},{10,... | collective-permute-start | bytes 983048 | tf_op jit(solution)/shard_map/ppermute | solution.py:27
  363.1 28.5 %collective-permute-start.82 = (bf16[8,40,1536]{2,1,0:T(8,128)(2,1)}, bf16[8,40,1536]{2,1,0:T(8,128)(2,1)}, u32[]{:S(2)}, u32[]{:S(2)}) collective-permute-start(bf16[8,40,1536]{2,1,0:T(8,128)(2,1)} %fusion.41), channel_id=1, source_target_pairs={{0,16},{1,17},{2,18},{3,19},{4,20},{5,21},{6,22},{7,23},{8,24},{9,... | collective-permute-start | bytes 2949128 | tf_op jit(solution)/shard_map/ppermute | solution.py:27
  393.9 16.3 %collective-permute-start.84 = (bf16[2,40,1536]{2,1,0:T(8,128)(2,1)S(1)}, bf16[2,40,1536]{2,1,0:T(8,128)(2,1)S(1)}, u32[]{:S(2)}, u32[]{:S(2)}) collective-permute-start(bf16[2,40,1536]{2,1,0:T(8,128)(2,1)S(1)} %get-tuple-element.50), channel_id=1, source_target_pairs={{0,64},{1,65},{2,66},{3,67},{4,68},{5,69},{6,70},{7,71},{8,72},{9,... | collective-permute-start | bytes 737288 | tf_op jit(solution)/shard_map/ppermute | solution.py:27
  398.2 14.5 %collective-permute-start.85 = (bf16[2,40,1536]{2,1,0:T(8,128)(2,1)S(1)}, bf16[2,40,1536]{2,1,0:T(8,128)(2,1)S(1)}, u32[]{:S(2)}, u32[]{:S(2)}) collective-permute-start(bf16[2,40,1536]{2,1,0:T(8,128)(2,1)S(1)} %get-tuple-element.51), channel_id=1, source_target_pairs={{0,96},{1,97},{2,98},{3,99},{4,100},{5,101},{6,102},{7,103},{8,104... | collective-permute-start | bytes 737288 | tf_op jit(solution)/shard_map/ppermute | solution.py:27
  399.0 23.0 %collective-permute-start.53 = (bf16[1,2,80,512]{3,2,1,0:T(8,128)(2,1)S(1)}, bf16[1,2,80,512]{3,2,1,0:T(8,128)(2,1)S(1)}, u32[]{:S(2)}, u32[]{:S(2)}) collective-permute-start(bf16[1,2,80,512]{3,2,1,0:T(8,128)(2,1)S(1)} %get-tuple-element.86), channel_id=1, source_target_pairs={{0,32},{1,33},{2,34},{3,35},{4,36},{5,37},{6,38},{7,39},{8,40},{9,... | collective-permute-start | bytes 491528 | tf_op jit(solution)/shard_map/ppermute | solution.py:27
  413.3 17.6 %collective-permute-start.55 = (bf16[1,2,80,512]{3,2,1,0:T(8,128)(2,1)S(1)}, bf16[1,2,80,512]{3,2,1,0:T(8,128)(2,1)S(1)}, u32[]{:S(2)}, u32[]{:S(2)}) collective-permute-start(bf16[1,2,80,512]{3,2,1,0:T(8,128)(2,1)S(1)} %get-tuple-element.84), channel_id=1, source_target_pairs={{0,96},{1,97},{2,98},{3,99},{4,100},{5,101},{6,102},{7,103},{8,104... | collective-permute-start | bytes 491528 | tf_op jit(solution)/shard_map/ppermute | solution.py:27
  415.7 15.2 %collective-permute-start.56 = (bf16[1,2,80,512]{3,2,1,0:T(8,128)(2,1)S(1)}, bf16[1,2,80,512]{3,2,1,0:T(8,128)(2,1)S(1)}, u32[]{:S(2)}, u32[]{:S(2)}) collective-permute-start(bf16[1,2,80,512]{3,2,1,0:T(8,128)(2,1)S(1)} %get-tuple-element.83), channel_id=1, source_target_pairs={{0,128},{1,129},{2,130},{3,131},{4,132},{5,133},{6,134},{7,135},{8... | collective-permute-start | bytes 491528 | tf_op jit(solution)/shard_map/ppermute | solution.py:27
  415.7 24.2 %collective-permute-start.57 = (bf16[1,2,80,512]{3,2,1,0:T(8,128)(2,1)S(1)}, bf16[1,2,80,512]{3,2,1,0:T(8,128)(2,1)S(1)}, u32[]{:S(2)}, u32[]{:S(2)}) collective-permute-start(bf16[1,2,80,512]{3,2,1,0:T(8,128)(2,1)S(1)} %get-tuple-element.82), channel_id=1, source_target_pairs={{0,160},{1,161},{2,162},{3,163},{4,164},{5,165},{6,166},{7,167},{8... | collective-permute-start | bytes 491528 | tf_op jit(solution)/shard_map/ppermute | solution.py:27
  422.1 23.0 %collective-permute-start.58 = (bf16[1,2,80,512]{3,2,1,0:T(8,128)(2,1)S(1)}, bf16[1,2,80,512]{3,2,1,0:T(8,128)(2,1)S(1)}, u32[]{:S(2)}, u32[]{:S(2)}) collective-permute-start(bf16[1,2,80,512]{3,2,1,0:T(8,128)(2,1)S(1)} %get-tuple-element.81), channel_id=1, source_target_pairs={{0,192},{1,193},{2,194},{3,195},{4,196},{5,197},{6,198},{7,199},{8... | collective-permute-start | bytes 491528 | tf_op jit(solution)/shard_map/ppermute | solution.py:27
  422.9 24.6 %collective-permute-start.59 = (bf16[1,2,80,512]{3,2,1,0:T(8,128)(2,1)S(1)}, bf16[1,2,80,512]{3,2,1,0:T(8,128)(2,1)S(1)}, u32[]{:S(2)}, u32[]{:S(2)}) collective-permute-start(bf16[1,2,80,512]{3,2,1,0:T(8,128)(2,1)S(1)} %get-tuple-element.80), channel_id=1, source_target_pairs={{0,224},{1,225},{2,226},{3,227},{4,228},{5,229},{6,230},{7,231},{8... | collective-permute-start | bytes 491528 | tf_op jit(solution)/shard_map/ppermute | solution.py:27
  465.5 12.5 %collective-permute-start.94 = (f32[384,128]{1,0:T(8,128)S(1)}, f32[384,128]{1,0:T(8,128)S(1)}, u32[]{:S(2)}, u32[]{:S(2)}) collective-permute-start(f32[384,128]{1,0:T(8,128)S(1)} %get-tuple-element.115), channel_id=1, source_target_pairs={{0,8},{1,9},{2,10},{3,11},{4,12},{5,13},{6,14},{7,15},{8,0},{9,1},... | collective-permute-start | bytes 589832 | tf_op jit(solution)/shard_map/ppermute | solution.py:27
  471.2 34.0 %collective-permute-start.60 = (bf16[1,8,80,512]{3,2,0,1:T(8,128)(2,1)S(1)}, bf16[1,8,80,512]{3,2,0,1:T(8,128)(2,1)S(1)}, u32[]{:S(2)}, u32[]{:S(2)}) collective-permute-start(bf16[1,8,80,512]{3,2,0,1:T(8,128)(2,1)S(1)} %dynamic-slice_bitcast_fusion.6), channel_id=1, source_target_pairs={{0,16},{1,17},{2,18},{3,19},{4,20},{5,21},{6,22},{7,23},{8,24},{9,... | collective-permute-start | bytes 1966088 | tf_op jit(solution)/shard_map/ppermute | solution.py:27
  491.0 16.4 %collective-permute-start.44 = (bf16[1,8,80,512]{3,2,0,1:T(8,128)(2,1)S(1)}, bf16[1,8,80,512]{3,2,0,1:T(8,128)(2,1)S(1)}, u32[]{:S(2)}, u32[]{:S(2)}) collective-permute-start(bf16[1,8,80,512]{3,2,0,1:T(8,128)(2,1)S(1)} %dynamic-slice_bitcast_fusion.8), channel_id=1, source_target_pairs={{0,16},{1,17},{2,18},{3,19},{4,20},{5,21},{6,22},{7,23},{8,24},{9,... | collective-permute-start | bytes 1966088 | tf_op jit(solution)/shard_map/ppermute | solution.py:27
  500.6 145.9 %collective-permute-start.86 = (bf16[40,384]{1,0:T(8,128)(2,1)}, bf16[40,384]{1,0:T(8,128)(2,1)}, u32[]{:S(2)}, u32[]{:S(2)}) collective-permute-start(bf16[40,384]{1,0:T(8,128)(2,1)} %get-tuple-element.117), channel_id=1, source_target_pairs={{0,1},{1,0},{2,3},{3,2},{4,5},{5,4},{6,7},{7,6},{8,9},{9,8},{10,11... | collective-permute-start | bytes 92168 | tf_op jit(solution)/shard_map/ppermute | solution.py:27
  502.1 149.6 %collective-permute-start.87 = (bf16[40,384]{1,0:T(8,128)(2,1)}, bf16[40,384]{1,0:T(8,128)(2,1)}, u32[]{:S(2)}, u32[]{:S(2)}) collective-permute-start(bf16[40,384]{1,0:T(8,128)(2,1)} %get-tuple-element.123), channel_id=1, source_target_pairs={{0,2},{1,3},{2,0},{3,1},{4,6},{5,7},{6,4},{7,5},{8,10},{9,11},{10,... | collective-permute-start | bytes 92168 | tf_op jit(solution)/shard_map/ppermute | solution.py:27
  505.0 100.0 %collective-permute-start.105 = (f32[24,128]{1,0:T(8,128)}, f32[24,128]{1,0:T(8,128)}, u32[]{:S(2)}, u32[]{:S(2)}) collective-permute-start(f32[24,128]{1,0:T(8,128)} %get-tuple-element.24), channel_id=1, source_target_pairs={{0,32},{1,33},{2,34},{3,35},{4,36},{5,37},{6,38},{7,39},{8,40},{9,... | collective-permute-start | bytes 36872 | tf_op jit(solution)/shard_map/ppermute | solution.py:27
  521.3 15.7 %collective-permute-start.65 = (bf16[1,2,80,512]{3,2,1,0:T(8,128)(2,1)S(1)}, bf16[1,2,80,512]{3,2,1,0:T(8,128)(2,1)S(1)}, u32[]{:S(2)}, u32[]{:S(2)}) collective-permute-start(bf16[1,2,80,512]{3,2,1,0:T(8,128)(2,1)S(1)} %get-tuple-element.75), channel_id=1, source_target_pairs={{0,160},{1,161},{2,162},{3,163},{4,164},{5,165},{6,166},{7,167},{8... | collective-permute-start | bytes 491528 | tf_op jit(solution)/shard_map/ppermute | solution.py:27
  528.9 16.4 %collective-permute-start.66 = (bf16[1,2,80,512]{3,2,1,0:T(8,128)(2,1)S(1)}, bf16[1,2,80,512]{3,2,1,0:T(8,128)(2,1)S(1)}, u32[]{:S(2)}, u32[]{:S(2)}) collective-permute-start(bf16[1,2,80,512]{3,2,1,0:T(8,128)(2,1)S(1)} %get-tuple-element.74), channel_id=1, source_target_pairs={{0,192},{1,193},{2,194},{3,195},{4,196},{5,197},{6,198},{7,199},{8... | collective-permute-start | bytes 491528 | tf_op jit(solution)/shard_map/ppermute | solution.py:27
  536.9 14.2 %collective-permute-start.67 = (bf16[1,2,80,512]{3,2,1,0:T(8,128)(2,1)S(1)}, bf16[1,2,80,512]{3,2,1,0:T(8,128)(2,1)S(1)}, u32[]{:S(2)}, u32[]{:S(2)}) collective-permute-start(bf16[1,2,80,512]{3,2,1,0:T(8,128)(2,1)S(1)} %get-tuple-element.73), channel_id=1, source_target_pairs={{0,224},{1,225},{2,226},{3,227},{4,228},{5,229},{6,230},{7,231},{8... | collective-permute-start | bytes 491528 | tf_op jit(solution)/shard_map/ppermute | solution.py:27
  552.0 13.2 %collective-permute-start.47 = (bf16[1,2,80,512]{3,2,1,0:T(8,128)(2,1)S(1)}, bf16[1,2,80,512]{3,2,1,0:T(8,128)(2,1)S(1)}, u32[]{:S(2)}, u32[]{:S(2)}) collective-permute-start(bf16[1,2,80,512]{3,2,1,0:T(8,128)(2,1)S(1)} %get-tuple-element.63), channel_id=1, source_target_pairs={{0,96},{1,97},{2,98},{3,99},{4,100},{5,101},{6,102},{7,103},{8,104... | collective-permute-start | bytes 491528 | tf_op jit(solution)/shard_map/ppermute | solution.py:27
  558.0 15.7 %collective-permute-start.48 = (bf16[1,2,80,512]{3,2,1,0:T(8,128)(2,1)S(1)}, bf16[1,2,80,512]{3,2,1,0:T(8,128)(2,1)S(1)}, u32[]{:S(2)}, u32[]{:S(2)}) collective-permute-start(bf16[1,2,80,512]{3,2,1,0:T(8,128)(2,1)S(1)} %get-tuple-element.62), channel_id=1, source_target_pairs={{0,128},{1,129},{2,130},{3,131},{4,132},{5,133},{6,134},{7,135},{8... | collective-permute-start | bytes 491528 | tf_op jit(solution)/shard_map/ppermute | solution.py:27
  565.2 12.8 %collective-permute-start.49 = (bf16[1,2,80,512]{3,2,1,0:T(8,128)(2,1)S(1)}, bf16[1,2,80,512]{3,2,1,0:T(8,128)(2,1)S(1)}, u32[]{:S(2)}, u32[]{:S(2)}) collective-permute-start(bf16[1,2,80,512]{3,2,1,0:T(8,128)(2,1)S(1)} %get-tuple-element.61), channel_id=1, source_target_pairs={{0,160},{1,161},{2,162},{3,163},{4,164},{5,165},{6,166},{7,167},{8... | collective-permute-start | bytes 491528 | tf_op jit(solution)/shard_map/ppermute | solution.py:27
  573.8 15.4 %collective-permute-start.50 = (bf16[1,2,80,512]{3,2,1,0:T(8,128)(2,1)}, bf16[1,2,80,512]{3,2,1,0:T(8,128)(2,1)S(1)}, u32[]{:S(2)}, u32[]{:S(2)}) collective-permute-start(bf16[1,2,80,512]{3,2,1,0:T(8,128)(2,1)} %get-tuple-element.60), channel_id=1, source_target_pairs={{0,192},{1,193},{2,194},{3,195},{4,196},{5,197},{6,198},{7,199},{8... | collective-permute-start | bytes 491528 | tf_op jit(solution)/shard_map/ppermute | solution.py:27
  578.1 14.1 %collective-permute-start.51 = (bf16[1,2,80,512]{3,2,1,0:T(8,128)(2,1)}, bf16[1,2,80,512]{3,2,1,0:T(8,128)(2,1)S(1)}, u32[]{:S(2)}, u32[]{:S(2)}) collective-permute-start(bf16[1,2,80,512]{3,2,1,0:T(8,128)(2,1)} %get-tuple-element.59), channel_id=1, source_target_pairs={{0,224},{1,225},{2,226},{3,227},{4,228},{5,229},{6,230},{7,231},{8... | collective-permute-start | bytes 491528 | tf_op jit(solution)/shard_map/ppermute | solution.py:27
  589.1 18.0 %collective-permute-start.106 = (f32[24,128]{1,0:T(8,128)}, f32[24,128]{1,0:T(8,128)}, u32[]{:S(2)}, u32[]{:S(2)}) collective-permute-start(f32[24,128]{1,0:T(8,128)} %get-tuple-element.24), channel_id=1, source_target_pairs={{0,64},{1,65},{2,66},{3,67},{4,68},{5,69},{6,70},{7,71},{8,72},{9,... | collective-permute-start | bytes 36872 | tf_op jit(solution)/shard_map/ppermute | solution.py:27
  592.2 17.3 %collective-permute-start.107 = (f32[24,128]{1,0:T(8,128)}, f32[24,128]{1,0:T(8,128)S(1)}, u32[]{:S(2)}, u32[]{:S(2)}) collective-permute-start(f32[24,128]{1,0:T(8,128)} %get-tuple-element.24), channel_id=1, source_target_pairs={{0,96},{1,97},{2,98},{3,99},{4,100},{5,101},{6,102},{7,103},{8,104... | collective-permute-start | bytes 36872 | tf_op jit(solution)/shard_map/ppermute | solution.py:27
  607.1 23.1 %collective-permute-start.69 = (bf16[160,1024]{1,0:T(8,128)(2,1)S(1)}, bf16[160,1024]{1,0:T(8,128)(2,1)S(1)}, u32[]{:S(2)}, u32[]{:S(2)}) collective-permute-start(bf16[160,1024]{1,0:T(8,128)(2,1)S(1)} %get-tuple-element.56), channel_id=1, source_target_pairs={{0,2},{1,3},{2,0},{3,1},{4,6},{5,7},{6,4},{7,5},{8,10},{9,11},{10,... | collective-permute-start | bytes 983048 | tf_op jit(solution)/shard_map/ppermute | solution.py:27
  609.5 26.8 %collective-permute-start.70 = (bf16[160,1024]{1,0:T(8,128)(2,1)S(1)}, bf16[160,1024]{1,0:T(8,128)(2,1)S(1)}, u32[]{:S(2)}, u32[]{:S(2)}) collective-permute-start(bf16[160,1024]{1,0:T(8,128)(2,1)S(1)} %get-tuple-element.55), channel_id=1, source_target_pairs={{0,3},{1,2},{2,1},{3,0},{4,7},{5,6},{6,5},{7,4},{8,11},{9,10},{10,... | collective-permute-start | bytes 983048 | tf_op jit(solution)/shard_map/ppermute | solution.py:27
  615.7 36.0 %collective-permute-start.88 = (bf16[40,384]{1,0:T(8,128)(2,1)S(1)}, bf16[40,384]{1,0:T(8,128)(2,1)S(1)}, u32[]{:S(2)}, u32[]{:S(2)}) collective-permute-start(bf16[40,384]{1,0:T(8,128)(2,1)S(1)} %copy-done.38), channel_id=1, source_target_pairs={{0,3},{1,2},{2,1},{3,0},{4,7},{5,6},{6,5},{7,4},{8,11},{9,10},{10,... | collective-permute-start | bytes 92168 | tf_op jit(solution)/shard_map/ppermute | solution.py:27
  638.7 32.2 %collective-permute-start.71 = (bf16[8,40,1536]{2,1,0:T(8,128)(2,1)S(1)}, bf16[8,40,1536]{2,1,0:T(8,128)(2,1)S(1)}, u32[]{:S(2)}, u32[]{:S(2)}) collective-permute-start(bf16[8,40,1536]{2,1,0:T(8,128)(2,1)S(1)} %fusion.40), channel_id=1, source_target_pairs={{0,16},{1,17},{2,18},{3,19},{4,20},{5,21},{6,22},{7,23},{8,24},{9,... | collective-permute-start | bytes 2949128 | tf_op jit(solution)/shard_map/ppermute | solution.py:27
  663.7 12.4 %collective-permute-start.113 = (f32[384,128]{1,0:T(8,128)S(1)}, f32[384,128]{1,0:T(8,128)S(1)}, u32[]{:S(2)}, u32[]{:S(2)}) collective-permute-start(f32[384,128]{1,0:T(8,128)S(1)} %constant_dynamic-update-slice_fusion.57), channel_id=1, source_target_pairs={{0,12},{1,13},{2,14},{3,15},{4,8},{5,9},{6,10},{7,11},{8,4},{9,5},... | collective-permute-start | bytes 589832 | tf_op jit(solution)/shard_map/ppermute | solution.py:27
  (112 other events, 675.4 us)

commit v2 on v1

v2 whole, which is shorter than its diff:
```python
import jax
import jax.numpy as jnp
from jax import lax
from jax.sharding import PartitionSpec as P

BF = jnp.bfloat16
F32 = jnp.float32
BLOCKS = 4
GROUP = 4
SEQ = 16
CHAN = 16
Z_LO = [0, 1, 2, 3]
Y = [0, 4, 8, 12]
CORE = [0, 16]
X = [0, 32, 64, 96]
Z_HI = [0, 128]


def join(high, low):
    return [h ^ l for h in high for l in low]


def swap(value, mask):
    if mask == 0:
        return value
    route = [(i, i ^ mask) for i in range(SEQ * CHAN)]
    return lax.ppermute(value, ("seq", "chan"), route)


def pieces_for(take, me, masks, behind=()):
    pieces = [take(jnp.bitwise_xor(me, step)) for step in range(len(masks))]
    return list(lax.optimization_barrier((*pieces, *behind))[: len(masks)])


def deliver(name, pieces, me, masks, axis, seen=None):
    size = pieces[0].shape[axis]
    shape = list(pieces[0].shape)
    shape[axis] = size * len(masks)
    out = jnp.zeros(shape, pieces[0].dtype)
    for step, mask in enumerate(masks):
        with jax.named_scope(name):
            arrived = swap(pieces[step], mask)
        if seen is not None:
            seen.append(arrived)
        out = lax.dynamic_update_slice_in_dim(out, arrived, jnp.bitwise_xor(me, step) * size, axis)
    return out


def after(value, *others):
    return lax.optimization_barrier((value, *others))[0]


def part_of(value, index, count, axis):
    size = value.shape[axis] // count
    return lax.dynamic_slice_in_dim(value, index * size, size, axis)


def sum_spread(name, take, me, masks):
    total = None
    for step, mask in enumerate(masks):
        piece = take(jnp.bitwise_xor(me, step))
        with jax.named_scope(name):
            arrived = swap(piece.astype(BF), mask).astype(F32) if mask else piece.astype(F32)
        total = arrived if total is None else total + arrived
    return total


def sum_spread_f32(name, take, me, masks):
    total = None
    for step, mask in enumerate(masks):
        with jax.named_scope(name):
            arrived = swap(take(jnp.bitwise_xor(me, step)), mask)
        total = arrived if total is None else total + arrived
    return total


def gather(name, value, me, masks, axis):
    return deliver(name, [value] * len(masks), me, masks, axis)


def seq_exchange(name, value):
    with jax.named_scope(name):
        return lax.all_to_all(value, "seq", split_axis=0, concat_axis=0, tiled=True)


def plane_exchange(name, value):
    groups = [list(range(8)), list(range(8, SEQ))]
    with jax.named_scope(name):
        return lax.all_to_all(
            value, "seq", split_axis=0, concat_axis=0, axis_index_groups=groups, tiled=True
        )


def group_exchange(name, value):
    groups = [list(range(first, first + GROUP)) for first in range(0, CHAN, GROUP)]
    with jax.named_scope(name):
        return lax.all_to_all(
            value, "chan", split_axis=0, concat_axis=0, axis_index_groups=groups, tiled=True
        )


def line_exchange(name, value):
    groups = [
        [(z_hi * 8 + plane) * CHAN + block * GROUP + z_lo for z_hi in range(2) for z_lo in range(GROUP)]
        for plane in range(8)
        for block in range(BLOCKS)
    ]
    with jax.named_scope(name):
        return lax.all_to_all(
            value, ("seq", "chan"), split_axis=0, concat_axis=0, axis_index_groups=groups, tiled=True
        )


def lower_mask(size):
    return jnp.arange(size)[:, None] >= jnp.arange(size)[None, :]


def weight_core(terms, core):
    count, rows, width = terms.shape
    split = terms.reshape(count, 8, 2, rows // 16, width)
    pair = sum_spread(
        "weight_core", lambda other: lax.dynamic_index_in_dim(split, other, 2, keepdims=False), core, CORE
    )
    return pair.reshape(count, 2, 4, rows // 16, width)


def weight_line(pair, x):
    return sum_spread(
        "weight_x", lambda other: lax.dynamic_index_in_dim(pair, other, 2, keepdims=False), x, X
    )


def weight_z(line, z_lo):
    return sum_spread("weight_z", lambda other: part_of(line, other, 4, 3), z_lo, Z_LO)


def weight_z_hi(line, z_hi):
    return sum_spread(
        "weight_z_hi", lambda other: lax.dynamic_index_in_dim(line, other, 1, keepdims=False), z_hi, Z_HI
    )


def body(
    layer_input,
    query_scale,
    key_scale,
    twiddle,
    seq_inner,
    seq_outer,
    grad_output,
    hidden_pre,
    up_right,
    up_left,
    down_right,
    down_left,
):
    outer_here, inner_len = twiddle.shape
    tokens, width = layer_input.shape
    outer_len = seq_outer.shape[0]
    hidden = hidden_pre.shape[1]
    quarter = tokens // GROUP
    seq = lax.axis_index("seq")
    chan = lax.axis_index("chan")
    z_lo, y = chan % 4, chan // 4
    core, x, z_hi = seq % 2, (seq // 2) % 4, seq // 8
    mine = width // SEQ
    inner_mask = lower_mask(inner_len)
    outer_mask = lower_mask(outer_len)
    inner_tri = jnp.where(inner_mask, seq_inner, jnp.zeros_like(seq_inner))
    outer_tri = jnp.where(outer_mask, seq_outer, jnp.zeros_like(seq_outer))
    layer_t = layer_input.T
    grad_t = grad_output.T
    piece = quarter // BLOCKS

    right = jnp.stack([down_right[0], up_right[0].T])
    right = part_of(right, core * 4 + x, 8, 1)

    grad_pieces = pieces_for(lambda other: part_of(grad_t, other, 4, 1), z_lo, Z_LO, (right,))
    layer_rows = layer_t.reshape(SEQ, mine * outer_here, inner_len)
    twiddle_high = twiddle.astype(BF)
    twiddle_low = (twiddle - twiddle_high.astype(F32)).astype(BF)
    twiddle_parts = jnp.concatenate([twiddle_high, twiddle_low], axis=0)
    twiddle_parts = jnp.broadcast_to(twiddle_parts, (SEQ,) + twiddle_parts.shape)
    right = gather("right_z", right, z_lo, Z_LO, 2)
    grad_rows = deliver("grad_z", grad_pieces, z_lo, Z_LO, 0)
    pre_send = after(hidden_pre.reshape(GROUP, quarter, hidden), grad_rows)
    pre_values = group_exchange("hidden_pre_z", pre_send)
    pre_values = pre_values.transpose(1, 0, 2).reshape(quarter, 4 * hidden)
    pre_values = lax.optimization_barrier(pre_values)
    right = gather("right_x", right, x, X, 1)

    grad_pieces = pieces_for(lambda other: part_of(grad_rows, other, 4, 1), y, Y)
    grad_blocks = deliver("grad_y", [p[None] for p in grad_pieces], y, Y, 0).astype(F32)
    left_down = down_left.astype(F32)
    down_mix = jnp.stack(
        [
            sum(left_down[j, k][:, None] * grad_blocks[j] for j in range(BLOCKS)).astype(BF)
            for k in range(BLOCKS)
        ]
    )
    down_pieces = pieces_for(
        lambda other: lax.dynamic_index_in_dim(down_mix, other, 0, keepdims=False), y, Y, (right,)
    )
    right = gather("right_core", right, core, CORE, 1)
    down_grad = deliver("down_y", down_pieces, y, Y, 1)

    layer_send = after(jnp.concatenate([layer_rows, twiddle_parts], axis=1), pre_values)
    layer_cols = seq_exchange("layer_seq", layer_send)

    def to_cols(value):
        return (
            value.reshape(SEQ, mine, outer_here, inner_len)
            .transpose(1, 0, 2, 3)
            .reshape(mine, outer_len, inner_len)
        )

    def to_rows(value):
        return (
            value.reshape(mine, SEQ, outer_here, inner_len)
            .transpose(1, 0, 2, 3)
            .reshape(SEQ, mine * outer_here, inner_len)
        )

    def blocks_to_cols(value, line):
        by_line = value.reshape(GROUP, 2, width // 2, quarter).transpose(1, 0, 2, 3)
        by_line = line_exchange("cols_z", by_line.reshape(8, width // 2, quarter))
        by_line, line = lax.optimization_barrier((by_line, line))
        by_line = by_line.reshape(2, GROUP, 8, mine, outer_here // GROUP, inner_len)
        by_line = by_line.transpose(2, 3, 0, 1, 4, 5).reshape(8, mine * 2 * outer_here, inner_len)
        by_plane = plane_exchange("cols_plane", by_line)
        by_plane = by_plane.reshape(8, mine, 2, outer_here, inner_len).transpose(1, 2, 0, 3, 4)
        return by_plane.reshape(mine, outer_len, inner_len), line

    def mixed_send(value):
        by_plane = value.reshape(mine, 2, 8, outer_here, inner_len).transpose(2, 0, 1, 3, 4)
        by_plane = plane_exchange("blocks_plane", by_plane.reshape(8, mine * 2 * outer_here, inner_len))
        return by_plane

    def mixed_arrive(by_plane):
        by_line = by_plane.reshape(width // 2, 2, outer_here, inner_len).transpose(1, 0, 2, 3)
        by_line = by_line.reshape(2, width // 2, GROUP, quarter).transpose(0, 2, 1, 3)
        by_line = by_line.reshape(8, width // 2, quarter)
        arrived = line_exchange("blocks_z", by_line)
        return arrived.reshape(2, GROUP, width // 2, quarter).transpose(1, 0, 2, 3).reshape(4 * width, quarter)

    layer_cols, twiddle_high, twiddle_low = jnp.split(
        layer_cols, [mine * outer_here, mine * outer_here + outer_here], axis=1
    )
    twiddle_all = (twiddle_high.astype(F32) + twiddle_low.astype(F32)).reshape(outer_len, inner_len)
    layer_cols = to_cols(layer_cols).astype(F32)
    key_mine = part_of(key_scale, seq, SEQ, 0)[:, None, None]
    query_mine = part_of(query_scale, seq, SEQ, 0)[:, None, None]
    key_input = (layer_cols * key_mine).astype(BF)
    first_pass = (
        jnp.einsum("bk,cak->cab", inner_tri, key_input, preferred_element_type=F32) * twiddle_all
    ).astype(BF)
    convolved = jnp.einsum("ij,cjb->cib", outer_tri, first_pass, preferred_element_type=F32).astype(BF)
    mixed = (layer_cols + layer_cols * query_mine * convolved.astype(F32)).astype(BF)
    mixed_plane = mixed_send(mixed)

    hidden_grad = jnp.einsum("pt,pq->tq", down_grad, right[0], preferred_element_type=F32)
    pre_f = pre_values.astype(F32)
    activated = jax.nn.gelu(pre_f).astype(BF)
    pre_grad = jax.vjp(jax.nn.gelu, pre_f)[1](hidden_grad)[0].astype(BF)
    down_terms = jnp.einsum("pt,tq->pq", down_grad, activated, preferred_element_type=F32)
    mix_pieces = pieces_for(lambda other: part_of(pre_grad, other, 4, 0)[None], y, Y)
    pre_blocks = deliver("pre_y", mix_pieces, y, Y, 0)
    pre_blocks = pre_blocks.astype(F32)
    left_up = up_left.astype(F32)
    right_mix = jnp.stack(
        [
            sum(left_up[j, k][None, :] * pre_blocks[j] for j in range(BLOCKS)).astype(BF)
            for k in range(BLOCKS)
        ]
    )
    right_pieces = pieces_for(
        lambda other: lax.dynamic_index_in_dim(right_mix, other, 0, keepdims=False), y, Y
    )
    seen = []
    right_grad = deliver("right_y", right_pieces, y, Y, 0, seen)
    mixed_rows = mixed_arrive(after(mixed_plane, seen[1]))
    partial_value = jnp.einsum("pq,tq->pt", right[1], right_grad, preferred_element_type=F32)
    mix_grad = (grad_rows.astype(F32) + partial_value).astype(BF)
    up_terms = jnp.einsum("pt,tq->pq", mixed_rows, right_grad, preferred_element_type=F32)
    weight_pair = weight_core(jnp.stack([down_terms, up_terms]), core)

    mix_grad, weight_sums = blocks_to_cols(mix_grad, weight_line(weight_pair, x))
    weight_sums = weight_z(weight_sums, z_lo)
    mix_grad, weight_sums = lax.optimization_barrier((mix_grad, weight_sums))
    weight_sums = weight_z_hi(weight_sums, z_hi)
    mix_grad = mix_grad.astype(F32)
    conv_f = convolved.astype(F32)
    grad_layer = mix_grad * layer_cols
    conv_grad = (grad_layer * query_mine).astype(BF)
    query_terms = jnp.sum(grad_layer * conv_f, axis=(1, 2))
    first_grad = jnp.einsum("ij,cib->cjb", outer_tri, conv_grad, preferred_element_type=F32).astype(BF)
    outer_terms = jnp.einsum("cib,cjb->ij", conv_grad, first_pass, preferred_element_type=F32)
    back_pass = (first_grad.astype(F32) * twiddle_all).astype(BF)
    key_grad = jnp.einsum("bk,cab->cak", inner_tri, back_pass, preferred_element_type=F32)
    inner_terms = jnp.einsum("cab,cak->bk", back_pass, key_input, preferred_element_type=F32)
    key_terms = jnp.sum(key_grad * layer_cols, axis=(1, 2))
    grad_input = (mix_grad * (1.0 + query_mine * conv_f) + key_mine * key_grad).astype(BF)
    grad_input = seq_exchange("grad_input_seq", to_rows(grad_input))

    side = 128
    count = inner_len // side
    tiles = [
        inner_terms[i * side : (i + 1) * side, j * side : (j + 1) * side]
        for i in range(count)
        for j in range(i + 1)
    ]
    model = CHAN * width
    at = chan * width + seq * mine
    scales = jnp.zeros((2, model), F32)
    scales = lax.dynamic_update_slice(scales, jnp.stack([query_terms, key_terms]), (0, at))
    scale_rows = 2 * model // side
    sums = jnp.concatenate(tiles + [outer_terms, scales.reshape(scale_rows, side)], axis=0)
    whole_rows = -(-sums.shape[0] // 512) * 512
    sums = jnp.pad(sums, ((0, whole_rows - sums.shape[0]), (0, 0)))
    sums, weight_sums = lax.optimization_barrier((sums, weight_sums))
    for me, masks in ((y, Y), (z_lo, Z_LO)):
        sums = sum_spread_f32("sums", lambda other, sums=sums: part_of(sums, other, 4, 0), me, masks)
    sums = sum_spread_f32("sums", lambda other, sums=sums: sums, x, X)
    sums, grad_input = lax.optimization_barrier((sums, grad_input))
    sums = sum_spread_f32("sums", lambda other, sums=sums: sums, x, join(Z_HI, CORE))
    for me, masks in ((z_lo, Z_LO), (y, Y)):
        sums = gather("sums_back", sums, me, masks, 0)
    blank = jnp.zeros((side, side), F32)
    rows, taken = [], 0
    for i in range(count):
        rows.append(
            jnp.concatenate(
                [sums[(taken + j) * side : (taken + j + 1) * side] for j in range(i + 1)]
                + [blank] * (count - 1 - i),
                axis=1,
            )
        )
        taken += i + 1
    inner_total = jnp.where(inner_mask, jnp.concatenate(rows, axis=0), 0.0)
    outer_total = jnp.where(outer_mask, sums[taken * side : (taken + 1) * side], 0.0)
    scale_total = sums[(taken + 1) * side : (taken + 1) * side + scale_rows].reshape(2, model)
    scale_total = lax.dynamic_slice_in_dim(scale_total, chan * width, width, 1)

    token_scale = (SEQ * tokens) ** (-0.5)
    weights = weight_sums * token_scale
    grad_down, grad_up = weights[0], weights[1].T
    return (
        grad_input.reshape(width, tokens).T,
        grad_up[None],
        grad_down[None],
        scale_total[0] * token_scale,
        scale_total[1] * token_scale,
        inner_total * (outer_len * model) ** (-0.5),
        outer_total * (inner_len * model) ** (-0.5),
    )


def solution(mesh):
    return jax.shard_map(
        body,
        mesh=mesh,
        in_specs=(
            P("seq", "chan"),
            P("chan"),
            P("chan"),
            P("seq", None),
            P(),
            P(),
            P("seq", "chan"),
            P("seq", "chan"),
            P("chan", None, None),
            P(),
            P("chan", None, None),
            P(),
        ),
        out_specs=(
            P("seq", "chan"),
            P("chan", None, "seq"),
            P("chan", "seq", None),
            P("chan"),
            P("chan"),
            P(),
            P(),
        ),
        check_vma=False,
    )
```

time: 718 us -> 523 us (0.73)
  the two profiles are of different devices: /device:TPU:32 before, /device:TPU:1 now
where the time goes in v2:
time: 523 us; the launch traced here: 514 us
  waiting for transfers between devices  253 us (48%)
  starting transfers between devices  125 us (24%)
  local copies, waits for them, and re-layouts  73.8 us (14%)
  matrix products  34.1 us (7%)
  other arithmetic  25.7 us (5%)
    ppermute x48, waiting for transfers between devices, swap(): return lax.ppermute(value, ('seq', 'chan'), route)  251 us
    ppermute x48, starting transfers between devices, swap(): return lax.ppermute(value, ('seq', 'chan'), route)  78.8 us
    dynamic_update_slice x36, local copies, waits for them, and re-layouts, deliver(): lax.dynamic_update_slice_in_dim(out, arrived, jnp.bitwise_xor(me, step) *...  19.8 us
    all_to_all x2, starting transfers between devices, line_exchange(): lax.all_to_all(value, ('seq', 'chan'), split_axis=0, concat_axis=0, axis_...  14.1 us
    unnamed x43, local copies, waits for them, and re-layouts  13.8 us
    all_to_all x2, starting transfers between devices, seq_exchange(): return lax.all_to_all(value, 'seq', split_axis=0, concat_axis=0, tiled=True)  11.8 us
    all_to_all x2, starting transfers between devices, plane_exchange(): lax.all_to_all(value, 'seq', split_axis=0, concat_axis=0, axis_index_grou...  10.9 us
  transfers between devices with their start and end apart: 55, of which 33 were waited for; matrix products, arithmetic and copies ran while one was open for 18% of the time, Pallas kernels for 0%

profile of v2, /device:TPU:1, one launch (start us, length us, event | category | flops | bytes accessed | tf_op | source)
XLA Modules:
  0.0 513.7 jit_solution(12590715084428587544)
XLA Ops:
  5.0 2.5 collective-permute-start
  7.5 3.0 collective-permute-start.1
  12.5 6.8 %collective-permute-done = bf16[160,1024]{1,0:T(8,128)(2,1)S(1)} collective-permute-done((bf16[160,1024]{1,0:T(8,128)(2,1)S(1)}, bf16[160,1024]{1,0:T(8,128)(2,1)S(1)}, u32[]{:S(2)}, u32[]{:S(2)}) %collective-permute-start) | collective-permute-done | bytes 327712 | tf_op jit(solution)/shard_map/grad_z/ppermute | solution.py:27
  21.7 9.9 %collective-permute-done.2 = bf16[160,1024]{1,0:T(8,128)(2,1)S(1)} collective-permute-done((bf16[160,1024]{1,0:T(8,128)(2,1)S(1)}, bf16[160,1024]{1,0:T(8,128)(2,1)S(1)}, u32[]{:S(2)}, u32[]{:S(2)}) %collective-permute-start.2) | collective-permute-done | bytes 327712 | tf_op jit(solution)/shard_map/grad_z/ppermute | solution.py:27
  32.3 9.5 %all-to-all-start = ((bf16[4,1024,384]{2,1,0:T(8,128)(2,1)}), bf16[4,1024,384]{2,1,0:T(8,128)(2,1)S(1)}, u32[]{:S(2)}, u32[]{:S(2)}) async-start(bf16[4,1024,384]{2,1,0:T(8,128)(2,1)} %bitcast.243), calls=%async_computation | async-start | bytes 6291456 | tf_op jit(solution)/shard_map/hidden_pre_z/all_to_all | solution.py:97
  45.8 3.3 reshape.352
  49.1 2.7 pad_maximum_fusion.1
  52.5 41.2 %collective-permute-done.3 = bf16[2,80,384]{2,1,0:T(8,128)(2,1)S(1)} collective-permute-done((bf16[2,80,384]{2,1,0:T(8,128)(2,1)}, bf16[2,80,384]{2,1,0:T(8,128)(2,1)S(1)}, u32[]{:S(2)}, u32[]{:S(2)}) %collective-permute-start.3) | collective-permute-done | bytes 122912 | tf_op jit(solution)/shard_map/right_z/ppermute | solution.py:27
  94.4 25.6 %collective-permute-done.4 = bf16[2,80,384]{2,1,0:T(8,128)(2,1)S(1)} collective-permute-done((bf16[2,80,384]{2,1,0:T(8,128)(2,1)}, bf16[2,80,384]{2,1,0:T(8,128)(2,1)S(1)}, u32[]{:S(2)}, u32[]{:S(2)}) %collective-permute-start.4) | collective-permute-done | bytes 122912 | tf_op jit(solution)/shard_map/right_z/ppermute | solution.py:27
  122.6 2.5 collective-permute-start.7
  129.3 2.6 collective-permute-start.11
  132.0 2.6 collective-permute-start.12
  134.6 10.0 %collective-permute-done.7 = bf16[2,80,1536]{2,1,0:T(8,128)(2,1)S(1)} collective-permute-done((bf16[2,80,1536]{2,1,0:T(8,128)(2,1)}, bf16[2,80,1536]{2,1,0:T(8,128)(2,1)S(1)}, u32[]{:S(2)}, u32[]{:S(2)}) %collective-permute-start.7) | collective-permute-done | bytes 491552 | tf_op jit(solution)/shard_map/right_x/ppermute | solution.py:27
  144.7 6.2 %collective-permute-start.9 = (bf16[2,320,1536]{2,1,0:T(8,128)(2,1)S(1)}, bf16[2,320,1536]{2,1,0:T(8,128)(2,1)S(1)}, u32[]{:S(2)}, u32[]{:S(2)}) collective-permute-start(bf16[2,320,1536]{2,1,0:T(8,128)(2,1)S(1)} %constant_dynamic-update-slice_fusion.26), channel_id=1, source_target_pairs={{0,16},{1,17},{2,18},{3,19},{4,20},{5,21},{6,22},{7,23},{8,24},{9,... | collective-permute-start | bytes 5898248 | tf_op jit(solution)/shard_map/right_core/ppermute | solution.py:27
  154.9 3.1 collective-permute-start.14
  158.0 2.2 broadcast_in_dim.78
  164.4 8.1 %collective-permute-done.14 = bf16[640,256]{1,0:T(8,128)(2,1)S(1)} collective-permute-done((bf16[640,256]{1,0:T(8,128)(2,1)S(1)}, bf16[640,256]{1,0:T(8,128)(2,1)S(1)}, u32[]{:S(2)}, u32[]{:S(2)}) %collective-permute-start.14) | collective-permute-done | bytes 327712 | tf_op jit(solution)/shard_map/down_y/ppermute | solution.py:27
  173.2 5.8 %collective-permute-done.15 = bf16[640,256]{1,0:T(8,128)(2,1)S(1)} collective-permute-done((bf16[640,256]{1,0:T(8,128)(2,1)S(1)}, bf16[640,256]{1,0:T(8,128)(2,1)S(1)}, u32[]{:S(2)}, u32[]{:S(2)}) %collective-permute-start.15) | collective-permute-done | bytes 327712 | tf_op jit(solution)/shard_map/down_y/ppermute | solution.py:27
  181.3 2.0 copy.71
  183.2 7.1 %all-to-all-start.2 = ((bf16[16,96,512]{2,1,0:T(8,128)(2,1)}), bf16[16,96,512]{2,1,0:T(8,128)(2,1)S(1)}, u32[]{:S(2)}, u32[]{:S(2)}) async-start(bf16[16,96,512]{2,1,0:T(8,128)(2,1)} %pad_maximum_fusion.1), calls=%async_computation.2 | async-start | bytes 3145728 | tf_op jit(solution)/shard_map/layer_seq/all_to_all | solution.py:83
  190.4 8.5 %fusion.3 = bf16[1024,1536]{1,0:T(8,128)(2,1)S(1)} fusion(bf16[1024,1536]{1,0:T(8,128)(2,1)} %bitcast.244, bf16[640,1024]{1,0:T(8,128)(2,1)} %constant_dynamic-update-slice_fusion.17, bf16[2,640,1536]{2,1,0:T(8,128)(2,1)} %constant_dynamic-update-slice_fusion.24), kind=kOutput, calls=%fused_computation.12 | convolution fusion | flops 2046296064 | bytes 9568256 | tf_op jit(solution)/shard_map/pt,pq->tq/dot_general | solution.py:261
  201.6 2.8 collective-permute-start.18
  205.1 14.7 %collective-permute-done.16 = bf16[1,256,1536]{2,1,0:T(8,128)(2,1)} collective-permute-done((bf16[1,256,1536]{2,1,0:T(8,128)(2,1)}, bf16[1,256,1536]{2,1,0:T(8,128)(2,1)}, u32[]{:S(2)}, u32[]{:S(2)}) %collective-permute-start.16) | collective-permute-done | bytes 786464 | tf_op jit(solution)/shard_map/pre_y/ppermute | solution.py:27
  221.0 15.4 %collective-permute-done.17 = bf16[1,256,1536]{2,1,0:T(8,128)(2,1)} collective-permute-done((bf16[1,256,1536]{2,1,0:T(8,128)(2,1)}, bf16[1,256,1536]{2,1,0:T(8,128)(2,1)}, u32[]{:S(2)}, u32[]{:S(2)}) %collective-permute-start.17) | collective-permute-done | bytes 786464 | tf_op jit(solution)/shard_map/pre_y/ppermute | solution.py:27
  239.4 2.0 add_convert_fusion.2
  241.5 2.0 add_convert_fusion.4
  247.5 6.1 %all-to-all-start.3 = ((bf16[8,160,512]{2,1,0:T(8,128)(2,1)}), bf16[8,160,512]{2,1,0:T(8,128)(2,1)S(1)}, u32[]{:S(2)}, u32[]{:S(2)}) async-start(bf16[8,160,512]{2,1,0:T(8,128)(2,1)} %bitcast.238), calls=%async_computation.3 | async-start | bytes 2621440 | tf_op jit(solution)/shard_map/blocks_plane/all_to_all | solution.py:89
  253.5 2.0 pad_maximum_fusion
  257.1 19.3 %collective-permute-done.19 = bf16[256,1536]{1,0:T(8,128)(2,1)} collective-permute-done((bf16[256,1536]{1,0:T(8,128)(2,1)S(1)}, bf16[256,1536]{1,0:T(8,128)(2,1)}, u32[]{:S(2)}, u32[]{:S(2)}) %collective-permute-start.19) | collective-permute-done | bytes 786464 | tf_op jit(solution)/shard_map/right_y/ppermute | solution.py:27
  278.1 3.1 copy.51
  281.2 7.4 %all-to-all-start.4 = ((bf16[8,80,1024]{2,1,0:T(8,128)(2,1)}), bf16[8,80,1024]{2,1,0:T(8,128)(2,1)S(1)}, u32[]{:S(2)}, u32[]{:S(2)}) async-start(bf16[8,80,1024]{2,1,0:T(8,128)(2,1)} %bitcast.236), calls=%async_computation.4 | async-start | bytes 2621440 | tf_op jit(solution)/shard_map/blocks_z/all_to_all | solution.py:109
  288.6 2.6 collective-permute-start.20
  291.4 6.7 %fusion.16 = f32[640,1536]{1,0:T(8,128)} fusion(bf16[640,1024]{1,0:T(8,128)(2,1)} %constant_dynamic-update-slice_fusion.17, bf16[1024,1536]{1,0:T(8,128)(2,1)} %bitcast.245), kind=kOutput, calls=%fused_computation.29 | convolution fusion | flops 2028994560 | bytes 8388608 | tf_op jit(solution)/shard_map/pt,tq->pq/dot_general | solution.py:265
  300.9 2.1 constant_dynamic-update-slice_fusion.11
  303.0 5.3 %collective-permute-done.20 = bf16[256,1536]{1,0:T(8,128)(2,1)S(1)} collective-permute-done((bf16[256,1536]{1,0:T(8,128)(2,1)}, bf16[256,1536]{1,0:T(8,128)(2,1)S(1)}, u32[]{:S(2)}, u32[]{:S(2)}) %collective-permute-start.20) | collective-permute-done | bytes 786464 | tf_op jit(solution)/shard_map/right_y/ppermute | solution.py:27
  309.3 17.3 %collective-permute-done.21 = bf16[256,1536]{1,0:T(8,128)(2,1)S(1)} collective-permute-done((bf16[256,1536]{1,0:T(8,128)(2,1)}, bf16[256,1536]{1,0:T(8,128)(2,1)S(1)}, u32[]{:S(2)}, u32[]{:S(2)}) %collective-permute-start.21) | collective-permute-done | bytes 786464 | tf_op jit(solution)/shard_map/right_y/ppermute | solution.py:27
  327.8 4.3 convolution_bitcast_fusion
  335.0 5.1 add_convert_fusion
  341.3 6.7 %all-to-all-start.1 = ((bf16[8,80,1024]{2,1,0:T(8,128)(2,1)}), bf16[8,80,1024]{2,1,0:T(8,128)(2,1)S(1)}, u32[]{:S(2)}, u32[]{:S(2)}) async-start(bf16[8,80,1024]{2,1,0:T(8,128)(2,1)} %bitcast.234), calls=%async_computation.1 | async-start | bytes 2621440 | tf_op jit(solution)/shard_map/cols_z/all_to_all | solution.py:109
  348.0 3.3 fusion.14
  353.3 2.2 collective-permute-start.25
  358.5 19.4 %collective-permute-done.25 = bf16[2,2,40,1536]{3,2,0,1:T(8,128)(2,1)} collective-permute-done((bf16[2,2,40,1536]{3,2,0,1:T(8,128)(2,1)}, bf16[2,2,40,1536]{3,2,0,1:T(8,128)(2,1)}, u32[]{:S(2)}, u32[]{:S(2)}) %collective-permute-start.25) | collective-permute-done | bytes 491552 | tf_op jit(solution)/shard_map/weight_x/ppermute | solution.py:27
  379.3 2.8 fusion.38
  387.7 4.8 all-to-all-start.5
  393.7 3.3 collective-permute-start.28
  397.4 3.3 collective-permute-done.28
  400.7 7.2 %collective-permute-done.27 = bf16[2,2,40,384]{3,2,0,1:T(8,128)(2,1)} collective-permute-done((bf16[2,2,40,384]{3,2,0,1:T(8,128)(2,1)S(1)}, bf16[2,2,40,384]{3,2,0,1:T(8,128)(2,1)}, u32[]{:S(2)}, u32[]{:S(2)}) %collective-permute-start.27) | collective-permute-done | bytes 122912 | tf_op jit(solution)/shard_map/weight_z/ppermute | solution.py:27
  416.5 3.1 fusion.23
  419.9 5.5 %collective-permute-start.29 = (bf16[2,40,384]{2,1,0:T(8,128)(2,1)S(1)}, bf16[2,40,384]{2,1,0:T(8,128)(2,1)S(1)}, u32[]{:S(2)}, u32[]{:S(2)}) collective-permute-start(bf16[2,40,384]{2,1,0:T(8,128)(2,1)S(1)} %fusion.51), channel_id=1, source_target_pairs={{0,128},{1,129},{2,130},{3,131},{4,132},{5,133},{6,134},{7,135},{8... | collective-permute-start | bytes 184328 | tf_op jit(solution)/shard_map/weight_z_hi/ppermute | solution.py:27
  425.4 2.5 copy.93
  427.9 4.6 all-to-all-start.6
  436.9 2.4 fusion.31
  441.2 2.4 collective-permute-start.32
  444.6 8.4 %collective-permute-done.32 = f32[384,128]{1,0:T(8,128)S(1)} collective-permute-done((f32[384,128]{1,0:T(8,128)S(1)}, f32[384,128]{1,0:T(8,128)S(1)}, u32[]{:S(2)}, u32[]{:S(2)}) %collective-permute-start.32) | collective-permute-done | bytes 196640 | tf_op jit(solution)/shard_map/sums/ppermute | solution.py:27
  453.4 2.2 collective-permute-start.35
  458.5 6.6 %collective-permute-done.34 = f32[96,128]{1,0:T(8,128)S(1)} collective-permute-done((f32[96,128]{1,0:T(8,128)S(1)}, f32[96,128]{1,0:T(8,128)S(1)}, u32[]{:S(2)}, u32[]{:S(2)}) %collective-permute-start.34) | collective-permute-done | bytes 49184 | tf_op jit(solution)/shard_map/sums/ppermute | solution.py:27
  473.1 7.7 %collective-permute-start.41 = (f32[96,128]{1,0:T(8,128)S(1)}, f32[96,128]{1,0:T(8,128)S(1)}, u32[]{:S(2)}, u32[]{:S(2)}) collective-permute-start(f32[96,128]{1,0:T(8,128)S(1)} %add_add_fusion.2), channel_id=1, source_target_pairs={{0,144},{1,145},{2,146},{3,147},{4,148},{5,149},{6,150},{7,151},{8... | collective-permute-start | bytes 147464 | tf_op jit(solution)/shard_map/sums/ppermute | solution.py:27
  480.8 2.5 collective-permute-start.40
  483.2 4.5 collective-permute-done.40
  487.9 2.3 collective-permute-start.43
  492.4 2.6 collective-permute-done.44
  497.5 3.2 collective-permute-start.46
  501.1 5.0 collective-permute-done.46
  506.2 4.6 collective-permute-done.47
  (213 shorter events, 105.5 us)
Async XLA Ops:
  0.7 3.6 copy-start.6
  5.0 14.2 %collective-permute-start = (bf16[160,1024]{1,0:T(8,128)(2,1)S(1)}, bf16[160,1024]{1,0:T(8,128)(2,1)S(1)}, u32[]{:S(2)}, u32[]{:S(2)}) collective-permute-start(bf16[160,1024]{1,0:T(8,128)(2,1)S(1)} %get-tuple-element.39), channel_id=1, source_target_pairs={{0,1},{1,0},{2,3},{3,2},{4,5},{5,4},{6,7},{7,6},{8,9},{9,8},{10,11... | collective-permute-start | bytes 983048 | tf_op jit(solution)/shard_map/grad_z/ppermute | solution.py:27
  7.5 13.4 %collective-permute-start.1 = (bf16[160,1024]{1,0:T(8,128)(2,1)S(1)}, bf16[160,1024]{1,0:T(8,128)(2,1)S(1)}, u32[]{:S(2)}, u32[]{:S(2)}) collective-permute-start(bf16[160,1024]{1,0:T(8,128)(2,1)S(1)} %get-tuple-element.40), channel_id=1, source_target_pairs={{0,2},{1,3},{2,0},{3,1},{4,6},{5,7},{6,4},{7,5},{8,10},{9,11},{10,... | collective-permute-start | bytes 983048 | tf_op jit(solution)/shard_map/grad_z/ppermute | solution.py:27
  10.5 21.1 %collective-permute-start.2 = (bf16[160,1024]{1,0:T(8,128)(2,1)S(1)}, bf16[160,1024]{1,0:T(8,128)(2,1)S(1)}, u32[]{:S(2)}, u32[]{:S(2)}) collective-permute-start(bf16[160,1024]{1,0:T(8,128)(2,1)S(1)} %get-tuple-element.41), channel_id=1, source_target_pairs={{0,3},{1,2},{2,1},{3,0},{4,7},{5,6},{6,5},{7,4},{8,11},{9,10},{10,... | collective-permute-start | bytes 983048 | tf_op jit(solution)/shard_map/grad_z/ppermute | solution.py:27
  32.3 149.0 %all-to-all-start = ((bf16[4,1024,384]{2,1,0:T(8,128)(2,1)}), bf16[4,1024,384]{2,1,0:T(8,128)(2,1)S(1)}, u32[]{:S(2)}, u32[]{:S(2)}) async-start(bf16[4,1024,384]{2,1,0:T(8,128)(2,1)} %bitcast.243), calls=%async_computation | async-start | bytes 6291456 | tf_op jit(solution)/shard_map/hidden_pre_z/all_to_all | solution.py:97
  41.8 7.2 %copy-start.10 = (f32[8,512]{1,0:T(8,128)S(1)}, f32[8,512]{1,0:T(8,128)}, u32[]{:S(2)}) copy-start(f32[8,512]{1,0:T(8,128)} %param.15) | copy-start | bytes 49156
  41.8 51.9 %collective-permute-start.3 = (bf16[2,80,384]{2,1,0:T(8,128)(2,1)}, bf16[2,80,384]{2,1,0:T(8,128)(2,1)S(1)}, u32[]{:S(2)}, u32[]{:S(2)}) collective-permute-start(bf16[2,80,384]{2,1,0:T(8,128)(2,1)} %get-tuple-element.106), channel_id=1, source_target_pairs={{0,1},{1,0},{2,3},{3,2},{4,5},{5,4},{6,7},{7,6},{8,9},{9,8},{10,11... | collective-permute-start | bytes 368648 | tf_op jit(solution)/shard_map/right_z/ppermute | solution.py:27
  43.6 76.4 %collective-permute-start.4 = (bf16[2,80,384]{2,1,0:T(8,128)(2,1)}, bf16[2,80,384]{2,1,0:T(8,128)(2,1)S(1)}, u32[]{:S(2)}, u32[]{:S(2)}) collective-permute-start(bf16[2,80,384]{2,1,0:T(8,128)(2,1)} %get-tuple-element.106), channel_id=1, source_target_pairs={{0,2},{1,3},{2,0},{3,1},{4,6},{5,7},{6,4},{7,5},{8,10},{9,11},{10,... | collective-permute-start | bytes 368648 | tf_op jit(solution)/shard_map/right_z/ppermute | solution.py:27
  45.4 75.3 %collective-permute-start.5 = (bf16[2,80,384]{2,1,0:T(8,128)(2,1)}, bf16[2,80,384]{2,1,0:T(8,128)(2,1)S(1)}, u32[]{:S(2)}, u32[]{:S(2)}) collective-permute-start(bf16[2,80,384]{2,1,0:T(8,128)(2,1)} %get-tuple-element.106), channel_id=1, source_target_pairs={{0,3},{1,2},{2,1},{3,0},{4,7},{5,6},{6,5},{7,4},{8,11},{9,10},{10,... | collective-permute-start | bytes 368648 | tf_op jit(solution)/shard_map/right_z/ppermute | solution.py:27
  121.3 10.7 %collective-permute-start.6 = (bf16[2,80,1536]{2,1,0:T(8,128)(2,1)}, bf16[2,80,1536]{2,1,0:T(8,128)(2,1)S(1)}, u32[]{:S(2)}, u32[]{:S(2)}) collective-permute-start(bf16[2,80,1536]{2,1,0:T(8,128)(2,1)} %constant_dynamic-update-slice_fusion.30), channel_id=1, source_target_pairs={{0,32},{1,33},{2,34},{3,35},{4,36},{5,37},{6,38},{7,39},{8,40},{9,... | collective-permute-start | bytes 1474568 | tf_op jit(solution)/shard_map/right_x/ppermute | solution.py:27
  122.6 22.0 %collective-permute-start.7 = (bf16[2,80,1536]{2,1,0:T(8,128)(2,1)}, bf16[2,80,1536]{2,1,0:T(8,128)(2,1)S(1)}, u32[]{:S(2)}, u32[]{:S(2)}) collective-permute-start(bf16[2,80,1536]{2,1,0:T(8,128)(2,1)} %constant_dynamic-update-slice_fusion.30), channel_id=1, source_target_pairs={{0,64},{1,65},{2,66},{3,67},{4,68},{5,69},{6,70},{7,71},{8,72},{9,... | collective-permute-start | bytes 1474568 | tf_op jit(solution)/shard_map/right_x/ppermute | solution.py:27
  125.2 19.5 %collective-permute-start.8 = (bf16[2,80,1536]{2,1,0:T(8,128)(2,1)}, bf16[2,80,1536]{2,1,0:T(8,128)(2,1)S(1)}, u32[]{:S(2)}, u32[]{:S(2)}) collective-permute-start(bf16[2,80,1536]{2,1,0:T(8,128)(2,1)} %constant_dynamic-update-slice_fusion.30), channel_id=1, source_target_pairs={{0,96},{1,97},{2,98},{3,99},{4,100},{5,101},{6,102},{7,103},{8,104... | collective-permute-start | bytes 1474568 | tf_op jit(solution)/shard_map/right_x/ppermute | solution.py:27
  127.9 23.1 %collective-permute-start.10 = (bf16[1,640,256]{2,1,0:T(8,128)(2,1)S(1)}, bf16[1,640,256]{2,1,0:T(8,128)(2,1)S(1)}, u32[]{:S(2)}, u32[]{:S(2)}) collective-permute-start(bf16[1,640,256]{2,1,0:T(8,128)(2,1)S(1)} %bitcast.253), channel_id=1, source_target_pairs={{0,4},{1,5},{2,6},{3,7},{4,0},{5,1},{6,2},{7,3},{8,12},{9,13},{10,... | collective-permute-start | bytes 983048 | tf_op jit(solution)/shard_map/grad_y/ppermute | solution.py:27
  129.3 21.7 %collective-permute-start.11 = (bf16[1,640,256]{2,1,0:T(8,128)(2,1)S(1)}, bf16[1,640,256]{2,1,0:T(8,128)(2,1)S(1)}, u32[]{:S(2)}, u32[]{:S(2)}) collective-permute-start(bf16[1,640,256]{2,1,0:T(8,128)(2,1)S(1)} %bitcast.252), channel_id=1, source_target_pairs={{0,8},{1,9},{2,10},{3,11},{4,12},{5,13},{6,14},{7,15},{8,0},{9,1},... | collective-permute-start | bytes 983048 | tf_op jit(solution)/shard_map/grad_y/ppermute | solution.py:27
  132.0 19.1 %collective-permute-start.12 = (bf16[1,640,256]{2,1,0:T(8,128)(2,1)S(1)}, bf16[1,640,256]{2,1,0:T(8,128)(2,1)S(1)}, u32[]{:S(2)}, u32[]{:S(2)}) collective-permute-start(bf16[1,640,256]{2,1,0:T(8,128)(2,1)S(1)} %bitcast.251), channel_id=1, source_target_pairs={{0,12},{1,13},{2,14},{3,15},{4,8},{5,9},{6,10},{7,11},{8,4},{9,5},... | collective-permute-start | bytes 983048 | tf_op jit(solution)/shard_map/grad_y/ppermute | solution.py:27
  144.7 35.2 %collective-permute-start.9 = (bf16[2,320,1536]{2,1,0:T(8,128)(2,1)S(1)}, bf16[2,320,1536]{2,1,0:T(8,128)(2,1)S(1)}, u32[]{:S(2)}, u32[]{:S(2)}) collective-permute-start(bf16[2,320,1536]{2,1,0:T(8,128)(2,1)S(1)} %constant_dynamic-update-slice_fusion.26), channel_id=1, source_target_pairs={{0,16},{1,17},{2,18},{3,19},{4,20},{5,21},{6,22},{7,23},{8,24},{9,... | collective-permute-start | bytes 5898248 | tf_op jit(solution)/shard_map/right_core/ppermute | solution.py:27
  153.5 10.1 %collective-permute-start.13 = (bf16[640,256]{1,0:T(8,128)(2,1)S(1)}, bf16[640,256]{1,0:T(8,128)(2,1)S(1)}, u32[]{:S(2)}, u32[]{:S(2)}) collective-permute-start(bf16[640,256]{1,0:T(8,128)(2,1)S(1)} %get-tuple-element.47), channel_id=1, source_target_pairs={{0,4},{1,5},{2,6},{3,7},{4,0},{5,1},{6,2},{7,3},{8,12},{9,13},{10,... | collective-permute-start | bytes 983048 | tf_op jit(solution)/shard_map/down_y/ppermute | solution.py:27
  154.9 17.5 %collective-permute-start.14 = (bf16[640,256]{1,0:T(8,128)(2,1)S(1)}, bf16[640,256]{1,0:T(8,128)(2,1)S(1)}, u32[]{:S(2)}, u32[]{:S(2)}) collective-permute-start(bf16[640,256]{1,0:T(8,128)(2,1)S(1)} %get-tuple-element.48), channel_id=1, source_target_pairs={{0,8},{1,9},{2,10},{3,11},{4,12},{5,13},{6,14},{7,15},{8,0},{9,1},... | collective-permute-start | bytes 983048 | tf_op jit(solution)/shard_map/down_y/ppermute | solution.py:27
  161.6 17.5 %collective-permute-start.15 = (bf16[640,256]{1,0:T(8,128)(2,1)S(1)}, bf16[640,256]{1,0:T(8,128)(2,1)S(1)}, u32[]{:S(2)}, u32[]{:S(2)}) collective-permute-start(bf16[640,256]{1,0:T(8,128)(2,1)S(1)} %get-tuple-element.49), channel_id=1, source_target_pairs={{0,12},{1,13},{2,14},{3,15},{4,8},{5,9},{6,10},{7,11},{8,4},{9,5},... | collective-permute-start | bytes 983048 | tf_op jit(solution)/shard_map/down_y/ppermute | solution.py:27
  183.2 60.2 %all-to-all-start.2 = ((bf16[16,96,512]{2,1,0:T(8,128)(2,1)}), bf16[16,96,512]{2,1,0:T(8,128)(2,1)S(1)}, u32[]{:S(2)}, u32[]{:S(2)}) async-start(bf16[16,96,512]{2,1,0:T(8,128)(2,1)} %pad_maximum_fusion.1), calls=%async_computation.2 | async-start | bytes 3145728 | tf_op jit(solution)/shard_map/layer_seq/all_to_all | solution.py:83
  198.9 2.6 copy-start.9
  198.9 5.7 %copy-start.13 = (f32[160]{0:T(256)S(1)}, f32[160]{0:T(256)}, u32[]{:S(2)}) copy-start(f32[160]{0:T(256)} %param.13) | copy-start | bytes 1924
  198.9 5.8 %copy-start.14 = (f32[160]{0:T(256)S(1)}, f32[160]{0:T(256)}, u32[]{:S(2)}) copy-start(f32[160]{0:T(256)} %param.14) | copy-start | bytes 1924
  200.4 19.4 %collective-permute-start.16 = (bf16[1,256,1536]{2,1,0:T(8,128)(2,1)}, bf16[1,256,1536]{2,1,0:T(8,128)(2,1)}, u32[]{:S(2)}, u32[]{:S(2)}) collective-permute-start(bf16[1,256,1536]{2,1,0:T(8,128)(2,1)} %get-tuple-element.52), channel_id=1, source_target_pairs={{0,4},{1,5},{2,6},{3,7},{4,0},{5,1},{6,2},{7,3},{8,12},{9,13},{10,... | collective-permute-start | bytes 2359304 | tf_op jit(solution)/shard_map/pre_y/ppermute | solution.py:27
  200.4 36.0 %collective-permute-start.17 = (bf16[1,256,1536]{2,1,0:T(8,128)(2,1)}, bf16[1,256,1536]{2,1,0:T(8,128)(2,1)}, u32[]{:S(2)}, u32[]{:S(2)}) collective-permute-start(bf16[1,256,1536]{2,1,0:T(8,128)(2,1)} %get-tuple-element.53), channel_id=1, source_target_pairs={{0,8},{1,9},{2,10},{3,11},{4,12},{5,13},{6,14},{7,15},{8,0},{9,1},... | collective-permute-start | bytes 2359304 | tf_op jit(solution)/shard_map/pre_y/ppermute | solution.py:27
  201.6 36.9 %collective-permute-start.18 = (bf16[1,256,1536]{2,1,0:T(8,128)(2,1)}, bf16[1,256,1536]{2,1,0:T(8,128)(2,1)S(1)}, u32[]{:S(2)}, u32[]{:S(2)}) collective-permute-start(bf16[1,256,1536]{2,1,0:T(8,128)(2,1)} %get-tuple-element.54), channel_id=1, source_target_pairs={{0,12},{1,13},{2,14},{3,15},{4,8},{5,9},{6,10},{7,11},{8,4},{9,5},... | collective-permute-start | bytes 2359304 | tf_op jit(solution)/shard_map/pre_y/ppermute | solution.py:27
  247.5 28.9 %all-to-all-start.3 = ((bf16[8,160,512]{2,1,0:T(8,128)(2,1)}), bf16[8,160,512]{2,1,0:T(8,128)(2,1)S(1)}, u32[]{:S(2)}, u32[]{:S(2)}) async-start(bf16[8,160,512]{2,1,0:T(8,128)(2,1)} %bitcast.238), calls=%async_computation.3 | async-start | bytes 2621440 | tf_op jit(solution)/shard_map/blocks_plane/all_to_all | solution.py:89
  257.1 19.3 %collective-permute-start.19 = (bf16[256,1536]{1,0:T(8,128)(2,1)S(1)}, bf16[256,1536]{1,0:T(8,128)(2,1)}, u32[]{:S(2)}, u32[]{:S(2)}) collective-permute-start(bf16[256,1536]{1,0:T(8,128)(2,1)S(1)} %get-tuple-element.56), channel_id=1, source_target_pairs={{0,4},{1,5},{2,6},{3,7},{4,0},{5,1},{6,2},{7,3},{8,12},{9,13},{10,... | collective-permute-start | bytes 2359304 | tf_op jit(solution)/shard_map/right_y/ppermute | solution.py:27
  281.2 46.5 %all-to-all-start.4 = ((bf16[8,80,1024]{2,1,0:T(8,128)(2,1)}), bf16[8,80,1024]{2,1,0:T(8,128)(2,1)S(1)}, u32[]{:S(2)}, u32[]{:S(2)}) async-start(bf16[8,80,1024]{2,1,0:T(8,128)(2,1)} %bitcast.236), calls=%async_computation.4 | async-start | bytes 2621440 | tf_op jit(solution)/shard_map/blocks_z/all_to_all | solution.py:109
  288.6 19.7 %collective-permute-start.20 = (bf16[256,1536]{1,0:T(8,128)(2,1)}, bf16[256,1536]{1,0:T(8,128)(2,1)S(1)}, u32[]{:S(2)}, u32[]{:S(2)}) collective-permute-start(bf16[256,1536]{1,0:T(8,128)(2,1)} %get-tuple-element.57), channel_id=1, source_target_pairs={{0,8},{1,9},{2,10},{3,11},{4,12},{5,13},{6,14},{7,15},{8,0},{9,1},... | collective-permute-start | bytes 2359304 | tf_op jit(solution)/shard_map/right_y/ppermute | solution.py:27
  291.2 35.4 %collective-permute-start.21 = (bf16[256,1536]{1,0:T(8,128)(2,1)}, bf16[256,1536]{1,0:T(8,128)(2,1)S(1)}, u32[]{:S(2)}, u32[]{:S(2)}) collective-permute-start(bf16[256,1536]{1,0:T(8,128)(2,1)} %get-tuple-element.58), channel_id=1, source_target_pairs={{0,12},{1,13},{2,14},{3,15},{4,8},{5,9},{6,10},{7,11},{8,4},{9,5},... | collective-permute-start | bytes 2359304 | tf_op jit(solution)/shard_map/right_y/ppermute | solution.py:27
  327.8 4.3 copy-start
  334.5 13.4 %collective-permute-start.22 = (bf16[2,8,40,1536]{3,2,1,0:T(8,128)(2,1)}, bf16[2,8,40,1536]{3,2,1,0:T(8,128)(2,1)}, u32[]{:S(2)}, u32[]{:S(2)}) collective-permute-start(bf16[2,8,40,1536]{3,2,1,0:T(8,128)(2,1)} %fusion.27), channel_id=1, source_target_pairs={{0,16},{1,17},{2,18},{3,19},{4,20},{5,21},{6,22},{7,23},{8,24},{9,... | collective-permute-start | bytes 5898248 | tf_op jit(solution)/shard_map/weight_core/ppermute | solution.py:27
  341.3 41.5 %all-to-all-start.1 = ((bf16[8,80,1024]{2,1,0:T(8,128)(2,1)}), bf16[8,80,1024]{2,1,0:T(8,128)(2,1)S(1)}, u32[]{:S(2)}, u32[]{:S(2)}) async-start(bf16[8,80,1024]{2,1,0:T(8,128)(2,1)} %bitcast.234), calls=%async_computation.1 | async-start | bytes 2621440 | tf_op jit(solution)/shard_map/cols_z/all_to_all | solution.py:109
  353.3 24.6 %collective-permute-start.25 = (bf16[2,2,40,1536]{3,2,0,1:T(8,128)(2,1)}, bf16[2,2,40,1536]{3,2,0,1:T(8,128)(2,1)}, u32[]{:S(2)}, u32[]{:S(2)}) collective-permute-start(bf16[2,2,40,1536]{3,2,0,1:T(8,128)(2,1)} %bitcast.226), channel_id=1, source_target_pairs={{0,96},{1,97},{2,98},{3,99},{4,100},{5,101},{6,102},{7,103},{8,104... | collective-permute-start | bytes 1474568 | tf_op jit(solution)/shard_map/weight_x/ppermute | solution.py:27
  356.4 21.5 %collective-permute-start.24 = (bf16[2,2,40,1536]{3,2,0,1:T(8,128)(2,1)}, bf16[2,2,40,1536]{3,2,0,1:T(8,128)(2,1)}, u32[]{:S(2)}, u32[]{:S(2)}) collective-permute-start(bf16[2,2,40,1536]{3,2,0,1:T(8,128)(2,1)} %bitcast.225), channel_id=1, source_target_pairs={{0,64},{1,65},{2,66},{3,67},{4,68},{5,69},{6,70},{7,71},{8,72},{9,... | collective-permute-start | bytes 1474568 | tf_op jit(solution)/shard_map/weight_x/ppermute | solution.py:27
  358.0 21.3 %collective-permute-start.23 = (bf16[2,2,40,1536]{3,2,0,1:T(8,128)(2,1)}, bf16[2,2,40,1536]{3,2,0,1:T(8,128)(2,1)}, u32[]{:S(2)}, u32[]{:S(2)}) collective-permute-start(bf16[2,2,40,1536]{3,2,0,1:T(8,128)(2,1)} %bitcast.224), channel_id=1, source_target_pairs={{0,32},{1,33},{2,34},{3,35},{4,36},{5,37},{6,38},{7,39},{8,40},{9,... | collective-permute-start | bytes 1474568 | tf_op jit(solution)/shard_map/weight_x/ppermute | solution.py:27
  387.7 22.7 %all-to-all-start.5 = ((bf16[8,160,512]{2,1,0:T(8,128)(2,1)}), bf16[8,160,512]{2,1,0:T(8,128)(2,1)S(1)}, u32[]{:S(2)}, u32[]{:S(2)}) async-start(bf16[8,160,512]{2,1,0:T(8,128)(2,1)} %copy.58), calls=%async_computation.5 | async-start | bytes 2621440 | tf_op jit(solution)/shard_map/cols_plane/all_to_all | solution.py:89
  393.7 7.0 %collective-permute-start.28 = (bf16[2,2,40,384]{3,2,0,1:T(8,128)(2,1)S(1)}, bf16[2,2,40,384]{3,2,0,1:T(8,128)(2,1)}, u32[]{:S(2)}, u32[]{:S(2)}) collective-permute-start(bf16[2,2,40,384]{3,2,0,1:T(8,128)(2,1)S(1)} %get-tuple-element.142), channel_id=1, source_target_pairs={{0,3},{1,2},{2,1},{3,0},{4,7},{5,6},{6,5},{7,4},{8,11},{9,10},{10,... | collective-permute-start | bytes 368648 | tf_op jit(solution)/shard_map/weight_z/ppermute | solution.py:27
  397.0 10.9 %collective-permute-start.27 = (bf16[2,2,40,384]{3,2,0,1:T(8,128)(2,1)S(1)}, bf16[2,2,40,384]{3,2,0,1:T(8,128)(2,1)}, u32[]{:S(2)}, u32[]{:S(2)}) collective-permute-start(bf16[2,2,40,384]{3,2,0,1:T(8,128)(2,1)S(1)} %get-tuple-element.143), channel_id=1, source_target_pairs={{0,2},{1,3},{2,0},{3,1},{4,6},{5,7},{6,4},{7,5},{8,10},{9,11},{10,... | collective-permute-start | bytes 368648 | tf_op jit(solution)/shard_map/weight_z/ppermute | solution.py:27
  397.0 10.9 %collective-permute-start.26 = (bf16[2,2,40,384]{3,2,0,1:T(8,128)(2,1)S(1)}, bf16[2,2,40,384]{3,2,0,1:T(8,128)(2,1)}, u32[]{:S(2)}, u32[]{:S(2)}) collective-permute-start(bf16[2,2,40,384]{3,2,0,1:T(8,128)(2,1)S(1)} %get-tuple-element.141), channel_id=1, source_target_pairs={{0,1},{1,0},{2,3},{3,2},{4,5},{5,4},{6,7},{7,6},{8,9},{9,8},{10,11... | collective-permute-start | bytes 368648 | tf_op jit(solution)/shard_map/weight_z/ppermute | solution.py:27
  411.6 4.8 copy-start.5
  411.6 4.8 copy-start.12
  412.6 3.2 copy-start.7
  419.9 21.3 %collective-permute-start.29 = (bf16[2,40,384]{2,1,0:T(8,128)(2,1)S(1)}, bf16[2,40,384]{2,1,0:T(8,128)(2,1)S(1)}, u32[]{:S(2)}, u32[]{:S(2)}) collective-permute-start(bf16[2,40,384]{2,1,0:T(8,128)(2,1)S(1)} %fusion.51), channel_id=1, source_target_pairs={{0,128},{1,129},{2,130},{3,131},{4,132},{5,133},{6,134},{7,135},{8... | collective-permute-start | bytes 184328 | tf_op jit(solution)/shard_map/weight_z_hi/ppermute | solution.py:27
  427.9 45.2 %all-to-all-start.6 = ((bf16[16,80,512]{2,1,0:T(8,128)(2,1)}), bf16[16,80,512]{2,1,0:T(8,128)(2,1)S(1)}, u32[]{:S(2)}, u32[]{:S(2)}) async-start(bf16[16,80,512]{2,1,0:T(8,128)(2,1)} %bitcast.232), calls=%async_computation.6 | async-start | bytes 2621440 | tf_op jit(solution)/shard_map/grad_input_seq/all_to_all | solution.py:83
  441.2 11.7 %collective-permute-start.32 = (f32[384,128]{1,0:T(8,128)S(1)}, f32[384,128]{1,0:T(8,128)S(1)}, u32[]{:S(2)}, u32[]{:S(2)}) collective-permute-start(f32[384,128]{1,0:T(8,128)S(1)} %get-tuple-element.156), channel_id=1, source_target_pairs={{0,12},{1,13},{2,14},{3,15},{4,8},{5,9},{6,10},{7,11},{8,4},{9,5},... | collective-permute-start | bytes 589832 | tf_op jit(solution)/shard_map/sums/ppermute | solution.py:27
  443.7 9.3 %collective-permute-start.31 = (f32[384,128]{1,0:T(8,128)S(1)}, f32[384,128]{1,0:T(8,128)S(1)}, u32[]{:S(2)}, u32[]{:S(2)}) collective-permute-start(f32[384,128]{1,0:T(8,128)S(1)} %get-tuple-element.157), channel_id=1, source_target_pairs={{0,8},{1,9},{2,10},{3,11},{4,12},{5,13},{6,14},{7,15},{8,0},{9,1},... | collective-permute-start | bytes 589832 | tf_op jit(solution)/shard_map/sums/ppermute | solution.py:27
  443.7 9.6 %collective-permute-start.30 = (f32[384,128]{1,0:T(8,128)S(1)}, f32[384,128]{1,0:T(8,128)S(1)}, u32[]{:S(2)}, u32[]{:S(2)}) collective-permute-start(f32[384,128]{1,0:T(8,128)S(1)} %get-tuple-element.155), channel_id=1, source_target_pairs={{0,4},{1,5},{2,6},{3,7},{4,0},{5,1},{6,2},{7,3},{8,12},{9,13},{10,... | collective-permute-start | bytes 589832 | tf_op jit(solution)/shard_map/sums/ppermute | solution.py:27
  453.4 5.1 collective-permute-start.35
  455.6 9.6 %collective-permute-start.34 = (f32[96,128]{1,0:T(8,128)S(1)}, f32[96,128]{1,0:T(8,128)S(1)}, u32[]{:S(2)}, u32[]{:S(2)}) collective-permute-start(f32[96,128]{1,0:T(8,128)S(1)} %get-tuple-element.160), channel_id=1, source_target_pairs={{0,2},{1,3},{2,0},{3,1},{4,6},{5,7},{6,4},{7,5},{8,10},{9,11},{10,... | collective-permute-start | bytes 147464 | tf_op jit(solution)/shard_map/sums/ppermute | solution.py:27
  455.8 11.2 %collective-permute-start.33 = (f32[96,128]{1,0:T(8,128)S(1)}, f32[96,128]{1,0:T(8,128)S(1)}, u32[]{:S(2)}, u32[]{:S(2)}) collective-permute-start(f32[96,128]{1,0:T(8,128)S(1)} %get-tuple-element.158), channel_id=1, source_target_pairs={{0,1},{1,0},{2,3},{3,2},{4,5},{5,4},{6,7},{7,6},{8,9},{9,8},{10,11... | collective-permute-start | bytes 147464 | tf_op jit(solution)/shard_map/sums/ppermute | solution.py:27
  467.0 4.2 collective-permute-start.38
  468.6 4.4 collective-permute-start.37
  469.9 3.2 collective-permute-start.36
  473.1 10.2 %collective-permute-start.41 = (f32[96,128]{1,0:T(8,128)S(1)}, f32[96,128]{1,0:T(8,128)S(1)}, u32[]{:S(2)}, u32[]{:S(2)}) collective-permute-start(f32[96,128]{1,0:T(8,128)S(1)} %add_add_fusion.2), channel_id=1, source_target_pairs={{0,144},{1,145},{2,146},{3,147},{4,148},{5,149},{6,150},{7,151},{8... | collective-permute-start | bytes 147464 | tf_op jit(solution)/shard_map/sums/ppermute | solution.py:27
  480.8 7.0 %collective-permute-start.40 = (f32[96,128]{1,0:T(8,128)S(1)}, f32[96,128]{1,0:T(8,128)S(1)}, u32[]{:S(2)}, u32[]{:S(2)}) collective-permute-start(f32[96,128]{1,0:T(8,128)S(1)} %add_add_fusion.2), channel_id=1, source_target_pairs={{0,128},{1,129},{2,130},{3,131},{4,132},{5,133},{6,134},{7,135},{8... | collective-permute-start | bytes 147464 | tf_op jit(solution)/shard_map/sums/ppermute | solution.py:27
  483.2 4.5 collective-permute-start.39
  487.8 3.8 collective-permute-start.42
  487.9 4.5 collective-permute-start.43
  490.2 4.8 collective-permute-start.44
  495.0 6.0 %collective-permute-start.45 = (f32[384,128]{1,0:T(8,128)S(1)}, f32[384,128]{1,0:T(8,128)S(1)}, u32[]{:S(2)}, u32[]{:S(2)}) collective-permute-start(f32[384,128]{1,0:T(8,128)S(1)} %constant_dynamic-update-slice_fusion.5), channel_id=1, source_target_pairs={{0,4},{1,5},{2,6},{3,7},{4,0},{5,1},{6,2},{7,3},{8,12},{9,13},{10,... | collective-permute-start | bytes 589832 | tf_op jit(solution)/shard_map/sums_back/ppermute | solution.py:27
  497.5 8.6 %collective-permute-start.46 = (f32[384,128]{1,0:T(8,128)S(1)}, f32[384,128]{1,0:T(8,128)S(1)}, u32[]{:S(2)}, u32[]{:S(2)}) collective-permute-start(f32[384,128]{1,0:T(8,128)S(1)} %constant_dynamic-update-slice_fusion.5), channel_id=1, source_target_pairs={{0,8},{1,9},{2,10},{3,11},{4,12},{5,13},{6,14},{7,15},{8,0},{9,1},... | collective-permute-start | bytes 589832 | tf_op jit(solution)/shard_map/sums_back/ppermute | solution.py:27
  500.7 10.1 %collective-permute-start.47 = (f32[384,128]{1,0:T(8,128)S(1)}, f32[384,128]{1,0:T(8,128)S(1)}, u32[]{:S(2)}, u32[]{:S(2)}) collective-permute-start(f32[384,128]{1,0:T(8,128)S(1)} %constant_dynamic-update-slice_fusion.5), channel_id=1, source_target_pairs={{0,12},{1,13},{2,14},{3,15},{4,8},{5,9},{6,10},{7,11},{8,4},{9,5},... | collective-permute-start | bytes 589832 | tf_op jit(solution)/shard_map/sums_back/ppermute | solution.py:27
  (6 other events, 11.2 us)

commit v3 on v2

--- a/solution.py
+++ b/solution.py
@@ -32,7 +32,7 @@
     return list(lax.optimization_barrier((*pieces, *behind))[: len(masks)])
 
 
-def deliver(name, pieces, me, masks, axis, seen=None):
+def deliver(name, pieces, me, masks, axis):
     size = pieces[0].shape[axis]
     shape = list(pieces[0].shape)
     shape[axis] = size * len(masks)
@@ -40,8 +40,6 @@
     for step, mask in enumerate(masks):
         with jax.named_scope(name):
             arrived = swap(pieces[step], mask)
-        if seen is not None:
-            seen.append(arrived)
         out = lax.dynamic_update_slice_in_dim(out, arrived, jnp.bitwise_xor(me, step) * size, axis)
     return out
 
@@ -183,7 +181,7 @@
     twiddle_parts = jnp.broadcast_to(twiddle_parts, (SEQ,) + twiddle_parts.shape)
     right = gather("right_z", right, z_lo, Z_LO, 2)
     grad_rows = deliver("grad_z", grad_pieces, z_lo, Z_LO, 0)
-    pre_send = after(hidden_pre.reshape(GROUP, quarter, hidden), grad_rows)
+    pre_send = after(hidden_pre.reshape(GROUP, quarter, hidden), grad_rows, right)
     pre_values = group_exchange("hidden_pre_z", pre_send)
     pre_values = pre_values.transpose(1, 0, 2).reshape(quarter, 4 * hidden)
     pre_values = lax.optimization_barrier(pre_values)
@@ -221,15 +219,14 @@
             .reshape(SEQ, mine * outer_here, inner_len)
         )
 
-    def blocks_to_cols(value, line):
+    def blocks_to_cols(value):
         by_line = value.reshape(GROUP, 2, width // 2, quarter).transpose(1, 0, 2, 3)
         by_line = line_exchange("cols_z", by_line.reshape(8, width // 2, quarter))
-        by_line, line = lax.optimization_barrier((by_line, line))
         by_line = by_line.reshape(2, GROUP, 8, mine, outer_here // GROUP, inner_len)
         by_line = by_line.transpose(2, 3, 0, 1, 4, 5).reshape(8, mine * 2 * outer_here, inner_len)
         by_plane = plane_exchange("cols_plane", by_line)
         by_plane = by_plane.reshape(8, mine, 2, outer_here, inner_len).transpose(1, 2, 0, 3, 4)
-        return by_plane.reshape(mine, outer_len, inner_len), line
+        return by_plane.reshape(mine, outer_len, inner_len)
 
     def mixed_send(value):
         by_plane = value.reshape(mine, 2, 8, outer_here, inner_len).transpose(2, 0, 1, 3, 4)
@@ -276,18 +273,14 @@
     right_pieces = pieces_for(
         lambda other: lax.dynamic_index_in_dim(right_mix, other, 0, keepdims=False), y, Y
     )
-    seen = []
-    right_grad = deliver("right_y", right_pieces, y, Y, 0, seen)
-    mixed_rows = mixed_arrive(after(mixed_plane, seen[1]))
+    right_grad = deliver("right_y", right_pieces, y, Y, 0)
     partial_value = jnp.einsum("pq,tq->pt", right[1], right_grad, preferred_element_type=F32)
     mix_grad = (grad_rows.astype(F32) + partial_value).astype(BF)
+
+    mix_grad = blocks_to_cols(mix_grad)
+    mixed_rows = mixed_arrive(after(mixed_plane, mix_grad))
     up_terms = jnp.einsum("pt,tq->pq", mixed_rows, right_grad, preferred_element_type=F32)
-    weight_pair = weight_core(jnp.stack([down_terms, up_terms]), core)
-
-    mix_grad, weight_sums = blocks_to_cols(mix_grad, weight_line(weight_pair, x))
-    weight_sums = weight_z(weight_sums, z_lo)
-    mix_grad, weight_sums = lax.optimization_barrier((mix_grad, weight_sums))
-    weight_sums = weight_z_hi(weight_sums, z_hi)
+    weight_sums = weight_core(jnp.stack([down_terms, up_terms]), core)
     mix_grad = mix_grad.astype(F32)
     conv_f = convolved.astype(F32)
     grad_layer = mix_grad * layer_cols
@@ -317,14 +310,18 @@
     sums = jnp.concatenate(tiles + [outer_terms, scales.reshape(scale_rows, side)], axis=0)
     whole_rows = -(-sums.shape[0] // 512) * 512
     sums = jnp.pad(sums, ((0, whole_rows - sums.shape[0]), (0, 0)))
-    sums, weight_sums = lax.optimization_barrier((sums, weight_sums))
     for me, masks in ((y, Y), (z_lo, Z_LO)):
         sums = sum_spread_f32("sums", lambda other, sums=sums: part_of(sums, other, 4, 0), me, masks)
     sums = sum_spread_f32("sums", lambda other, sums=sums: sums, x, X)
-    sums, grad_input = lax.optimization_barrier((sums, grad_input))
+    sums, weight_sums = lax.optimization_barrier((sums, weight_sums))
+    weight_sums = weight_line(weight_sums, x)
     sums = sum_spread_f32("sums", lambda other, sums=sums: sums, x, join(Z_HI, CORE))
-    for me, masks in ((z_lo, Z_LO), (y, Y)):
-        sums = gather("sums_back", sums, me, masks, 0)
+    sums, weight_sums, grad_input = lax.optimization_barrier((sums, weight_sums, grad_input))
+    weight_sums = weight_z(weight_sums, z_lo)
+    sums = gather("sums_back", sums, z_lo, Z_LO, 0)
+    sums, weight_sums = lax.optimization_barrier((sums, weight_sums))
+    weight_sums = weight_z_hi(weight_sums, z_hi)
+    sums = gather("sums_back", sums, y, Y, 0)
     blank = jnp.zeros((side, side), F32)
     rows, taken = [], 0
     for i in range(count):

time: 523 us -> 530 us (1.013)
  the two profiles are of different devices: /device:TPU:1 before, /device:TPU:32 now
where the time goes in v3:
time: 530 us; the launch traced here: 521 us
  waiting for transfers between devices  298 us (56%)
  starting transfers between devices  120 us (23%)
  local copies, waits for them, and re-layouts  48.3 us (9%)
  matrix products  34.1 us (6%)
  other arithmetic  17.8 us (3%)
    ppermute x48, waiting for transfers between devices, swap(): return lax.ppermute(value, ('seq', 'chan'), route)  171 us
    ppermute x48, starting transfers between devices, swap(): return lax.ppermute(value, ('seq', 'chan'), route)  79.3 us
    all_to_all x2, waiting for transfers between devices, line_exchange(): lax.all_to_all(value, ('seq', 'chan'), split_axis=0, concat_axis=0, axis_...  47.3 us
    all_to_all x2, waiting for transfers between devices, seq_exchange(): return lax.all_to_all(value, 'seq', split_axis=0, concat_axis=0, tiled=True)  38 us
    all_to_all x2, waiting for transfers between devices, plane_exchange(): lax.all_to_all(value, 'seq', split_axis=0, concat_axis=0, axis_index_grou...  34 us
    all_to_all x2, starting transfers between devices, line_exchange(): lax.all_to_all(value, ('seq', 'chan'), split_axis=0, concat_axis=0, axis_...  19.9 us
  transfers between devices with their start and end apart: 55, of which 36 were waited for; matrix products, arithmetic and copies ran while one was open for 9% of the time, Pallas kernels for 0%

profile of v3, /device:TPU:32, one launch (start us, length us, event | category | flops | bytes accessed | tf_op | source)
XLA Modules:
  0.0 520.8 jit_solution(5223001152122667791)
XLA Ops:
  8.5 2.4 collective-permute-start
  14.1 2.2 collective-permute-done.4
  17.3 2.6 collective-permute-done.5
  20.8 3.8 collective-permute-done
  24.7 15.3 %collective-permute-done.1 = bf16[160,1024]{1,0:T(8,128)(2,1)S(1)} collective-permute-done((bf16[160,1024]{1,0:T(8,128)(2,1)}, bf16[160,1024]{1,0:T(8,128)(2,1)S(1)}, u32[]{:S(2)}, u32[]{:S(2)}) %collective-permute-start.1) | collective-permute-done | bytes 327712 | tf_op jit(solution)/shard_map/grad_z/ppermute | solution.py:27
  40.1 6.7 %collective-permute-done.2 = bf16[160,1024]{1,0:T(8,128)(2,1)S(1)} collective-permute-done((bf16[160,1024]{1,0:T(8,128)(2,1)S(1)}, bf16[160,1024]{1,0:T(8,128)(2,1)S(1)}, u32[]{:S(2)}, u32[]{:S(2)}) %collective-permute-start.2) | collective-permute-done | bytes 327712 | tf_op jit(solution)/shard_map/grad_z/ppermute | solution.py:27
  47.9 4.2 all-to-all-start
  53.8 2.8 collective-permute-start.7
  59.2 2.9 collective-permute-start.11
  62.1 4.5 collective-permute-done.6
  66.6 3.0 collective-permute-start.12
  69.7 7.3 %collective-permute-done.7 = bf16[2,80,1536]{2,1,0:T(8,128)(2,1)S(1)} collective-permute-done((bf16[2,80,1536]{2,1,0:T(8,128)(2,1)}, bf16[2,80,1536]{2,1,0:T(8,128)(2,1)S(1)}, u32[]{:S(2)}, u32[]{:S(2)}) %collective-permute-start.7) | collective-permute-done | bytes 491552 | tf_op jit(solution)/shard_map/right_x/ppermute | solution.py:27
  77.0 2.7 collective-permute-done.8
  84.2 2.9 collective-permute-start.14
  87.1 2.2 broadcast_in_dim.78
  94.2 8.2 %collective-permute-done.14 = bf16[640,256]{1,0:T(8,128)(2,1)S(1)} collective-permute-done((bf16[640,256]{1,0:T(8,128)(2,1)S(1)}, bf16[640,256]{1,0:T(8,128)(2,1)S(1)}, u32[]{:S(2)}, u32[]{:S(2)}) %collective-permute-start.14) | collective-permute-done | bytes 327712 | tf_op jit(solution)/shard_map/down_y/ppermute | solution.py:27
  103.1 5.7 %collective-permute-done.15 = bf16[640,256]{1,0:T(8,128)(2,1)S(1)} collective-permute-done((bf16[640,256]{1,0:T(8,128)(2,1)S(1)}, bf16[640,256]{1,0:T(8,128)(2,1)S(1)}, u32[]{:S(2)}, u32[]{:S(2)}) %collective-permute-start.15) | collective-permute-done | bytes 327712 | tf_op jit(solution)/shard_map/down_y/ppermute | solution.py:27
  111.1 7.6 %all-to-all-done = bf16[4,1024,384]{2,1,0:T(8,128)(2,1)S(1)} async-done(((bf16[4,1024,384]{2,1,0:T(8,128)(2,1)}), bf16[4,1024,384]{2,1,0:T(8,128)(2,1)S(1)}, u32[]{:S(2)}, u32[]{:S(2)}) %all-to-all-start) | async-done | bytes 3145760 | tf_op jit(solution)/shard_map/hidden_pre_z/all_to_all | solution.py:95
  119.0 9.2 %fusion.3 = bf16[1024,1536]{1,0:T(8,128)(2,1)S(1)} fusion(bf16[1024,1536]{1,0:T(8,128)(2,1)S(1)} %bitcast.235, bf16[640,1024]{1,0:T(8,128)(2,1)} %constant_dynamic-update-slice_fusion.17, bf16[2,640,1536]{2,1,0:T(8,128)(2,1)} %constant_dynamic-update-slice_fusion.24), kind=kOutput, calls=%fused_computation.12 | convolution fusion | flops 2046296064 | bytes 9568256 | tf_op jit(solution)/shard_map/pt,pq->tq/dot_general | solution.py:258
  130.0 2.9 collective-permute-start.17
  133.9 15.1 %collective-permute-done.16 = bf16[1,256,1536]{2,1,0:T(8,128)(2,1)S(1)} collective-permute-done((bf16[1,256,1536]{2,1,0:T(8,128)(2,1)S(1)}, bf16[1,256,1536]{2,1,0:T(8,128)(2,1)S(1)}, u32[]{:S(2)}, u32[]{:S(2)}) %collective-permute-start.16) | collective-permute-done | bytes 786464 | tf_op jit(solution)/shard_map/pre_y/ppermute | solution.py:27
  149.1 16.0 %collective-permute-done.17 = bf16[1,256,1536]{2,1,0:T(8,128)(2,1)S(1)} collective-permute-done((bf16[1,256,1536]{2,1,0:T(8,128)(2,1)S(1)}, bf16[1,256,1536]{2,1,0:T(8,128)(2,1)S(1)}, u32[]{:S(2)}, u32[]{:S(2)}) %collective-permute-start.17) | collective-permute-done | bytes 786464 | tf_op jit(solution)/shard_map/pre_y/ppermute | solution.py:27
  165.2 2.6 collective-permute-done.18
  173.0 3.0 collective-permute-start.21
  176.3 15.4 %collective-permute-done.19 = bf16[256,1536]{1,0:T(8,128)(2,1)S(1)} collective-permute-done((bf16[256,1536]{1,0:T(8,128)(2,1)S(1)}, bf16[256,1536]{1,0:T(8,128)(2,1)S(1)}, u32[]{:S(2)}, u32[]{:S(2)}) %collective-permute-start.19) | collective-permute-done | bytes 786464 | tf_op jit(solution)/shard_map/right_y/ppermute | solution.py:27
  191.7 10.0 %collective-permute-done.20 = bf16[256,1536]{1,0:T(8,128)(2,1)S(1)} collective-permute-done((bf16[256,1536]{1,0:T(8,128)(2,1)S(1)}, bf16[256,1536]{1,0:T(8,128)(2,1)S(1)}, u32[]{:S(2)}, u32[]{:S(2)}) %collective-permute-start.20) | collective-permute-done | bytes 786464 | tf_op jit(solution)/shard_map/right_y/ppermute | solution.py:27
  201.8 2.7 collective-permute-done.21
  204.5 4.9 add_convert_fusion
  210.6 14.3 %all-to-all-start.1 = ((bf16[8,80,1024]{2,1,0:T(8,128)(2,1)}), bf16[8,80,1024]{2,1,0:T(8,128)(2,1)S(1)}, u32[]{:S(2)}, u32[]{:S(2)}) async-start(bf16[8,80,1024]{2,1,0:T(8,128)(2,1)} %bitcast.29), calls=%async_computation.1 | async-start | bytes 2621440 | tf_op jit(solution)/shard_map/cols_z/all_to_all | solution.py:107
  224.9 2.4 reshape.356
  228.7 23.3 %all-to-all-done.1 = bf16[8,80,1024]{2,1,0:T(8,128)(2,1)S(1)} async-done(((bf16[8,80,1024]{2,1,0:T(8,128)(2,1)}), bf16[8,80,1024]{2,1,0:T(8,128)(2,1)S(1)}, u32[]{:S(2)}, u32[]{:S(2)}) %all-to-all-start.1) | async-done | bytes 1310752 | tf_op jit(solution)/shard_map/cols_z/all_to_all | solution.py:107
  252.0 4.9 all-to-all-start.3
  261.8 38.0 %all-to-all-done.3 = bf16[16,96,512]{2,1,0:T(8,128)(2,1)S(1)} async-done(((bf16[16,96,512]{2,1,0:T(8,128)(2,1)}), bf16[16,96,512]{2,1,0:T(8,128)(2,1)S(1)}, u32[]{:S(2)}, u32[]{:S(2)}) %all-to-all-start.3) | async-done | bytes 1572896 | tf_op jit(solution)/shard_map/layer_seq/all_to_all | solution.py:81
  299.8 3.6 all-to-all-start.2
  303.7 3.1 multiply_convert_fusion
  306.8 15.3 %all-to-all-done.2 = bf16[8,160,512]{2,1,0:T(8,128)(2,1)S(1)} async-done(((bf16[8,160,512]{2,1,0:T(8,128)(2,1)}), bf16[8,160,512]{2,1,0:T(8,128)(2,1)S(1)}, u32[]{:S(2)}, u32[]{:S(2)}) %all-to-all-start.2) | async-done | bytes 1310752 | tf_op jit(solution)/shard_map/cols_plane/all_to_all | solution.py:87
  325.9 3.0 fusion.20
  330.2 4.3 all-to-all-start.4
  334.5 18.7 %all-to-all-done.4 = bf16[8,160,512]{2,1,0:T(8,128)(2,1)} async-done(((bf16[8,160,512]{2,1,0:T(8,128)(2,1)}), bf16[8,160,512]{2,1,0:T(8,128)(2,1)}, u32[]{:S(2)}, u32[]{:S(2)}) %all-to-all-start.4) | async-done | bytes 1310752 | tf_op jit(solution)/shard_map/blocks_plane/all_to_all | solution.py:87
  353.2 3.8 reshape.361
  357.0 3.1 copy.66
  360.1 5.6 %all-to-all-start.5 = ((bf16[8,80,1024]{2,1,0:T(8,128)(2,1)}), bf16[8,80,1024]{2,1,0:T(8,128)(2,1)}, u32[]{:S(2)}, u32[]{:S(2)}) async-start(bf16[8,80,1024]{2,1,0:T(8,128)(2,1)} %bitcast.231), calls=%async_computation.5 | async-start | bytes 2621440 | tf_op jit(solution)/shard_map/blocks_z/all_to_all | solution.py:107
  365.7 6.8 %fusion.16 = f32[640,1536]{1,0:T(8,128)} fusion(bf16[640,1024]{1,0:T(8,128)(2,1)} %constant_dynamic-update-slice_fusion.17, bf16[1024,1536]{1,0:T(8,128)(2,1)} %bitcast.236), kind=kOutput, calls=%fused_computation.29 | convolution fusion | flops 2028994560 | bytes 8388608 | tf_op jit(solution)/shard_map/pt,tq->pq/dot_general | solution.py:262
  374.4 24.0 %all-to-all-done.5 = bf16[8,80,1024]{2,1,0:T(8,128)(2,1)} async-done(((bf16[8,80,1024]{2,1,0:T(8,128)(2,1)}), bf16[8,80,1024]{2,1,0:T(8,128)(2,1)}, u32[]{:S(2)}, u32[]{:S(2)}) %all-to-all-start.5) | async-done | bytes 1310752 | tf_op jit(solution)/shard_map/blocks_z/all_to_all | solution.py:107
  399.9 4.3 convolution_bitcast_fusion
  408.5 4.3 collective-permute-start.23
  413.2 3.0 collective-permute-done.22
  416.2 6.2 %collective-permute-done.23 = f32[384,128]{1,0:T(8,128)S(1)} collective-permute-done((f32[384,128]{1,0:T(8,128)S(1)}, f32[384,128]{1,0:T(8,128)S(1)}, u32[]{:S(2)}, u32[]{:S(2)}) %collective-permute-start.23) | collective-permute-done | bytes 196640 | tf_op jit(solution)/shard_map/sums/ppermute | solution.py:27
  422.4 2.6 collective-permute-done.24
  429.3 2.5 collective-permute-done.26
  433.0 2.0 collective-permute-start.29
  435.0 2.1 collective-permute-start.30
  438.3 4.0 all-to-all-start.6
  442.4 3.3 fusion.14
  450.6 2.7 collective-permute-start.36
  453.2 5.9 %collective-permute-start.33 = (f32[96,128]{1,0:T(8,128)S(1)}, f32[96,128]{1,0:T(8,128)S(1)}, u32[]{:S(2)}, u32[]{:S(2)}) collective-permute-start(f32[96,128]{1,0:T(8,128)S(1)} %add_add_fusion.1), channel_id=1, source_target_pairs={{0,128},{1,129},{2,130},{3,131},{4,132},{5,133},{6,134},{7,135},{8... | collective-permute-start | bytes 147464 | tf_op jit(solution)/shard_map/sums/ppermute | solution.py:27
  460.2 17.4 %collective-permute-done.33 = f32[96,128]{1,0:T(8,128)S(1)} collective-permute-done((f32[96,128]{1,0:T(8,128)S(1)}, f32[96,128]{1,0:T(8,128)S(1)}, u32[]{:S(2)}, u32[]{:S(2)}) %collective-permute-start.33) | collective-permute-done | bytes 49184 | tf_op jit(solution)/shard_map/sums/ppermute | solution.py:27
  477.7 4.5 collective-permute-done.36
  488.4 2.3 collective-permute-start.41
  495.3 5.2 collective-permute-done.42
  500.5 2.7 collective-permute-done.43
  505.2 2.8 collective-permute-start.47
  508.1 5.7 %collective-permute-start.44 = (bf16[2,40,384]{2,1,0:T(8,128)(2,1)S(1)}, bf16[2,40,384]{2,1,0:T(8,128)(2,1)S(1)}, u32[]{:S(2)}, u32[]{:S(2)}) collective-permute-start(bf16[2,40,384]{2,1,0:T(8,128)(2,1)S(1)} %fusion.55), channel_id=1, source_target_pairs={{0,128},{1,129},{2,130},{3,131},{4,132},{5,133},{6,134},{7,135},{8... | collective-permute-start | bytes 184328 | tf_op jit(solution)/shard_map/weight_z_hi/ppermute | solution.py:27
  513.8 3.2 collective-permute-done.44
  (230 shorter events, 88.8 us)
Async XLA Ops:
  0.6 6.9 %copy-start.15 = (bf16[4096,160]{0,1:T(8,128)(2,1)S(1)}, bf16[4096,160]{0,1:T(8,128)(2,1)}, u32[]{:S(2)}) copy-start(bf16[4096,160]{0,1:T(8,128)(2,1)} %param.18) | copy-start | bytes 3932164
  3.6 8.9 %collective-permute-start.3 = (bf16[2,80,384]{2,1,0:T(8,128)(2,1)}, bf16[2,80,384]{2,1,0:T(8,128)(2,1)}, u32[]{:S(2)}, u32[]{:S(2)}) collective-permute-start(bf16[2,80,384]{2,1,0:T(8,128)(2,1)} %get-tuple-element.102), channel_id=1, source_target_pairs={{0,1},{1,0},{2,3},{3,2},{4,5},{5,4},{6,7},{7,6},{8,9},{9,8},{10,11... | collective-permute-start | bytes 368648 | tf_op jit(solution)/shard_map/right_z/ppermute | solution.py:27
  5.5 10.9 %collective-permute-start.4 = (bf16[2,80,384]{2,1,0:T(8,128)(2,1)}, bf16[2,80,384]{2,1,0:T(8,128)(2,1)}, u32[]{:S(2)}, u32[]{:S(2)}) collective-permute-start(bf16[2,80,384]{2,1,0:T(8,128)(2,1)} %get-tuple-element.102), channel_id=1, source_target_pairs={{0,2},{1,3},{2,0},{3,1},{4,6},{5,7},{6,4},{7,5},{8,10},{9,11},{10,... | collective-permute-start | bytes 368648 | tf_op jit(solution)/shard_map/right_z/ppermute | solution.py:27
  7.0 12.9 %collective-permute-start.5 = (bf16[2,80,384]{2,1,0:T(8,128)(2,1)}, bf16[2,80,384]{2,1,0:T(8,128)(2,1)}, u32[]{:S(2)}, u32[]{:S(2)}) collective-permute-start(bf16[2,80,384]{2,1,0:T(8,128)(2,1)} %get-tuple-element.102), channel_id=1, source_target_pairs={{0,3},{1,2},{2,1},{3,0},{4,7},{5,6},{6,5},{7,4},{8,11},{9,10},{10,... | collective-permute-start | bytes 368648 | tf_op jit(solution)/shard_map/right_z/ppermute | solution.py:27
  8.5 16.2 %collective-permute-start = (bf16[160,1024]{1,0:T(8,128)(2,1)}, bf16[160,1024]{1,0:T(8,128)(2,1)S(1)}, u32[]{:S(2)}, u32[]{:S(2)}) collective-permute-start(bf16[160,1024]{1,0:T(8,128)(2,1)} %get-tuple-element.38), channel_id=1, source_target_pairs={{0,1},{1,0},{2,3},{3,2},{4,5},{5,4},{6,7},{7,6},{8,9},{9,8},{10,11... | collective-permute-start | bytes 983048 | tf_op jit(solution)/shard_map/grad_z/ppermute | solution.py:27
  10.8 29.2 %collective-permute-start.1 = (bf16[160,1024]{1,0:T(8,128)(2,1)}, bf16[160,1024]{1,0:T(8,128)(2,1)S(1)}, u32[]{:S(2)}, u32[]{:S(2)}) collective-permute-start(bf16[160,1024]{1,0:T(8,128)(2,1)} %get-tuple-element.39), channel_id=1, source_target_pairs={{0,2},{1,3},{2,0},{3,1},{4,6},{5,7},{6,4},{7,5},{8,10},{9,11},{10,... | collective-permute-start | bytes 983048 | tf_op jit(solution)/shard_map/grad_z/ppermute | solution.py:27
  12.5 34.3 %collective-permute-start.2 = (bf16[160,1024]{1,0:T(8,128)(2,1)S(1)}, bf16[160,1024]{1,0:T(8,128)(2,1)S(1)}, u32[]{:S(2)}, u32[]{:S(2)}) collective-permute-start(bf16[160,1024]{1,0:T(8,128)(2,1)S(1)} %copy-done.18), channel_id=1, source_target_pairs={{0,3},{1,2},{2,1},{3,0},{4,7},{5,6},{6,5},{7,4},{8,11},{9,10},{10,... | collective-permute-start | bytes 983048 | tf_op jit(solution)/shard_map/grad_z/ppermute | solution.py:27
  20.8 26.0 %copy-start.10 = (bf16[2,80,1536]{2,1,0:T(8,128)(2,1)}, bf16[2,80,1536]{2,1,0:T(8,128)(2,1)S(1)}, u32[]{:S(2)}) copy-start(bf16[2,80,1536]{2,1,0:T(8,128)(2,1)S(1)} %constant_dynamic-update-slice_fusion.30) | copy-start | bytes 1474564
  46.8 5.2 %copy-start.21 = (bf16[4,4,640]{2,1,0:T(4,128)(2,1)S(1)}, bf16[4,4,640]{2,1,0:T(4,128)(2,1)}, u32[]{:S(2)}) copy-start(bf16[4,4,640]{2,1,0:T(4,128)(2,1)} %param.23) | copy-start | bytes 61444
  47.9 70.8 %all-to-all-start = ((bf16[4,1024,384]{2,1,0:T(8,128)(2,1)}), bf16[4,1024,384]{2,1,0:T(8,128)(2,1)S(1)}, u32[]{:S(2)}, u32[]{:S(2)}) async-start(bf16[4,1024,384]{2,1,0:T(8,128)(2,1)} %bitcast.234), calls=%async_computation | async-start | bytes 6291456 | tf_op jit(solution)/shard_map/hidden_pre_z/all_to_all | solution.py:95
  52.2 14.5 %collective-permute-start.6 = (bf16[2,80,1536]{2,1,0:T(8,128)(2,1)}, bf16[2,80,1536]{2,1,0:T(8,128)(2,1)S(1)}, u32[]{:S(2)}, u32[]{:S(2)}) collective-permute-start(bf16[2,80,1536]{2,1,0:T(8,128)(2,1)} %copy-done.10), channel_id=1, source_target_pairs={{0,32},{1,33},{2,34},{3,35},{4,36},{5,37},{6,38},{7,39},{8,40},{9,... | collective-permute-start | bytes 1474568 | tf_op jit(solution)/shard_map/right_x/ppermute | solution.py:27
  53.8 23.1 %collective-permute-start.7 = (bf16[2,80,1536]{2,1,0:T(8,128)(2,1)}, bf16[2,80,1536]{2,1,0:T(8,128)(2,1)S(1)}, u32[]{:S(2)}, u32[]{:S(2)}) collective-permute-start(bf16[2,80,1536]{2,1,0:T(8,128)(2,1)} %copy-done.10), channel_id=1, source_target_pairs={{0,64},{1,65},{2,66},{3,67},{4,68},{5,69},{6,70},{7,71},{8,72},{9,... | collective-permute-start | bytes 1474568 | tf_op jit(solution)/shard_map/right_x/ppermute | solution.py:27
  56.7 23.1 %collective-permute-start.8 = (bf16[2,80,1536]{2,1,0:T(8,128)(2,1)}, bf16[2,80,1536]{2,1,0:T(8,128)(2,1)S(1)}, u32[]{:S(2)}, u32[]{:S(2)}) collective-permute-start(bf16[2,80,1536]{2,1,0:T(8,128)(2,1)} %copy-done.10), channel_id=1, source_target_pairs={{0,96},{1,97},{2,98},{3,99},{4,100},{5,101},{6,102},{7,103},{8,104... | collective-permute-start | bytes 1474568 | tf_op jit(solution)/shard_map/right_x/ppermute | solution.py:27
  57.5 22.5 %collective-permute-start.10 = (bf16[1,640,256]{2,1,0:T(8,128)(2,1)S(1)}, bf16[1,640,256]{2,1,0:T(8,128)(2,1)S(1)}, u32[]{:S(2)}, u32[]{:S(2)}) collective-permute-start(bf16[1,640,256]{2,1,0:T(8,128)(2,1)S(1)} %bitcast.245), channel_id=1, source_target_pairs={{0,4},{1,5},{2,6},{3,7},{4,0},{5,1},{6,2},{7,3},{8,12},{9,13},{10,... | collective-permute-start | bytes 983048 | tf_op jit(solution)/shard_map/grad_y/ppermute | solution.py:27
  59.2 20.9 %collective-permute-start.11 = (bf16[1,640,256]{2,1,0:T(8,128)(2,1)S(1)}, bf16[1,640,256]{2,1,0:T(8,128)(2,1)S(1)}, u32[]{:S(2)}, u32[]{:S(2)}) collective-permute-start(bf16[1,640,256]{2,1,0:T(8,128)(2,1)S(1)} %bitcast.244), channel_id=1, source_target_pairs={{0,8},{1,9},{2,10},{3,11},{4,12},{5,13},{6,14},{7,15},{8,0},{9,1},... | collective-permute-start | bytes 983048 | tf_op jit(solution)/shard_map/grad_y/ppermute | solution.py:27
  66.6 13.5 %collective-permute-start.12 = (bf16[1,640,256]{2,1,0:T(8,128)(2,1)S(1)}, bf16[1,640,256]{2,1,0:T(8,128)(2,1)S(1)}, u32[]{:S(2)}, u32[]{:S(2)}) collective-permute-start(bf16[1,640,256]{2,1,0:T(8,128)(2,1)S(1)} %bitcast.243), channel_id=1, source_target_pairs={{0,12},{1,13},{2,14},{3,15},{4,8},{5,9},{6,10},{7,11},{8,4},{9,5},... | collective-permute-start | bytes 983048 | tf_op jit(solution)/shard_map/grad_y/ppermute | solution.py:27
  79.8 29.9 %collective-permute-start.9 = (bf16[2,320,1536]{2,1,0:T(8,128)(2,1)S(1)}, bf16[2,320,1536]{2,1,0:T(8,128)(2,1)S(1)}, u32[]{:S(2)}, u32[]{:S(2)}) collective-permute-start(bf16[2,320,1536]{2,1,0:T(8,128)(2,1)S(1)} %constant_dynamic-update-slice_fusion.26), channel_id=1, source_target_pairs={{0,16},{1,17},{2,18},{3,19},{4,20},{5,21},{6,22},{7,23},{8,24},{9,... | collective-permute-start | bytes 5898248 | tf_op jit(solution)/shard_map/right_core/ppermute | solution.py:27
  82.6 10.8 %collective-permute-start.13 = (bf16[640,256]{1,0:T(8,128)(2,1)S(1)}, bf16[640,256]{1,0:T(8,128)(2,1)S(1)}, u32[]{:S(2)}, u32[]{:S(2)}) collective-permute-start(bf16[640,256]{1,0:T(8,128)(2,1)S(1)} %get-tuple-element.46), channel_id=1, source_target_pairs={{0,4},{1,5},{2,6},{3,7},{4,0},{5,1},{6,2},{7,3},{8,12},{9,13},{10,... | collective-permute-start | bytes 983048 | tf_op jit(solution)/shard_map/down_y/ppermute | solution.py:27
  84.2 18.1 %collective-permute-start.14 = (bf16[640,256]{1,0:T(8,128)(2,1)S(1)}, bf16[640,256]{1,0:T(8,128)(2,1)S(1)}, u32[]{:S(2)}, u32[]{:S(2)}) collective-permute-start(bf16[640,256]{1,0:T(8,128)(2,1)S(1)} %get-tuple-element.47), channel_id=1, source_target_pairs={{0,8},{1,9},{2,10},{3,11},{4,12},{5,13},{6,14},{7,15},{8,0},{9,1},... | collective-permute-start | bytes 983048 | tf_op jit(solution)/shard_map/down_y/ppermute | solution.py:27
  90.7 18.2 %collective-permute-start.15 = (bf16[640,256]{1,0:T(8,128)(2,1)S(1)}, bf16[640,256]{1,0:T(8,128)(2,1)S(1)}, u32[]{:S(2)}, u32[]{:S(2)}) collective-permute-start(bf16[640,256]{1,0:T(8,128)(2,1)S(1)} %get-tuple-element.48), channel_id=1, source_target_pairs={{0,12},{1,13},{2,14},{3,15},{4,8},{5,9},{6,10},{7,11},{8,4},{9,5},... | collective-permute-start | bytes 983048 | tf_op jit(solution)/shard_map/down_y/ppermute | solution.py:27
  119.0 9.2 %copy-start.8 = (bf16[4,128,8,384]{3,2,0,1:T(8,128)(2,1)}, bf16[4,128,8,384]{3,2,0,1:T(8,128)(2,1)S(1)}, u32[]{:S(2)}) copy-start(bf16[4,128,8,384]{3,2,0,1:T(8,128)(2,1)S(1)} %copy.79) | copy-start | bytes 9437188
  128.5 20.6 %collective-permute-start.16 = (bf16[1,256,1536]{2,1,0:T(8,128)(2,1)S(1)}, bf16[1,256,1536]{2,1,0:T(8,128)(2,1)S(1)}, u32[]{:S(2)}, u32[]{:S(2)}) collective-permute-start(bf16[1,256,1536]{2,1,0:T(8,128)(2,1)S(1)} %get-tuple-element.51), channel_id=1, source_target_pairs={{0,4},{1,5},{2,6},{3,7},{4,0},{5,1},{6,2},{7,3},{8,12},{9,13},{10,... | collective-permute-start | bytes 2359304 | tf_op jit(solution)/shard_map/pre_y/ppermute | solution.py:27
  130.0 35.1 %collective-permute-start.17 = (bf16[1,256,1536]{2,1,0:T(8,128)(2,1)S(1)}, bf16[1,256,1536]{2,1,0:T(8,128)(2,1)S(1)}, u32[]{:S(2)}, u32[]{:S(2)}) collective-permute-start(bf16[1,256,1536]{2,1,0:T(8,128)(2,1)S(1)} %get-tuple-element.52), channel_id=1, source_target_pairs={{0,8},{1,9},{2,10},{3,11},{4,12},{5,13},{6,14},{7,15},{8,0},{9,1},... | collective-permute-start | bytes 2359304 | tf_op jit(solution)/shard_map/pre_y/ppermute | solution.py:27
  133.0 34.8 %collective-permute-start.18 = (bf16[1,256,1536]{2,1,0:T(8,128)(2,1)S(1)}, bf16[1,256,1536]{2,1,0:T(8,128)(2,1)S(1)}, u32[]{:S(2)}, u32[]{:S(2)}) collective-permute-start(bf16[1,256,1536]{2,1,0:T(8,128)(2,1)S(1)} %get-tuple-element.53), channel_id=1, source_target_pairs={{0,12},{1,13},{2,14},{3,15},{4,8},{5,9},{6,10},{7,11},{8,4},{9,5},... | collective-permute-start | bytes 2359304 | tf_op jit(solution)/shard_map/pre_y/ppermute | solution.py:27
  171.1 20.6 %collective-permute-start.19 = (bf16[256,1536]{1,0:T(8,128)(2,1)S(1)}, bf16[256,1536]{1,0:T(8,128)(2,1)S(1)}, u32[]{:S(2)}, u32[]{:S(2)}) collective-permute-start(bf16[256,1536]{1,0:T(8,128)(2,1)S(1)} %get-tuple-element.55), channel_id=1, source_target_pairs={{0,4},{1,5},{2,6},{3,7},{4,0},{5,1},{6,2},{7,3},{8,12},{9,13},{10,... | collective-permute-start | bytes 2359304 | tf_op jit(solution)/shard_map/right_y/ppermute | solution.py:27
  171.2 30.5 %collective-permute-start.20 = (bf16[256,1536]{1,0:T(8,128)(2,1)S(1)}, bf16[256,1536]{1,0:T(8,128)(2,1)S(1)}, u32[]{:S(2)}, u32[]{:S(2)}) collective-permute-start(bf16[256,1536]{1,0:T(8,128)(2,1)S(1)} %get-tuple-element.56), channel_id=1, source_target_pairs={{0,8},{1,9},{2,10},{3,11},{4,12},{5,13},{6,14},{7,15},{8,0},{9,1},... | collective-permute-start | bytes 2359304 | tf_op jit(solution)/shard_map/right_y/ppermute | solution.py:27
  173.0 31.4 %collective-permute-start.21 = (bf16[256,1536]{1,0:T(8,128)(2,1)S(1)}, bf16[256,1536]{1,0:T(8,128)(2,1)S(1)}, u32[]{:S(2)}, u32[]{:S(2)}) collective-permute-start(bf16[256,1536]{1,0:T(8,128)(2,1)S(1)} %get-tuple-element.57), channel_id=1, source_target_pairs={{0,12},{1,13},{2,14},{3,15},{4,8},{5,9},{6,10},{7,11},{8,4},{9,5},... | collective-permute-start | bytes 2359304 | tf_op jit(solution)/shard_map/right_y/ppermute | solution.py:27
  191.7 12.8 %copy-start.5 = (bf16[640,1024]{1,0:T(8,128)(2,1)S(1)}, bf16[640,1024]{1,0:T(8,128)(2,1)}, u32[]{:S(2)}) copy-start(bf16[640,1024]{1,0:T(8,128)(2,1)} %copy-done.3) | copy-start | bytes 3932164
  210.6 41.4 %all-to-all-start.1 = ((bf16[8,80,1024]{2,1,0:T(8,128)(2,1)}), bf16[8,80,1024]{2,1,0:T(8,128)(2,1)S(1)}, u32[]{:S(2)}, u32[]{:S(2)}) async-start(bf16[8,80,1024]{2,1,0:T(8,128)(2,1)} %bitcast.29), calls=%async_computation.1 | async-start | bytes 2621440 | tf_op jit(solution)/shard_map/cols_z/all_to_all | solution.py:107
  252.0 47.7 %all-to-all-start.3 = ((bf16[16,96,512]{2,1,0:T(8,128)(2,1)}), bf16[16,96,512]{2,1,0:T(8,128)(2,1)S(1)}, u32[]{:S(2)}, u32[]{:S(2)}) async-start(bf16[16,96,512]{2,1,0:T(8,128)(2,1)} %pad_maximum_fusion.1), calls=%async_computation.3 | async-start | bytes 3145728 | tf_op jit(solution)/shard_map/layer_seq/all_to_all | solution.py:81
  261.8 41.6 %copy-start.23 = (f32[160]{0:T(256)S(1)}, f32[160]{0:T(256)}, u32[]{:S(2)}) copy-start(f32[160]{0:T(256)} %param.13) | copy-start | bytes 1924
  261.8 41.6 %copy-start.24 = (f32[160]{0:T(256)S(1)}, f32[160]{0:T(256)}, u32[]{:S(2)}) copy-start(f32[160]{0:T(256)} %param.14) | copy-start | bytes 1924
  299.8 22.3 %all-to-all-start.2 = ((bf16[8,160,512]{2,1,0:T(8,128)(2,1)}), bf16[8,160,512]{2,1,0:T(8,128)(2,1)S(1)}, u32[]{:S(2)}, u32[]{:S(2)}) async-start(bf16[8,160,512]{2,1,0:T(8,128)(2,1)} %copy.56), calls=%async_computation.2 | async-start | bytes 2621440 | tf_op jit(solution)/shard_map/cols_plane/all_to_all | solution.py:87
  330.2 23.0 %all-to-all-start.4 = ((bf16[8,160,512]{2,1,0:T(8,128)(2,1)}), bf16[8,160,512]{2,1,0:T(8,128)(2,1)}, u32[]{:S(2)}, u32[]{:S(2)}) async-start(bf16[8,160,512]{2,1,0:T(8,128)(2,1)} %bitcast.230), calls=%async_computation.4 | async-start | bytes 2621440 | tf_op jit(solution)/shard_map/blocks_plane/all_to_all | solution.py:87
  360.1 38.3 %all-to-all-start.5 = ((bf16[8,80,1024]{2,1,0:T(8,128)(2,1)}), bf16[8,80,1024]{2,1,0:T(8,128)(2,1)}, u32[]{:S(2)}, u32[]{:S(2)}) async-start(bf16[8,80,1024]{2,1,0:T(8,128)(2,1)} %bitcast.231), calls=%async_computation.5 | async-start | bytes 2621440 | tf_op jit(solution)/shard_map/blocks_z/all_to_all | solution.py:107
  365.7 6.8 %copy-start.7 = (bf16[10,128,512]{1,2,0:T(8,128)(2,1)S(1)}, bf16[10,128,512]{1,2,0:T(8,128)(2,1)}, u32[]{:S(2)}) copy-start(bf16[10,128,512]{1,2,0:T(8,128)(2,1)} %copy-done.6) | copy-start | bytes 3932164
  406.6 35.7 %collective-permute-start.31 = (bf16[2,8,40,1536]{3,2,1,0:T(8,128)(2,1)}, bf16[2,8,40,1536]{3,2,1,0:T(8,128)(2,1)}, u32[]{:S(2)}, u32[]{:S(2)}) collective-permute-start(bf16[2,8,40,1536]{3,2,1,0:T(8,128)(2,1)} %fusion.27), channel_id=1, source_target_pairs={{0,16},{1,17},{2,18},{3,19},{4,20},{5,21},{6,22},{7,23},{8,24},{9,... | collective-permute-start | bytes 5898248 | tf_op jit(solution)/shard_map/weight_core/ppermute | solution.py:27
  408.3 28.8 %copy-start.12 = (bf16[10,16,8,512]{3,2,1,0:T(8,128)(2,1)S(1)}, bf16[10,16,8,512]{3,2,1,0:T(8,128)(2,1)}, u32[]{:S(2)}) copy-start(bf16[10,16,8,512]{3,2,1,0:T(8,128)(2,1)} %get-tuple-element.109) | copy-start | bytes 3932164
  408.4 7.8 %collective-permute-start.22 = (f32[384,128]{1,0:T(8,128)S(1)}, f32[384,128]{1,0:T(8,128)S(1)}, u32[]{:S(2)}, u32[]{:S(2)}) collective-permute-start(f32[384,128]{1,0:T(8,128)S(1)} %get-tuple-element.152), channel_id=1, source_target_pairs={{0,4},{1,5},{2,6},{3,7},{4,0},{5,1},{6,2},{7,3},{8,12},{9,13},{10,... | collective-permute-start | bytes 589832 | tf_op jit(solution)/shard_map/sums/ppermute | solution.py:27
  408.5 13.9 %collective-permute-start.23 = (f32[384,128]{1,0:T(8,128)S(1)}, f32[384,128]{1,0:T(8,128)S(1)}, u32[]{:S(2)}, u32[]{:S(2)}) collective-permute-start(f32[384,128]{1,0:T(8,128)S(1)} %get-tuple-element.153), channel_id=1, source_target_pairs={{0,8},{1,9},{2,10},{3,11},{4,12},{5,13},{6,14},{7,15},{8,0},{9,1},... | collective-permute-start | bytes 589832 | tf_op jit(solution)/shard_map/sums/ppermute | solution.py:27
  412.8 12.2 %collective-permute-start.24 = (f32[384,128]{1,0:T(8,128)S(1)}, f32[384,128]{1,0:T(8,128)S(1)}, u32[]{:S(2)}, u32[]{:S(2)}) collective-permute-start(f32[384,128]{1,0:T(8,128)S(1)} %get-tuple-element.154), channel_id=1, source_target_pairs={{0,12},{1,13},{2,14},{3,15},{4,8},{5,9},{6,10},{7,11},{8,4},{9,5},... | collective-permute-start | bytes 589832 | tf_op jit(solution)/shard_map/sums/ppermute | solution.py:27
  425.1 4.2 collective-permute-start.25
  426.6 5.1 collective-permute-start.26
  426.9 5.4 %collective-permute-start.27 = (f32[96,128]{1,0:T(8,128)S(1)}, f32[96,128]{1,0:T(8,128)S(1)}, u32[]{:S(2)}, u32[]{:S(2)}) collective-permute-start(f32[96,128]{1,0:T(8,128)S(1)} %get-tuple-element.156), channel_id=1, source_target_pairs={{0,3},{1,2},{2,1},{3,0},{4,7},{5,6},{6,5},{7,4},{8,11},{9,10},{10,... | collective-permute-start | bytes 147464 | tf_op jit(solution)/shard_map/sums/ppermute | solution.py:27
  432.3 10.0 %collective-permute-start.28 = (f32[96,128]{1,0:T(8,128)S(1)}, f32[96,128]{1,0:T(8,128)S(1)}, u32[]{:S(2)}, u32[]{:S(2)}) collective-permute-start(f32[96,128]{1,0:T(8,128)S(1)} %add_add_fusion.2), channel_id=1, source_target_pairs={{0,32},{1,33},{2,34},{3,35},{4,36},{5,37},{6,38},{7,39},{8,40},{9,... | collective-permute-start | bytes 147464 | tf_op jit(solution)/shard_map/sums/ppermute | solution.py:27
  433.0 9.3 %collective-permute-start.29 = (f32[96,128]{1,0:T(8,128)S(1)}, f32[96,128]{1,0:T(8,128)S(1)}, u32[]{:S(2)}, u32[]{:S(2)}) collective-permute-start(f32[96,128]{1,0:T(8,128)S(1)} %add_add_fusion.2), channel_id=1, source_target_pairs={{0,64},{1,65},{2,66},{3,67},{4,68},{5,69},{6,70},{7,71},{8,72},{9,... | collective-permute-start | bytes 147464 | tf_op jit(solution)/shard_map/sums/ppermute | solution.py:27
  435.0 7.3 %collective-permute-start.30 = (f32[96,128]{1,0:T(8,128)S(1)}, f32[96,128]{1,0:T(8,128)S(1)}, u32[]{:S(2)}, u32[]{:S(2)}) collective-permute-start(f32[96,128]{1,0:T(8,128)S(1)} %add_add_fusion.2), channel_id=1, source_target_pairs={{0,96},{1,97},{2,98},{3,99},{4,100},{5,101},{6,102},{7,103},{8,104... | collective-permute-start | bytes 147464 | tf_op jit(solution)/shard_map/sums/ppermute | solution.py:27
  438.3 46.3 %all-to-all-start.6 = ((bf16[16,80,512]{2,1,0:T(8,128)(2,1)}), bf16[16,80,512]{2,1,0:T(8,128)(2,1)S(1)}, u32[]{:S(2)}, u32[]{:S(2)}) async-start(bf16[16,80,512]{2,1,0:T(8,128)(2,1)} %bitcast.224), calls=%async_computation.6 | async-start | bytes 2621440 | tf_op jit(solution)/shard_map/grad_input_seq/all_to_all | solution.py:81
  448.5 29.2 %collective-permute-start.35 = (bf16[2,2,40,1536]{3,2,0,1:T(8,128)(2,1)}, bf16[2,2,40,1536]{3,2,0,1:T(8,128)(2,1)S(1)}, u32[]{:S(2)}, u32[]{:S(2)}) collective-permute-start(bf16[2,2,40,1536]{3,2,0,1:T(8,128)(2,1)} %get-tuple-element.123), channel_id=1, source_target_pairs={{0,32},{1,33},{2,34},{3,35},{4,36},{5,37},{6,38},{7,39},{8,40},{9,... | collective-permute-start | bytes 1474568 | tf_op jit(solution)/shard_map/weight_x/ppermute | solution.py:27
  450.6 31.7 %collective-permute-start.36 = (bf16[2,2,40,1536]{3,2,0,1:T(8,128)(2,1)S(1)}, bf16[2,2,40,1536]{3,2,0,1:T(8,128)(2,1)S(1)}, u32[]{:S(2)}, u32[]{:S(2)}) collective-permute-start(bf16[2,2,40,1536]{3,2,0,1:T(8,128)(2,1)S(1)} %get-tuple-element.125), channel_id=1, source_target_pairs={{0,64},{1,65},{2,66},{3,67},{4,68},{5,69},{6,70},{7,71},{8,72},{9,... | collective-permute-start | bytes 1474568 | tf_op jit(solution)/shard_map/weight_x/ppermute | solution.py:27
  453.2 29.8 %collective-permute-start.37 = (bf16[2,2,40,1536]{3,2,0,1:T(8,128)(2,1)S(1)}, bf16[2,2,40,1536]{3,2,0,1:T(8,128)(2,1)}, u32[]{:S(2)}, u32[]{:S(2)}) collective-permute-start(bf16[2,2,40,1536]{3,2,0,1:T(8,128)(2,1)S(1)} %get-tuple-element.124), channel_id=1, source_target_pairs={{0,96},{1,97},{2,98},{3,99},{4,100},{5,101},{6,102},{7,103},{8,104... | collective-permute-start | bytes 1474568 | tf_op jit(solution)/shard_map/weight_x/ppermute | solution.py:27
  453.2 5.9 %collective-permute-start.32 = (f32[96,128]{1,0:T(8,128)S(1)}, f32[96,128]{1,0:T(8,128)S(1)}, u32[]{:S(2)}, u32[]{:S(2)}) collective-permute-start(f32[96,128]{1,0:T(8,128)S(1)} %add_add_fusion.1), channel_id=1, source_target_pairs={{0,16},{1,17},{2,18},{3,19},{4,20},{5,21},{6,22},{7,23},{8,24},{9,... | collective-permute-start | bytes 147464 | tf_op jit(solution)/shard_map/sums/ppermute | solution.py:27
  453.2 24.3 %collective-permute-start.33 = (f32[96,128]{1,0:T(8,128)S(1)}, f32[96,128]{1,0:T(8,128)S(1)}, u32[]{:S(2)}, u32[]{:S(2)}) collective-permute-start(f32[96,128]{1,0:T(8,128)S(1)} %add_add_fusion.1), channel_id=1, source_target_pairs={{0,128},{1,129},{2,130},{3,131},{4,132},{5,133},{6,134},{7,135},{8... | collective-permute-start | bytes 147464 | tf_op jit(solution)/shard_map/sums/ppermute | solution.py:27
  459.2 18.5 %collective-permute-start.34 = (f32[96,128]{1,0:T(8,128)S(1)}, f32[96,128]{1,0:T(8,128)S(1)}, u32[]{:S(2)}, u32[]{:S(2)}) collective-permute-start(f32[96,128]{1,0:T(8,128)S(1)} %add_add_fusion.1), channel_id=1, source_target_pairs={{0,144},{1,145},{2,146},{3,147},{4,148},{5,149},{6,150},{7,151},{8... | collective-permute-start | bytes 147464 | tf_op jit(solution)/shard_map/sums/ppermute | solution.py:27
  484.6 9.3 %collective-permute-start.38 = (f32[96,128]{1,0:T(8,128)S(1)}, f32[96,128]{1,0:T(8,128)S(1)}, u32[]{:S(2)}, u32[]{:S(2)}) collective-permute-start(f32[96,128]{1,0:T(8,128)S(1)} %add_add_fusion), channel_id=1, source_target_pairs={{0,1},{1,0},{2,3},{3,2},{4,5},{5,4},{6,7},{7,6},{8,9},{9,8},{10,11... | collective-permute-start | bytes 147464 | tf_op jit(solution)/shard_map/sums_back/ppermute | solution.py:27
  486.1 8.3 %collective-permute-start.39 = (f32[96,128]{1,0:T(8,128)S(1)}, f32[96,128]{1,0:T(8,128)S(1)}, u32[]{:S(2)}, u32[]{:S(2)}) collective-permute-start(f32[96,128]{1,0:T(8,128)S(1)} %add_add_fusion), channel_id=1, source_target_pairs={{0,2},{1,3},{2,0},{3,1},{4,6},{5,7},{6,4},{7,5},{8,10},{9,11},{10,... | collective-permute-start | bytes 147464 | tf_op jit(solution)/shard_map/sums_back/ppermute | solution.py:27
  487.9 6.5 %collective-permute-start.40 = (f32[96,128]{1,0:T(8,128)S(1)}, f32[96,128]{1,0:T(8,128)S(1)}, u32[]{:S(2)}, u32[]{:S(2)}) collective-permute-start(f32[96,128]{1,0:T(8,128)S(1)} %add_add_fusion), channel_id=1, source_target_pairs={{0,3},{1,2},{2,1},{3,0},{4,7},{5,6},{6,5},{7,4},{8,11},{9,10},{10,... | collective-permute-start | bytes 147464 | tf_op jit(solution)/shard_map/sums_back/ppermute | solution.py:27
  488.4 6.9 %collective-permute-start.41 = (bf16[2,2,40,384]{3,2,0,1:T(8,128)(2,1)S(1)}, bf16[2,2,40,384]{3,2,0,1:T(8,128)(2,1)S(1)}, u32[]{:S(2)}, u32[]{:S(2)}) collective-permute-start(bf16[2,2,40,384]{3,2,0,1:T(8,128)(2,1)S(1)} %get-tuple-element.138), channel_id=1, source_target_pairs={{0,1},{1,0},{2,3},{3,2},{4,5},{5,4},{6,7},{7,6},{8,9},{9,8},{10,11... | collective-permute-start | bytes 368648 | tf_op jit(solution)/shard_map/weight_z/ppermute | solution.py:27
  490.7 9.8 %collective-permute-start.42 = (bf16[2,2,40,384]{3,2,0,1:T(8,128)(2,1)S(1)}, bf16[2,2,40,384]{3,2,0,1:T(8,128)(2,1)S(1)}, u32[]{:S(2)}, u32[]{:S(2)}) collective-permute-start(bf16[2,2,40,384]{3,2,0,1:T(8,128)(2,1)S(1)} %get-tuple-element.140), channel_id=1, source_target_pairs={{0,2},{1,3},{2,0},{3,1},{4,6},{5,7},{6,4},{7,5},{8,10},{9,11},{10,... | collective-permute-start | bytes 368648 | tf_op jit(solution)/shard_map/weight_z/ppermute | solution.py:27
  493.9 9.3 %collective-permute-start.43 = (bf16[2,2,40,384]{3,2,0,1:T(8,128)(2,1)S(1)}, bf16[2,2,40,384]{3,2,0,1:T(8,128)(2,1)S(1)}, u32[]{:S(2)}, u32[]{:S(2)}) collective-permute-start(bf16[2,2,40,384]{3,2,0,1:T(8,128)(2,1)S(1)} %get-tuple-element.139), channel_id=1, source_target_pairs={{0,3},{1,2},{2,1},{3,0},{4,7},{5,6},{6,5},{7,4},{8,11},{9,10},{10,... | collective-permute-start | bytes 368648 | tf_op jit(solution)/shard_map/weight_z/ppermute | solution.py:27
  503.3 14.5 %collective-permute-start.45 = (f32[384,128]{1,0:T(8,128)S(1)}, f32[384,128]{1,0:T(8,128)S(1)}, u32[]{:S(2)}, u32[]{:S(2)}) collective-permute-start(f32[384,128]{1,0:T(8,128)S(1)} %constant_dynamic-update-slice_fusion.5), channel_id=1, source_target_pairs={{0,4},{1,5},{2,6},{3,7},{4,0},{5,1},{6,2},{7,3},{8,12},{9,13},{10,... | collective-permute-start | bytes 589832 | tf_op jit(solution)/shard_map/sums_back/ppermute | solution.py:27
  503.4 14.4 %collective-permute-start.46 = (f32[384,128]{1,0:T(8,128)S(1)}, f32[384,128]{1,0:T(8,128)S(1)}, u32[]{:S(2)}, u32[]{:S(2)}) collective-permute-start(f32[384,128]{1,0:T(8,128)S(1)} %constant_dynamic-update-slice_fusion.5), channel_id=1, source_target_pairs={{0,8},{1,9},{2,10},{3,11},{4,12},{5,13},{6,14},{7,15},{8,0},{9,1},... | collective-permute-start | bytes 589832 | tf_op jit(solution)/shard_map/sums_back/ppermute | solution.py:27
  505.2 12.6 %collective-permute-start.47 = (f32[384,128]{1,0:T(8,128)S(1)}, f32[384,128]{1,0:T(8,128)S(1)}, u32[]{:S(2)}, u32[]{:S(2)}) collective-permute-start(f32[384,128]{1,0:T(8,128)S(1)} %constant_dynamic-update-slice_fusion.5), channel_id=1, source_target_pairs={{0,12},{1,13},{2,14},{3,15},{4,8},{5,9},{6,10},{7,11},{8,4},{9,5},... | collective-permute-start | bytes 589832 | tf_op jit(solution)/shard_map/sums_back/ppermute | solution.py:27
  508.1 9.0 %collective-permute-start.44 = (bf16[2,40,384]{2,1,0:T(8,128)(2,1)S(1)}, bf16[2,40,384]{2,1,0:T(8,128)(2,1)S(1)}, u32[]{:S(2)}, u32[]{:S(2)}) collective-permute-start(bf16[2,40,384]{2,1,0:T(8,128)(2,1)S(1)} %fusion.55), channel_id=1, source_target_pairs={{0,128},{1,129},{2,130},{3,131},{4,132},{5,133},{6,134},{7,135},{8... | collective-permute-start | bytes 184328 | tf_op jit(solution)/shard_map/weight_z_hi/ppermute | solution.py:27
  (16 other events, 45.7 us)
